TPU v7x, 512 devices: a whole 4x8x8 slice. The times are simulated.
512 devices in a mesh: gx: 8 (over y), gy: 8 (over z), gz: 8 (over x, core).
Axes of the slice: x: 4, y: 8, z: 8, core: 2. Of those that a mesh axis runs over, the one named last changes fastest.
Arguments:
- couplings: float32 [18, 64, 64, 1024], P(None, 'gx', 'gy', 'gz'), may hold values from 0.05 to 2
- diagonal: float32 [3, 64, 64, 1024], P(None, 'gx', 'gy', 'gz'), may hold values from 0.01 to 0.1
- right_side: float32 [3, 64, 64, 1024], P(None, 'gx', 'gy', 'gz'), may hold values from -6 to 6
- guess: float32 [3, 64, 64, 1024], P(None, 'gx', 'gy', 'gz'), may hold values from -4 to 4
Outputs:
- solution: float32 [3, 64, 64, 1024], P(None, 'gx', 'gy', 'gz')
All inputs are finite; a program needn't handle non-finite values.
Results may differ from a plain program's by a relative error of at most 0.00011.
Values sent between devices are 32-bit elements; how exact they have to be, the bound alone decides.
No kernel may reach another device: no remote copies, remote signals or barrier semaphores. Data moves between devices by JAX's collectives and lax.ppermute only.
A program may use at most 128 MiB of HBM per device.

v0:
```python
import jax
import jax.numpy as jnp
from jax import lax
from jax.sharding import PartitionSpec as P

LEVELS = 4
SWEEPS = 2
COARSE_SWEEPS = 8


damping = 0.8


def extended(value, sides, width):
    edges = {}
    for axis, dim in sides:
        devices, length = (lax.axis_size(axis), value.shape[dim])
        up = [(i, (i + 1) % devices) for i in range(devices - 1)]
        last = lax.slice_in_dim(value, length - width, length, axis=dim)
        first = lax.slice_in_dim(value, 0, width, axis=dim)
        edges[dim] = (
            lax.ppermute(last, axis, up),
            lax.ppermute(first, axis, [(b, a) for a, b in up]),
        )
    done = []
    for _, dim in sides:
        low, high = edges[dim]
        around = [(width, width) if d in done else (0, 0) for d in range(value.ndim)]
        value = jnp.concatenate([jnp.pad(low, around), value, jnp.pad(high, around)], axis=dim)
        done.append(dim)
    return value


def operate(field, padded, weights, total):
    near = [
        padded[:, 2:, 1:-1, 1:-1],
        padded[:, :-2, 1:-1, 1:-1],
        padded[:, 1:-1, 2:, 1:-1],
        padded[:, 1:-1, :-2, 1:-1],
        padded[:, 1:-1, 1:-1, 2:],
        padded[:, 1:-1, 1:-1, :-2],
    ]
    offdiag = weights[:, 0] * near[0]
    for index in range(1, 6):
        offdiag = offdiag + weights[:, index] * near[index]
    return total * field - offdiag


def coarsen(array):
    shape = array.shape
    count = len(shape)
    blocks = array.reshape(shape[:-3] + (shape[-3] // 2, 2, shape[-2] // 2, 2, shape[-1] // 2, 2))
    return jnp.mean(blocks, axis=(count - 2, count, count + 2))


def refine(array):
    return jnp.repeat(jnp.repeat(jnp.repeat(array, 2, axis=-3), 2, axis=-2), 2, axis=-1)


def hierarchy(couplings, diagonal):
    weights = couplings.reshape((3, 6) + diagonal.shape[1:])
    local_diag = diagonal
    result = []
    for level in range(LEVELS):
        if level > 0:
            weights = coarsen(weights) * 0.25
            local_diag = coarsen(local_diag)
        result.append((weights, local_diag + jnp.sum(weights, axis=1)))
    return result


def apply_brick(field, weights, total):
    padded = extended(field, (("gx", 1), ("gy", 2), ("gz", 3)), 1)
    return operate(field, padded, weights, total)


def apply_coarse(field, weights, total):
    padded = extended(field, (("gx", 1), ("gy", 2), ("gz", 3)), 1)
    return operate(field, padded, weights, total)


def per_device(couplings, diagonal, right_side, guess):
    levels = hierarchy(couplings, diagonal)
    coarse_weights, coarse_total = levels[LEVELS - 1]

    def coarsest(rhs):
        value = damping * rhs / coarse_total
        for step in range(COARSE_SWEEPS - 1):
            value = (
                value
                + damping * (rhs - apply_coarse(value, coarse_weights, coarse_total)) / coarse_total
            )
        return value

    def cycle(level, field, rhs):
        if level == LEVELS - 1:
            return coarsest(rhs)
        weights, total = levels[level]
        if field is None:
            field = damping * rhs / total
            first = 1
        else:
            first = 0
        for step in range(first, SWEEPS):
            field = field + damping * (rhs - apply_brick(field, weights, total)) / total
        resid = rhs - apply_brick(field, weights, total)
        correction = cycle(level + 1, None, coarsen(resid))
        field = field + refine(correction)
        for step in range(SWEEPS):
            field = field + damping * (rhs - apply_brick(field, weights, total)) / total
        return field

    return cycle(0, guess, right_side)


def solution(mesh):
    return jax.shard_map(
        per_device,
        mesh=mesh,
        in_specs=(
            P(None, "gx", "gy", "gz"),
            P(None, "gx", "gy", "gz"),
            P(None, "gx", "gy", "gz"),
            P(None, "gx", "gy", "gz"),
        ),
        out_specs=P(None, "gx", "gy", "gz"),
        check_vma=False,
    )
```

profile of v0, /device:TPU:220, one launch (start us, length us, event | category | flops | bytes accessed | tf_op | source)
XLA Modules:
  0.0 484.9 jit_solution(9974005334212800324)
XLA Ops:
  21.0 16.2 %reshape_reshape.3 = f32[3,6,4,2,4,2,64,2]{1,0,7,6,5,4,3,2:T(4,128)} reshape(f32[18,8,8,128]{0,3,2,1:T(8,128)} %copy.742) | data formatting | bytes 1179648 | tf_op jit(solution)/shard_map/reshape;reshape | solution.py:52
  37.3 10.0 %reduce_sum.141 = f32[3,6,4,4,64]{1,0,4,3,2:T(4,128)S(1)} reduce(f32[3,6,4,2,4,2,64,2]{1,0,7,6,5,4,3,2:T(4,128)} %reshape_reshape.3, f32[]{:T(128)} %constant.31.clone.1), dimensions={3,5,7}, to_apply=%region_3.0 | reduce | flops 129024 | bytes 663556 | tf_op jit(solution)/shard_map/reduce_sum | solution.py:53
  50.1 5.5 %collective-permute-start.3 = (f32[3,8,1,128]{3,2,1,0:T(1,128)S(1)}, f32[3,8,1,128]{3,2,1,0:T(1,128)S(1)}, u32[]{:S(2)}, u32[]{:S(2)}) collective-permute-start(f32[3,8,1,128]{3,2,1,0:T(1,128)S(1)} %copy-done.5), channel_id=1, source_target_pairs={{0,8},{8,16},{16,24},{24,32},{32,40},{40,48},{48,56},{1,9},{9,17},... | collective-permute-start | bytes 36872 | tf_op jit(solution)/shard_map/ppermute | solution.py:22
  71.7 5.1 %collective-permute-start.7 = (f32[3,1,8,128]{3,2,1,0:T(8,128)S(1)}, f32[3,1,8,128]{3,2,1,0:T(8,128)S(1)}, u32[]{:S(2)}, u32[]{:S(2)}) collective-permute-start(f32[3,1,8,128]{3,2,1,0:T(8,128)S(1)} %get-tuple-element.50), channel_id=1, source_target_pairs={{0,64},{64,128},{128,192},{192,256},{256,320},{320,384},{384,448},... | collective-permute-start | bytes 36872 | tf_op jit(solution)/shard_map/ppermute | solution.py:22
  91.9 5.5 %collective-permute-start.13 = (f32[3,1,8,128]{3,2,1,0:T(8,128)S(1)}, f32[3,1,8,128]{3,2,1,0:T(8,128)S(1)}, u32[]{:S(2)}, u32[]{:S(2)}) collective-permute-start(f32[3,1,8,128]{3,2,1,0:T(8,128)S(1)} %get-tuple-element.44), channel_id=1, source_target_pairs={{0,64},{64,128},{128,192},{192,256},{256,320},{320,384},{384,448},... | collective-permute-start | bytes 36872 | tf_op jit(solution)/shard_map/ppermute | solution.py:22
  97.6 7.6 %reshape.129 = f32[3,4,2,4,2,64,2]{6,5,4,3,2,1,0:T(8,128)} reshape(f32[3,8,8,128]{3,2,1,0:T(8,128)S(1)} %copy-done.3) | data formatting | bytes 196608 | tf_op jit(solution)/shard_map/reshape | solution.py:52
  108.8 7.6 %reshape.128 = f32[3,4,2,4,2,64,2]{6,5,4,3,2,1,0:T(8,128)} reshape(f32[3,8,8,128]{3,2,1,0:T(8,128)S(1)} %fusion.40) | data formatting | bytes 196608 | tf_op jit(solution)/shard_map/reshape | solution.py:52
  121.8 5.1 %collective-permute-start.21 = (f32[3,4,1,64]{3,2,1,0:T(1,128)S(1)}, f32[3,4,1,64]{3,2,1,0:T(1,128)S(1)}, u32[]{:S(2)}, u32[]{:S(2)}) collective-permute-start(f32[3,4,1,64]{3,2,1,0:T(1,128)S(1)} %get-tuple-element.85), channel_id=1, source_target_pairs={{0,8},{8,16},{16,24},{24,32},{32,40},{40,48},{48,56},{1,9},{9,17},... | collective-permute-start | bytes 9224 | tf_op jit(solution)/shard_map/ppermute | solution.py:22
  128.8 5.1 %collective-permute-start.19 = (f32[3,1,4,64]{3,2,1,0:T(4,128)S(1)}, f32[3,1,4,64]{3,2,1,0:T(4,128)S(1)}, u32[]{:S(2)}, u32[]{:S(2)}) collective-permute-start(f32[3,1,4,64]{3,2,1,0:T(4,128)S(1)} %get-tuple-element.83), channel_id=1, source_target_pairs={{0,64},{64,128},{128,192},{192,256},{256,320},{320,384},{384,448},... | collective-permute-start | bytes 9224 | tf_op jit(solution)/shard_map/ppermute | solution.py:22
  144.2 5.1 %collective-permute-start.27 = (f32[3,4,1,64]{3,2,1,0:T(1,128)S(1)}, f32[3,4,1,64]{3,2,1,0:T(1,128)S(1)}, u32[]{:S(2)}, u32[]{:S(2)}) collective-permute-start(f32[3,4,1,64]{3,2,1,0:T(1,128)S(1)} %get-tuple-element.79), channel_id=1, source_target_pairs={{0,8},{8,16},{16,24},{24,32},{32,40},{40,48},{48,56},{1,9},{9,17},... | collective-permute-start | bytes 9224 | tf_op jit(solution)/shard_map/ppermute | solution.py:22
  166.7 5.1 %collective-permute-start.33 = (f32[3,2,1,32]{3,2,1,0:T(1,128)S(1)}, f32[3,2,1,32]{3,2,1,0:T(1,128)S(1)}, u32[]{:S(2)}, u32[]{:S(2)}) collective-permute-start(f32[3,2,1,32]{3,2,1,0:T(1,128)S(1)} %get-tuple-element.108), channel_id=1, source_target_pairs={{0,8},{8,16},{16,24},{24,32},{32,40},{40,48},{48,56},{1,9},{9,17},... | collective-permute-start | bytes 2312 | tf_op jit(solution)/shard_map/ppermute | solution.py:22
  173.8 5.1 %collective-permute-start.31 = (f32[3,1,2,32]{3,2,1,0:T(2,128)S(1)}, f32[3,1,2,32]{3,2,1,0:T(2,128)S(1)}, u32[]{:S(2)}, u32[]{:S(2)}) collective-permute-start(f32[3,1,2,32]{3,2,1,0:T(2,128)S(1)} %get-tuple-element.110), channel_id=1, source_target_pairs={{0,64},{64,128},{128,192},{192,256},{256,320},{320,384},{384,448},... | collective-permute-start | bytes 2312 | tf_op jit(solution)/shard_map/ppermute | solution.py:22
  195.2 5.1 %collective-permute-start.37 = (f32[3,1,2,32]{3,2,1,0:T(2,128)S(1)}, f32[3,1,2,32]{3,2,1,0:T(2,128)S(1)}, u32[]{:S(2)}, u32[]{:S(2)}) collective-permute-start(f32[3,1,2,32]{3,2,1,0:T(2,128)S(1)} %get-tuple-element.104), channel_id=1, source_target_pairs={{0,64},{64,128},{128,192},{192,256},{256,320},{320,384},{384,448},... | collective-permute-start | bytes 2312 | tf_op jit(solution)/shard_map/ppermute | solution.py:22
  215.5 5.1 %collective-permute-start.43 = (f32[3,1,1,16]{3,0,2,1:T(4,128)S(1)}, f32[3,1,1,16]{3,0,2,1:T(4,128)S(1)}, u32[]{:S(2)}, u32[]{:S(2)}) collective-permute-start(f32[3,1,1,16]{3,0,2,1:T(4,128)S(1)} %get-tuple-element.19), channel_id=1, source_target_pairs={{0,64},{64,128},{128,192},{192,256},{256,320},{320,384},{384,448},... | collective-permute-start | bytes 584 | tf_op jit(solution)/shard_map/ppermute | solution.py:22
  235.4 5.1 %collective-permute-start.49 = (f32[3,1,1,16]{3,0,2,1:T(4,128)S(1)}, f32[3,1,1,16]{3,0,2,1:T(4,128)S(1)}, u32[]{:S(2)}, u32[]{:S(2)}) collective-permute-start(f32[3,1,1,16]{3,0,2,1:T(4,128)S(1)} %fusion.290), channel_id=1, source_target_pairs={{0,64},{64,128},{128,192},{192,256},{256,320},{320,384},{384,448},... | collective-permute-start | bytes 584 | tf_op jit(solution)/shard_map/ppermute | solution.py:22
  298.0 5.1 %collective-permute-start.67 = (f32[3,1,1,16]{3,0,2,1:T(4,128)S(1)}, f32[3,1,1,16]{3,0,2,1:T(4,128)S(1)}, u32[]{:S(2)}, u32[]{:S(2)}) collective-permute-start(f32[3,1,1,16]{3,0,2,1:T(4,128)S(1)} %fusion.257), channel_id=1, source_target_pairs={{0,64},{64,128},{128,192},{192,256},{256,320},{320,384},{384,448},... | collective-permute-start | bytes 584 | tf_op jit(solution)/shard_map/ppermute | solution.py:22
  319.1 5.1 %collective-permute-start.73 = (f32[3,1,1,16]{3,0,2,1:T(4,128)S(1)}, f32[3,1,1,16]{3,0,2,1:T(4,128)S(1)}, u32[]{:S(2)}, u32[]{:S(2)}) collective-permute-start(f32[3,1,1,16]{3,0,2,1:T(4,128)S(1)} %fusion.246), channel_id=1, source_target_pairs={{0,64},{64,128},{128,192},{192,256},{256,320},{320,384},{384,448},... | collective-permute-start | bytes 584 | tf_op jit(solution)/shard_map/ppermute | solution.py:22
  340.2 5.1 %collective-permute-start.79 = (f32[3,1,1,16]{3,0,2,1:T(4,128)S(1)}, f32[3,1,1,16]{3,0,2,1:T(4,128)S(1)}, u32[]{:S(2)}, u32[]{:S(2)}) collective-permute-start(f32[3,1,1,16]{3,0,2,1:T(4,128)S(1)} %fusion.235), channel_id=1, source_target_pairs={{0,64},{64,128},{128,192},{192,256},{256,320},{320,384},{384,448},... | collective-permute-start | bytes 584 | tf_op jit(solution)/shard_map/ppermute | solution.py:22
  354.4 5.1 %collective-permute-start.87 = (f32[3,2,1,32]{3,2,1,0:T(1,128)S(1)}, f32[3,2,1,32]{3,2,1,0:T(1,128)S(1)}, u32[]{:S(2)}, u32[]{:S(2)}) collective-permute-start(f32[3,2,1,32]{3,2,1,0:T(1,128)S(1)} %get-tuple-element.95), channel_id=1, source_target_pairs={{0,8},{8,16},{16,24},{24,32},{32,40},{40,48},{48,56},{1,9},{9,17},... | collective-permute-start | bytes 2312 | tf_op jit(solution)/shard_map/ppermute | solution.py:22
  382.8 5.1 %collective-permute-start.91 = (f32[3,1,2,32]{3,2,1,0:T(2,128)S(1)}, f32[3,1,2,32]{3,2,1,0:T(2,128)S(1)}, u32[]{:S(2)}, u32[]{:S(2)}) collective-permute-start(f32[3,1,2,32]{3,2,1,0:T(2,128)S(1)} %get-tuple-element.91), channel_id=1, source_target_pairs={{0,64},{64,128},{128,192},{192,256},{256,320},{320,384},{384,448},... | collective-permute-start | bytes 2312 | tf_op jit(solution)/shard_map/ppermute | solution.py:22
  397.5 5.1 %collective-permute-start.99 = (f32[3,4,1,64]{3,2,1,0:T(1,128)S(1)}, f32[3,4,1,64]{3,2,1,0:T(1,128)S(1)}, u32[]{:S(2)}, u32[]{:S(2)}) collective-permute-start(f32[3,4,1,64]{3,2,1,0:T(1,128)S(1)} %get-tuple-element.70), channel_id=1, source_target_pairs={{0,8},{8,16},{16,24},{24,32},{32,40},{40,48},{48,56},{1,9},{9,17},... | collective-permute-start | bytes 9224 | tf_op jit(solution)/shard_map/ppermute | solution.py:22
  419.0 5.1 %collective-permute-start.105 = (f32[3,4,1,64]{3,2,1,0:T(1,128)S(1)}, f32[3,4,1,64]{3,2,1,0:T(1,128)S(1)}, u32[]{:S(2)}, u32[]{:S(2)}) collective-permute-start(f32[3,4,1,64]{3,2,1,0:T(1,128)S(1)} %get-tuple-element.64), channel_id=1, source_target_pairs={{0,8},{8,16},{16,24},{24,32},{32,40},{40,48},{48,56},{1,9},{9,17},... | collective-permute-start | bytes 9224 | tf_op jit(solution)/shard_map/ppermute | solution.py:22
  426.1 5.1 %collective-permute-start.103 = (f32[3,1,4,64]{3,2,1,0:T(4,128)S(1)}, f32[3,1,4,64]{3,2,1,0:T(4,128)S(1)}, u32[]{:S(2)}, u32[]{:S(2)}) collective-permute-start(f32[3,1,4,64]{3,2,1,0:T(4,128)S(1)} %get-tuple-element.62), channel_id=1, source_target_pairs={{0,64},{64,128},{128,192},{192,256},{256,320},{320,384},{384,448},... | collective-permute-start | bytes 9224 | tf_op jit(solution)/shard_map/ppermute | solution.py:22
  448.6 5.1 %collective-permute-start.109 = (f32[3,1,8,128]{3,2,1,0:T(8,128)S(1)}, f32[3,1,8,128]{3,2,1,0:T(8,128)S(1)}, u32[]{:S(2)}, u32[]{:S(2)}) collective-permute-start(f32[3,1,8,128]{3,2,1,0:T(8,128)S(1)} %get-tuple-element.38), channel_id=1, source_target_pairs={{0,64},{64,128},{128,192},{192,256},{256,320},{320,384},{384,448},... | collective-permute-start | bytes 36872 | tf_op jit(solution)/shard_map/ppermute | solution.py:22
  (381 shorter events, 337.7 us)
Async XLA Ops:
  1.3 48.7 %collective-permute-start.1 = (f32[3,1,8,128]{3,2,1,0:T(8,128)}, f32[3,1,8,128]{3,2,1,0:T(8,128)S(1)}, u32[]{:S(2)}, u32[]{:S(2)}) collective-permute-start(f32[3,1,8,128]{3,2,1,0:T(8,128)} %get-tuple-element.59), channel_id=1, source_target_pairs={{0,64},{64,128},{128,192},{192,256},{256,320},{320,384},{384,448},... | collective-permute-start | bytes 36872 | tf_op jit(solution)/shard_map/ppermute | solution.py:22
  6.0 49.6 %collective-permute-start = (f32[3,1,8,128]{3,2,1,0:T(8,128)}, f32[3,1,8,128]{3,2,1,0:T(8,128)S(1)}, u32[]{:S(2)}, u32[]{:S(2)}) collective-permute-start(f32[3,1,8,128]{3,2,1,0:T(8,128)} %get-tuple-element.58), channel_id=1, source_target_pairs={{64,0},{128,64},{192,128},{256,192},{320,256},{384,320},{448,384},... | collective-permute-start | bytes 36872 | tf_op jit(solution)/shard_map/ppermute | solution.py:23
  9.6 47.4 %collective-permute-start.4 = (f32[3,8,8,1]{3,2,1,0:T(8,128)}, f32[3,8,8,1]{3,2,1,0:T(8,128)S(1)}, u32[]{:S(2)}, u32[]{:S(2)}) collective-permute-start(f32[3,8,8,1]{3,2,1,0:T(8,128)} %get-tuple-element.54), channel_id=1, source_target_pairs={{1,0},{2,1},{3,2},{4,3},{5,4},{6,5},{7,6},{9,8},{10,9},{11,10},{12... | collective-permute-start | bytes 2312 | tf_op jit(solution)/shard_map/ppermute | solution.py:23
  11.5 45.5 %collective-permute-start.5 = (f32[3,8,8,1]{3,2,1,0:T(8,128)S(1)}, f32[3,8,8,1]{3,2,1,0:T(8,128)S(1)}, u32[]{:S(2)}, u32[]{:S(2)}) collective-permute-start(f32[3,8,8,1]{3,2,1,0:T(8,128)S(1)} %get-tuple-element.55), channel_id=1, source_target_pairs={{0,1},{1,2},{2,3},{3,4},{4,5},{5,6},{6,7},{8,9},{9,10},{10,11},{11... | collective-permute-start | bytes 2312 | tf_op jit(solution)/shard_map/ppermute | solution.py:22
  15.5 40.7 %collective-permute-start.2 = (f32[3,8,1,128]{3,2,1,0:T(1,128)}, f32[3,8,1,128]{3,2,1,0:T(1,128)}, u32[]{:S(2)}, u32[]{:S(2)}) collective-permute-start(f32[3,8,1,128]{3,2,1,0:T(1,128)} %get-tuple-element.57), channel_id=1, source_target_pairs={{8,0},{16,8},{24,16},{32,24},{40,32},{48,40},{56,48},{9,1},{17,9},... | collective-permute-start | bytes 36872 | tf_op jit(solution)/shard_map/ppermute | solution.py:23
  60.0 17.6 %collective-permute-start.10 = (f32[3,8,8,1]{3,2,1,0:T(8,128)S(1)}, f32[3,8,8,1]{3,2,1,0:T(8,128)S(1)}, u32[]{:S(2)}, u32[]{:S(2)}) collective-permute-start(f32[3,8,8,1]{3,2,1,0:T(8,128)S(1)} %get-tuple-element.48), channel_id=1, source_target_pairs={{1,0},{2,1},{3,2},{4,3},{5,4},{6,5},{7,6},{9,8},{10,9},{11,10},{12... | collective-permute-start | bytes 2312 | tf_op jit(solution)/shard_map/ppermute | solution.py:23
  80.5 28.1 %collective-permute-start.16 = (f32[3,8,8,1]{3,2,1,0:T(8,128)S(1)}, f32[3,8,8,1]{3,2,1,0:T(8,128)S(1)}, u32[]{:S(2)}, u32[]{:S(2)}) collective-permute-start(f32[3,8,8,1]{3,2,1,0:T(8,128)S(1)} %get-tuple-element.42), channel_id=1, source_target_pairs={{1,0},{2,1},{3,2},{4,3},{5,4},{6,5},{7,6},{9,8},{10,9},{11,10},{12... | collective-permute-start | bytes 2312 | tf_op jit(solution)/shard_map/ppermute | solution.py:23
  82.9 25.7 %collective-permute-start.17 = (f32[3,8,8,1]{3,2,1,0:T(8,128)S(1)}, f32[3,8,8,1]{3,2,1,0:T(8,128)S(1)}, u32[]{:S(2)}, u32[]{:S(2)}) collective-permute-start(f32[3,8,8,1]{3,2,1,0:T(8,128)S(1)} %get-tuple-element.43), channel_id=1, source_target_pairs={{0,1},{1,2},{2,3},{3,4},{4,5},{5,6},{6,7},{8,9},{9,10},{10,11},{11... | collective-permute-start | bytes 2312 | tf_op jit(solution)/shard_map/ppermute | solution.py:22
  84.8 23.7 %collective-permute-start.15 = (f32[3,8,1,128]{3,2,1,0:T(1,128)S(1)}, f32[3,8,1,128]{3,2,1,0:T(1,128)S(1)}, u32[]{:S(2)}, u32[]{:S(2)}) collective-permute-start(f32[3,8,1,128]{3,2,1,0:T(1,128)S(1)} %get-tuple-element.46), channel_id=1, source_target_pairs={{0,8},{8,16},{16,24},{24,32},{32,40},{40,48},{48,56},{1,9},{9,17},... | collective-permute-start | bytes 36872 | tf_op jit(solution)/shard_map/ppermute | solution.py:22
  90.0 18.7 %collective-permute-start.12 = (f32[3,1,8,128]{3,2,1,0:T(8,128)S(1)}, f32[3,1,8,128]{3,2,1,0:T(8,128)S(1)}, u32[]{:S(2)}, u32[]{:S(2)}) collective-permute-start(f32[3,1,8,128]{3,2,1,0:T(8,128)S(1)} %get-tuple-element.45), channel_id=1, source_target_pairs={{64,0},{128,64},{192,128},{256,192},{320,256},{384,320},{448,384},... | collective-permute-start | bytes 36872 | tf_op jit(solution)/shard_map/ppermute | solution.py:23
  91.9 16.7 %collective-permute-start.13 = (f32[3,1,8,128]{3,2,1,0:T(8,128)S(1)}, f32[3,1,8,128]{3,2,1,0:T(8,128)S(1)}, u32[]{:S(2)}, u32[]{:S(2)}) collective-permute-start(f32[3,1,8,128]{3,2,1,0:T(8,128)S(1)} %get-tuple-element.44), channel_id=1, source_target_pairs={{0,64},{64,128},{128,192},{192,256},{256,320},{320,384},{384,448},... | collective-permute-start | bytes 36872 | tf_op jit(solution)/shard_map/ppermute | solution.py:22
  119.8 17.1 %collective-permute-start.20 = (f32[3,4,1,64]{3,2,1,0:T(1,128)S(1)}, f32[3,4,1,64]{3,2,1,0:T(1,128)S(1)}, u32[]{:S(2)}, u32[]{:S(2)}) collective-permute-start(f32[3,4,1,64]{3,2,1,0:T(1,128)S(1)} %get-tuple-element.86), channel_id=1, source_target_pairs={{8,0},{16,8},{24,16},{32,24},{40,32},{48,40},{56,48},{9,1},{17,9},... | collective-permute-start | bytes 9224 | tf_op jit(solution)/shard_map/ppermute | solution.py:23
  121.8 17.6 %collective-permute-start.21 = (f32[3,4,1,64]{3,2,1,0:T(1,128)S(1)}, f32[3,4,1,64]{3,2,1,0:T(1,128)S(1)}, u32[]{:S(2)}, u32[]{:S(2)}) collective-permute-start(f32[3,4,1,64]{3,2,1,0:T(1,128)S(1)} %get-tuple-element.85), channel_id=1, source_target_pairs={{0,8},{8,16},{16,24},{24,32},{32,40},{40,48},{48,56},{1,9},{9,17},... | collective-permute-start | bytes 9224 | tf_op jit(solution)/shard_map/ppermute | solution.py:22
  144.2 16.7 %collective-permute-start.27 = (f32[3,4,1,64]{3,2,1,0:T(1,128)S(1)}, f32[3,4,1,64]{3,2,1,0:T(1,128)S(1)}, u32[]{:S(2)}, u32[]{:S(2)}) collective-permute-start(f32[3,4,1,64]{3,2,1,0:T(1,128)S(1)} %get-tuple-element.79), channel_id=1, source_target_pairs={{0,8},{8,16},{16,24},{24,32},{32,40},{40,48},{48,56},{1,9},{9,17},... | collective-permute-start | bytes 9224 | tf_op jit(solution)/shard_map/ppermute | solution.py:22
  164.8 16.3 %collective-permute-start.32 = (f32[3,2,1,32]{3,2,1,0:T(1,128)S(1)}, f32[3,2,1,32]{3,2,1,0:T(1,128)S(1)}, u32[]{:S(2)}, u32[]{:S(2)}) collective-permute-start(f32[3,2,1,32]{3,2,1,0:T(1,128)S(1)} %get-tuple-element.109), channel_id=1, source_target_pairs={{8,0},{16,8},{24,16},{32,24},{40,32},{48,40},{56,48},{9,1},{17,9},... | collective-permute-start | bytes 2312 | tf_op jit(solution)/shard_map/ppermute | solution.py:23
  166.7 16.8 %collective-permute-start.33 = (f32[3,2,1,32]{3,2,1,0:T(1,128)S(1)}, f32[3,2,1,32]{3,2,1,0:T(1,128)S(1)}, u32[]{:S(2)}, u32[]{:S(2)}) collective-permute-start(f32[3,2,1,32]{3,2,1,0:T(1,128)S(1)} %get-tuple-element.108), channel_id=1, source_target_pairs={{0,8},{8,16},{16,24},{24,32},{32,40},{40,48},{48,56},{1,9},{9,17},... | collective-permute-start | bytes 2312 | tf_op jit(solution)/shard_map/ppermute | solution.py:22
  188.1 16.6 %collective-permute-start.39 = (f32[3,2,1,32]{3,2,1,0:T(1,128)S(1)}, f32[3,2,1,32]{3,2,1,0:T(1,128)S(1)}, u32[]{:S(2)}, u32[]{:S(2)}) collective-permute-start(f32[3,2,1,32]{3,2,1,0:T(1,128)S(1)} %get-tuple-element.102), channel_id=1, source_target_pairs={{0,8},{8,16},{16,24},{24,32},{32,40},{40,48},{48,56},{1,9},{9,17},... | collective-permute-start | bytes 2312 | tf_op jit(solution)/shard_map/ppermute | solution.py:22
  354.4 16.6 %collective-permute-start.87 = (f32[3,2,1,32]{3,2,1,0:T(1,128)S(1)}, f32[3,2,1,32]{3,2,1,0:T(1,128)S(1)}, u32[]{:S(2)}, u32[]{:S(2)}) collective-permute-start(f32[3,2,1,32]{3,2,1,0:T(1,128)S(1)} %get-tuple-element.95), channel_id=1, source_target_pairs={{0,8},{8,16},{16,24},{24,32},{32,40},{40,48},{48,56},{1,9},{9,17},... | collective-permute-start | bytes 2312 | tf_op jit(solution)/shard_map/ppermute | solution.py:22
  375.7 16.6 %collective-permute-start.93 = (f32[3,2,1,32]{3,2,1,0:T(1,128)S(1)}, f32[3,2,1,32]{3,2,1,0:T(1,128)S(1)}, u32[]{:S(2)}, u32[]{:S(2)}) collective-permute-start(f32[3,2,1,32]{3,2,1,0:T(1,128)S(1)} %get-tuple-element.89), channel_id=1, source_target_pairs={{0,8},{8,16},{16,24},{24,32},{32,40},{40,48},{48,56},{1,9},{9,17},... | collective-permute-start | bytes 2312 | tf_op jit(solution)/shard_map/ppermute | solution.py:22
  397.5 16.7 %collective-permute-start.99 = (f32[3,4,1,64]{3,2,1,0:T(1,128)S(1)}, f32[3,4,1,64]{3,2,1,0:T(1,128)S(1)}, u32[]{:S(2)}, u32[]{:S(2)}) collective-permute-start(f32[3,4,1,64]{3,2,1,0:T(1,128)S(1)} %get-tuple-element.70), channel_id=1, source_target_pairs={{0,8},{8,16},{16,24},{24,32},{32,40},{40,48},{48,56},{1,9},{9,17},... | collective-permute-start | bytes 9224 | tf_op jit(solution)/shard_map/ppermute | solution.py:22
  419.0 16.7 %collective-permute-start.105 = (f32[3,4,1,64]{3,2,1,0:T(1,128)S(1)}, f32[3,4,1,64]{3,2,1,0:T(1,128)S(1)}, u32[]{:S(2)}, u32[]{:S(2)}) collective-permute-start(f32[3,4,1,64]{3,2,1,0:T(1,128)S(1)} %get-tuple-element.64), channel_id=1, source_target_pairs={{0,8},{8,16},{16,24},{24,32},{32,40},{40,48},{48,56},{1,9},{9,17},... | collective-permute-start | bytes 9224 | tf_op jit(solution)/shard_map/ppermute | solution.py:22
  441.5 16.7 %collective-permute-start.111 = (f32[3,8,1,128]{3,2,1,0:T(1,128)S(1)}, f32[3,8,1,128]{3,2,1,0:T(1,128)S(1)}, u32[]{:S(2)}, u32[]{:S(2)}) collective-permute-start(f32[3,8,1,128]{3,2,1,0:T(1,128)S(1)} %get-tuple-element.40), channel_id=1, source_target_pairs={{0,8},{8,16},{16,24},{24,32},{32,40},{40,48},{48,56},{1,9},{9,17},... | collective-permute-start | bytes 36872 | tf_op jit(solution)/shard_map/ppermute | solution.py:22
  461.9 16.2 %collective-permute-start.116 = (f32[3,8,1,128]{3,2,1,0:T(1,128)S(1)}, f32[3,8,1,128]{3,2,1,0:T(1,128)S(1)}, u32[]{:S(2)}, u32[]{:S(2)}) collective-permute-start(f32[3,8,1,128]{3,2,1,0:T(1,128)S(1)} %get-tuple-element.35), channel_id=1, source_target_pairs={{8,0},{16,8},{24,16},{32,24},{40,32},{48,40},{56,48},{9,1},{17,9},... | collective-permute-start | bytes 36872 | tf_op jit(solution)/shard_map/ppermute | solution.py:23
  463.8 16.7 %collective-permute-start.117 = (f32[3,8,1,128]{3,2,1,0:T(1,128)S(1)}, f32[3,8,1,128]{3,2,1,0:T(1,128)S(1)}, u32[]{:S(2)}, u32[]{:S(2)}) collective-permute-start(f32[3,8,1,128]{3,2,1,0:T(1,128)S(1)} %get-tuple-element.34), channel_id=1, source_target_pairs={{0,8},{8,16},{16,24},{24,32},{32,40},{40,48},{48,56},{1,9},{9,17},... | collective-permute-start | bytes 36872 | tf_op jit(solution)/shard_map/ppermute | solution.py:22
  (102 other events, 1040.9 us)
where the time goes:
time: 489 us; the launch traced here: 485 us
  starting transfers between devices  366 us (75%)
  local copies, waits for them, and re-layouts  48.6 us (10%)
  waiting for transfers between devices  45.5 us (9%)
  other arithmetic  22.6 us (5%)
    ppermute x60, starting transfers between devices, extended(): lax.ppermute(last, axis, up)  246 us
    ppermute x60, starting transfers between devices, extended(): lax.ppermute(first, axis, [(b, a) for a, b in up])  120 us
    ppermute x60, waiting for transfers between devices, extended(): lax.ppermute(last, axis, up)  45.4 us
    reduce_sum x11, other arithmetic, coarsen(): return jnp.mean(blocks, axis=(count - 2, count, count + 2))  18.3 us
    another operation x1, local copies, waits for them, and re-layouts, coarsen(): array.reshape(shape[:-3] + (shape[-3] // 2, 2, shape[-2] // 2, 2, shape[-...  16.2 us
    reshape x3, local copies, waits for them, and re-layouts, coarsen(): array.reshape(shape[:-3] + (shape[-3] // 2, 2, shape[-2] // 2, 2, shape[-...  16.1 us
  transfers between devices with their start and end apart: 120, of which 18 were waited for; matrix products, arithmetic and copies ran while one was open for 11% of the time, Pallas kernels for 0%

commit v1 on v0

v1 whole, which is shorter than its diff:
```python
import jax
import jax.numpy as jnp
from jax import lax
from jax.experimental import pallas as pl
from jax.experimental.pallas import tpu as pltpu
from jax.sharding import PartitionSpec as P


F32 = jnp.float32
LANES = 128
STATIC = 21
HALO2 = 20
MEANS = 84


def rolled(value, shift, axis):
    shift %= value.shape[axis]
    return value if shift == 0 else pltpu.roll(value, shift, axis)


def lanes_of(rows):
    return lax.broadcasted_iota(jnp.int32, (rows, LANES), 1)


def pair_matrix(weight):
    fine = lax.broadcasted_iota(jnp.int32, (LANES, LANES), 0)
    coarse = lax.broadcasted_iota(jnp.int32, (LANES, LANES), 1)
    return jnp.where((fine >> 1) == coarse, F32(weight), F32(0))


def exact_dot(left, right):
    return jnp.dot(left, right, precision=lax.Precision.HIGHEST, preferred_element_type=F32)


def call(body, name, outs, args, scratch=(), scalars=()):
    vmem = pl.BlockSpec(memory_space=pltpu.VMEM)
    smem = pl.BlockSpec(memory_space=pltpu.SMEM)
    return pl.pallas_call(
        body,
        name=name,
        out_shape=[jax.ShapeDtypeStruct((rows, LANES), F32) for rows in outs],
        in_specs=[smem] * len(scalars) + [vmem] * len(args),
        out_specs=[vmem] * len(outs),
        scratch_shapes=[pltpu.VMEM((rows, LANES), F32) for rows in scratch],
        compiler_params=pltpu.CompilerParams(vmem_limit_bytes=40 * 1024 * 1024),
    )(*scalars, *args)


class Stream:
    def __init__(self, count, rows, planes, halo, reach):
        self.count, self.rows, self.planes, self.halo, self.reach = count, rows, planes, halo, reach

    def extent(self, depth):
        return self.reach - depth

    def halo_rows(self):
        return self.halo * self.count * self.rows

    def grown_rows(self):
        return (self.planes + 2 * self.halo) * self.count * 16


FINE = [Stream(STATIC, 8, 8, 2, 2), Stream(3, 8, 8, 3, 3), Stream(1, 8, 8, 3, 3), Stream(1, 8, 8, 3, 3)]
MIDDLE = [Stream(18, 4, 4, 3, 4), Stream(3, 4, 4, 4, 5), Stream(3, 8, 8, 2, 2), Stream(1, 8, 8, 2, 2), Stream(1, 8, 8, 2, 2)]


def x_rows(streams):
    return sum(s.halo_rows() for s in streams)


def y_pieces(streams):
    offset = 0
    pieces = []
    for depth in range(1, 1 + max(s.halo for s in streams)):
        for index, s in enumerate(streams):
            if depth <= s.halo:
                planes = s.planes + 2 * s.extent(depth)
                pieces.append((index, depth, offset))
                offset += planes * s.count
    return pieces, offset


def y_rows(streams):
    total = y_pieces(streams)[1]
    return -(-total // 8) * 8


def pack_x(streams, mains, up, down):
    offset = 0
    for s, main in zip(streams, mains):
        size = s.halo_rows()
        whole = s.planes * s.count * s.rows
        up[pl.ds(offset, size), :] = main[pl.ds(whole - size, size), :]
        down[pl.ds(offset, size), :] = main[pl.ds(0, size), :]
        offset += size


def pack_y(streams, mains, low, high, up, down):
    starts = [sum(s.halo_rows() for s in streams[:i]) for i in range(len(streams))]
    pieces, total = y_pieces(streams)
    padded = y_rows(streams)
    for out, upward in ((up, True), (down, False)):
        if padded > total:
            out[pl.ds(padded - 8, 8), :] = jnp.zeros((8, LANES), F32)
        for index, depth, offset in pieces:
            s = streams[index]
            row = s.rows - depth if upward else depth - 1
            beyond = s.extent(depth)
            side = beyond * s.count
            middle = s.planes * s.count
            if beyond:
                first = starts[index] + (s.halo - beyond) * s.count * s.rows + row
                out[pl.ds(offset, side), :] = low[pl.ds(first, side, s.rows), :]
            out[pl.ds(offset + side, middle), :] = mains[index][pl.ds(row, middle, s.rows), :]
            if beyond:
                out[pl.ds(offset + side + middle, side), :] = high[pl.ds(starts[index] + row, side, s.rows), :]


def grow(streams, mains, low, high, below, above, grown):
    starts = [sum(s.halo_rows() for s in streams[:i]) for i in range(len(streams))]
    for index, s in enumerate(streams):
        out = grown[index]
        out[...] = jnp.zeros(out.shape, F32)
        edge = s.halo * s.count
        middle = s.planes * s.count
        for source, base, first, number in (
            (low, starts[index], 0, edge),
            (mains[index], 0, edge, middle),
            (high, starts[index], edge + middle, edge),
        ):
            if s.rows == 8:
                for tile in range(number):
                    out[pl.ds((first + tile) * 16, 8), :] = source[pl.ds(base + tile * 8, 8), :]
            else:
                for row in range(s.rows):
                    out[pl.ds(first * 16 + row, number, 16), :] = source[pl.ds(base + row, number, s.rows), :]
    for index, depth, offset in y_pieces(streams)[0]:
        s = streams[index]
        beyond = s.extent(depth)
        number = (s.planes + 2 * beyond) * s.count
        first = (s.halo - beyond) * s.count * 16
        grown[index][pl.ds(first + s.rows + depth - 1, number, 16), :] = above[pl.ds(offset, number), :]
        grown[index][pl.ds(first + 16 - depth, number, 16), :] = below[pl.ds(offset, number), :]


def prepare(c, d, b, g, stat, field, total, zup, zdown, coef1, scale1, total1, summed, means1, half2, sum2, sum3):
    lane = lanes_of(8)
    for x in range(8):
        up = jnp.zeros((8, LANES), F32)
        down = jnp.zeros((8, LANES), F32)
        packed = []
        for e in range(3):
            w = [c[6 * e + k, x] for k in range(6)]
            tot = d[e, x] + (((w[0] + w[1]) + (w[2] + w[3])) + (w[4] + w[5]))
            inverse = 0.8 / tot
            for k in range(6):
                packed.append((6 * e + k, w[k] * inverse))
            packed.append((18 + e, b[e, x] * inverse))
            field[pl.ds((x * 3 + e) * 8, 8), :] = g[e, x]
            total[pl.ds((x * 3 + e) * 8, 8), :] = tot * 1.25
        for a, value in packed:
            stat[pl.ds((x * STATIC + a) * 8, 8), :] = value
            inside = (lane >= 2 * a) & (lane < 2 * a + 2)
            up = jnp.where(inside, rolled(value, 2 * a + 2, 1), up)
            down = jnp.where(inside, rolled(value, 2 * a, 1), down)
        for e in range(3):
            base = 42 + 3 * e
            inside = (lane >= base) & (lane < base + 3)
            up = jnp.where(inside, rolled(g[e, x], base + 3, 1), up)
            down = jnp.where(inside, rolled(g[e, x], base, 1), down)
        zup[pl.ds(x * 8, 8), :] = up
        zdown[pl.ds(x * 8, 8), :] = down

    halve = pair_matrix(0.125)
    for x in range(4):
        for a in range(STATIC):
            one = c[a, 2 * x] + c[a, 2 * x + 1] if a < 18 else d[a - 18, 2 * x] + d[a - 18, 2 * x + 1]
            summed[pl.ds((x * STATIC + a) * 8, 8), :] = one
    means1[...] = exact_dot(summed[pl.ds(0, 336, 2), :] + summed[pl.ds(1, 336, 2), :], halve)
    for x in range(4):
        for e in range(3):
            w = [0.25 * means1[pl.ds((x * STATIC + 6 * e + k) * 4, 4), :] for k in range(6)]
            tot = means1[pl.ds((x * STATIC + 18 + e) * 4, 4), :] + (((w[0] + w[1]) + (w[2] + w[3])) + (w[4] + w[5]))
            tot = jnp.where(tot > 0, tot, F32(1))
            inverse = 0.8 / tot
            for k in range(6):
                coef1[pl.ds((x * 18 + 6 * e + k) * 4, 4), :] = w[k] * inverse
            scale1[pl.ds((x * 3 + e) * 4, 4), :] = inverse
            total1[pl.ds((x * 3 + e) * 4, 4), :] = tot * 1.25
    half2[...] = means1[pl.ds(0, 168, 2), :] + means1[pl.ds(1, 168, 2), :]
    for i in range(2):
        sum2[pl.ds(42 * i, 42), :] = half2[pl.ds(84 * i, 42), :] + half2[pl.ds(84 * i + 42, 42), :]
    sum2[pl.ds(0, MEANS), :] = exact_dot(sum2[...], halve)[:MEANS]
    sum3[pl.ds(0, 42), :] = sum2[pl.ds(0, 42), :] + sum2[pl.ds(42, 42), :]
    sum3[pl.ds(42, 6), :] = jnp.zeros((6, LANES), F32)
    means3 = exact_dot(sum3[pl.ds(0, 24, 2), :] + sum3[pl.ds(1, 24, 2), :], halve)
    sum2[pl.ds(0, STATIC), :] = sum2[pl.ds(0, STATIC), :] + rolled(means3, 32, 1)[:STATIC]
    zup[pl.ds(64, MEANS), :] = sum2[pl.ds(0, MEANS), :]
    zdown[pl.ds(64, MEANS), :] = sum2[pl.ds(0, MEANS), :]


def prepare_whole(c, d, b, g, stat, field, total, zup, zdown, coef1, scale1, total1, summed, means1, half2, sum2, sum3):
    sum2[pl.ds(80, 8), :] = jnp.zeros((8, LANES), F32)
    prepare(c, d, b, g, stat, field, total, zup, zdown, coef1, scale1, total1, summed, means1, half2, sum2, sum3)
    for out in (zup, zdown):
        out[pl.ds(148, 4), :] = jnp.zeros((4, LANES), F32)


Z_ROWS = 152


def fine_x(stat, field, zlow, zhigh, zown, up, down, gathered):
    pack_x(FINE, [stat, field, zlow, zhigh], up, down)
    lane = lanes_of(MEANS)
    low, own, high = (ref[pl.ds(64, MEANS), :] for ref in (zlow, zown, zhigh))
    value = jnp.zeros((MEANS, LANES), F32)
    for source, shift, first, last in (
        (low, -12, 0, 20),
        (own, 20, 20, 52),
        (high, 52, 52, 72),
        (low, 34, 72, 82),
        (own, 50, 82, 98),
        (high, 66, 98, 108),
    ):
        value = jnp.where((lane >= first) & (lane < last), rolled(source, shift, 1), value)
    gathered[pl.ds(0, MEANS), :] = value
    gathered[pl.ds(MEANS, 4), :] = jnp.zeros((4, LANES), F32)


def fine_y(stat, field, zlow, zhigh, low, high, up, down):
    pack_y(FINE, [stat, field, zlow, zhigh], low, high, up, down)


def z_near(tiles):
    if len(tiles) == 1:
        return [rolled(tiles[0], -1, 1)], [rolled(tiles[0], 1, 1)]
    lane = lanes_of(tiles[0].shape[0])
    ahead = [rolled(t, -1, 1) for t in tiles]
    behind = [rolled(t, 1, 1) for t in tiles]
    last, first = lane == LANES - 1, lane == 0
    plus = [jnp.where(last, ahead[1], ahead[0]), jnp.where(last, ahead[0], ahead[1])]
    minus = [jnp.where(first, behind[1], behind[0]), jnp.where(first, behind[0], behind[1])]
    return plus, minus


def swept(x, value, coef, tiles):
    plus, minus = z_near(value[x])
    out = []
    for t in range(tiles):
        v = value[x][t]
        near = [value[x + 1][t], value[x - 1][t], rolled(v, -1, 0), rolled(v, 1, 0), plus[t], minus[t]]
        terms = [coef(x, k, t) * near[k] for k in range(6)]
        out.append((0.2 * v + coef(x, 6, t)) + (((terms[0] + terms[1]) + (terms[2] + terms[3])) + (terms[4] + terms[5])))
    return out


def side_tile(zlow, zhigh, row, base, width):
    lane = lanes_of(16)
    high = rolled(zhigh[pl.ds(row, 16), :], -base, 1)
    low = rolled(zlow[pl.ds(row, 16), :], -width - base, 1)
    return jnp.where(lane < width, high, jnp.where(lane >= LANES - width, low, F32(0)))


def fine_coef(stat, zlow, zhigh, e):
    cache = {}

    def coef(x, k, t):
        a = 6 * e + k if k < 6 else 18 + e
        if t == 0:
            return stat[pl.ds(((x + 2) * STATIC + a) * 16, 16), :]
        if (x, k) not in cache:
            cache[x, k] = side_tile(zlow, zhigh, (x + 3) * 16, 2 * a, 2)
        return cache[x, k]

    return coef


def fine_sweeps(stat0, field0, zlow0, zhigh0, low, high, below, above, total, coef1, scale1,
                stat, zlow, zhigh, field2, middle, zup, zdown, field, sums):
    grow(FINE, [stat0, field0, zlow0, zhigh0], low, high, below, above, [stat, field, zlow, zhigh])
    for e in range(3):
        coef = fine_coef(stat, zlow, zhigh, e)
        value = {}
        for x in range(-3, 11):
            value[x] = [
                field[pl.ds(((x + 3) * 3 + e) * 16, 16), :],
                side_tile(zlow, zhigh, (x + 3) * 16, 42 + 3 * e, 3),
            ]
        value = {x: swept(x, value, coef, 2) for x in range(-2, 10)}
        value = {x: swept(x, value, coef, 2) for x in range(-1, 9)}
        resid = []
        for x in range(8):
            now = value[x][0]
            field2[pl.ds((x * 3 + e) * 8, 8), :] = now[:8]
            change = swept(x, value, coef, 1)[0] - now
            resid.append(change[:8] * total[pl.ds((x * 3 + e) * 8, 8), :])
        for x in range(4):
            sums[pl.ds((x * 3 + e) * 8, 8), :] = resid[2 * x] + resid[2 * x + 1]
    right = exact_dot(sums[pl.ds(0, 48, 2), :] + sums[pl.ds(1, 48, 2), :], pair_matrix(0.125))
    middle[pl.ds(0, 288), :] = coef1[...]
    middle[pl.ds(288, 48), :] = right * scale1[...]
    lane = lanes_of(48)
    up = jnp.zeros((48, LANES), F32)
    down = jnp.zeros((48, LANES), F32)
    for group in range(7):
        value = middle[pl.ds(48 * group, 48), :]
        inside = (lane >= 4 * group) & (lane < 4 * group + 4)
        up = jnp.where(inside, rolled(value, 4 * group - 60, 1), up)
        down = jnp.where(inside, rolled(value, 4 * group, 1), down)
    zup[pl.ds(64, 48), :] = up
    zdown[pl.ds(64, 48), :] = down
    lane = lanes_of(8)
    for x in range(8):
        up = jnp.zeros((8, LANES), F32)
        down = jnp.zeros((8, LANES), F32)
        for e in range(3):
            value = field2[pl.ds((x * 3 + e) * 8, 8), :]
            inside = (lane >= 2 * e) & (lane < 2 * e + 2)
            up = jnp.where(inside, rolled(value, 2 * e + 2, 1), up)
            down = jnp.where(inside, rolled(value, 2 * e, 1), down)
        zup[pl.ds(x * 8, 8), :] = up
        zdown[pl.ds(x * 8, 8), :] = down


def middle_x(middle, field, zlow, zhigh, coef, right, up, down):
    lane = lanes_of(48)
    low, high = zlow[pl.ds(64, 48), :], zhigh[pl.ds(64, 48), :]
    for group in range(7):
        value = middle[pl.ds(48 * group, 48), :]
        value = jnp.where((lane >= 64) & (lane < 68), rolled(high, 64 - 4 * group, 1), value)
        value = jnp.where(lane >= 124, rolled(low, 124 - 4 * group, 1), value)
        if group < 6:
            coef[pl.ds(48 * group, 48), :] = value
        else:
            right[...] = value
    pack_x(MIDDLE, [coef, right, field, zlow, zhigh], up, down)


def middle_y(coef, right, field, zlow, zhigh, low, high, up, down):
    pack_y(MIDDLE, [coef, right, field, zlow, zhigh], low, high, up, down)


def middle_coef(coef, right, e):
    def get(x, k, t):
        if k < 6:
            return coef[pl.ds(((x + 3) * 18 + 6 * e + k) * 16, 16), :]
        return right[pl.ds(((x + 4) * 3 + e) * 16, 16), :]

    return get


def middle_sweeps(coef0, right0, field0, zlow0, zhigh0, low, high, below, above, total1,
                  coef, right, field, zlow, zhigh, error, coarse, sums):
    grow(MIDDLE, [coef0, right0, field0, zlow0, zhigh0], low, high, below, above, [coef, right, field, zlow, zhigh])
    for e in range(3):
        get = middle_coef(coef, right, e)
        value = {x: [get(x, 6, 0)] for x in range(-4, 8)}
        value = {x: swept(x, value, get, 1) for x in range(-3, 7)}
        for x in range(-3, 7):
            error[pl.ds(((x + 3) * 3 + e) * 16, 16), :] = value[x][0]
        resid = []
        for x in range(4):
            change = swept(x, value, get, 1)[0] - value[x][0]
            resid.append(change[:4] * total1[pl.ds((x * 3 + e) * 4, 4), :])
        for i in range(2):
            sums[pl.ds((i * 3 + e) * 4, 4), :] = resid[2 * i] + resid[2 * i + 1]
    sums[pl.ds(24, 8), :] = jnp.zeros((8, LANES), F32)
    coarse[...] = exact_dot(sums[pl.ds(0, 16, 2), :] + sums[pl.ds(1, 16, 2), :], pair_matrix(0.125))


def spread(coarse, zlow, zhigh, out, wide):
    lane = lanes_of(16)
    value = jnp.where(lane < HALO2, rolled(zlow[...], -12, 1), F32(0))
    value = jnp.where((lane >= 20) & (lane < 52), rolled(coarse[...], 20, 1), value)
    value = jnp.where((lane >= 52) & (lane < 72), rolled(zhigh[...], 52, 1), value)
    wide[...] = value
    lane = lanes_of(8)
    first, second = wide[pl.ds(0, 8), :], wide[pl.ds(6, 8), :]
    block = jnp.where(lane < 64, first, rolled(second, 64, 1))
    tail = jnp.zeros((1, LANES), F32)
    lane = lanes_of(1)
    for row in range(12):
        inside = (lane >= 8 * row) & (lane < 8 * row + 8)
        tail = jnp.where(inside, rolled(wide[pl.ds(row, 1), :], 8 * row - 64, 1), tail)
    rows = lax.broadcasted_iota(jnp.int32, (8, LANES), 0)
    block = jnp.where(rows < 6, block, jnp.where(rows == 6, jnp.broadcast_to(tail, (8, LANES)), F32(0)))
    for copy in range(out.shape[0] // 8):
        out[pl.ds(copy * 8, 8), :] = block


def coarse_levels(gx, gy, me_x, me_y, packed, means, coef, total, coef3, error2, rows6):
    planes = 2 * gx
    lane = lanes_of(gy)
    used = lane < 72
    row = lax.broadcasted_iota(jnp.int32, (gy, LANES), 0)
    first_row, last_row = row == 0, row == gy - 1
    zero = jnp.zeros((gy, LANES), F32)

    def place(x, e, j):
        return (x * 3 + e) * 2 + j

    for g in range(gx):
        blocks = [packed[pl.ds(g * gy * 8 + r, gy, 8), :] for r in range(7)]
        for i in range(2):
            x = 2 * g + i
            for e in range(3):
                for j in range(2):

                    def mean(a):
                        return jnp.where(used, means[pl.ds(g * gy * 88 + i * 42 + a * 2 + j, gy, 88), :], F32(0))

                    w = [mean(6 * e + k) * 0.0625 for k in range(6)]
                    tot = mean(18 + e) + (((w[0] + w[1]) + (w[2] + w[3])) + (w[4] + w[5]))
                    tot = jnp.where(tot > 0, tot, F32(1))
                    inverse = 0.8 / tot
                    r = (i * 3 + e) * 2 + j
                    right = blocks[r] if r < 6 else rolled(blocks[r - 6], 64, 1)
                    right = jnp.where(lane < 64, right, rolled(blocks[6], 64 - 8 * r, 1))
                    right = jnp.where(used, right, F32(0))
                    base = place(x, e, j)
                    for k in range(6):
                        coef[pl.ds((base * 7 + k) * gy, gy), :] = w[k] * inverse
                    coef[pl.ds((base * 7 + 6) * gy, gy), :] = right * inverse
                    total[pl.ds(base * gy, gy), :] = tot * 1.25
        for e in range(3):

            def mean3(a):
                value = rolled(means[pl.ds(g * gy * 88 + a, gy, 88), :], -72, 1)
                return jnp.where(lane < 36, value, F32(0))

            w = [mean3(6 * e + k) * 0.015625 for k in range(6)]
            tot = mean3(18 + e) + (((w[0] + w[1]) + (w[2] + w[3])) + (w[4] + w[5]))
            inverse = 0.8 / jnp.where(tot > 0, tot, F32(1))
            for k in range(6):
                coef3[pl.ds(((g * 3 + e) * 7 + k) * gy, gy), :] = w[k] * inverse
            coef3[pl.ds(((g * 3 + e) * 7 + 6) * gy, gy), :] = inverse

    def sweep2(value, x, e, j):
        base = place(x, e, j)
        v = value[x, j]
        near = [
            value[x + 1, j] if x + 1 < planes else None,
            value[x - 1, j] if x > 0 else None,
            value[x, 1] if j == 0 else jnp.where(last_row, zero, rolled(value[x, 0], -1, 0)),
            value[x, 0] if j == 1 else jnp.where(first_row, zero, rolled(value[x, 1], 1, 0)),
            rolled(v, -1, 1),
            rolled(v, 1, 1),
        ]
        out = 0.2 * v + coef[pl.ds((base * 7 + 6) * gy, gy), :]
        for k in range(6):
            if near[k] is not None:
                out = out + coef[pl.ds((base * 7 + k) * gy, gy), :] * near[k]
        return out

    cells = [(x, j) for x in range(planes) for j in range(2)]
    halve, double = pair_matrix(0.125), None
    fine = lax.broadcasted_iota(jnp.int32, (LANES, LANES), 1)
    coarse = lax.broadcasted_iota(jnp.int32, (LANES, LANES), 0)
    double = jnp.where((fine >> 1) == coarse, F32(1), F32(0))
    for ref in (error2,):
        ref[...] = jnp.zeros(ref.shape, F32)
    before, sums = [], []
    for e in range(3):
        value = {(x, j): coef[pl.ds((place(x, e, j) * 7 + 6) * gy, gy), :] for x, j in cells}
        value = {(x, j): sweep2(value, x, e, j) for x, j in cells}
        before.append(value)
        resid = {
            (x, j): (sweep2(value, x, e, j) - value[x, j]) * total[pl.ds(place(x, e, j) * gy, gy), :] for x, j in cells
        }
        for g in range(gx):
            sums.append(
                (resid[2 * g, 0] + resid[2 * g, 1]) + (resid[2 * g + 1, 0] + resid[2 * g + 1, 1])
            )
    right3 = exact_dot(jnp.concatenate(sums, axis=0), halve)
    found = []
    for e in range(3):

        def coef_of(g, k):
            return coef3[pl.ds(((g * 3 + e) * 7 + k) * gy, gy), :]

        right = [right3[(e * gx + g) * gy : (e * gx + g + 1) * gy] * coef_of(g, 6) for g in range(gx)]
        value = right
        for step in range(7):
            new = []
            for g in range(gx):
                v = value[g]
                out = 0.2 * v + right[g]
                if g + 1 < gx:
                    out = out + coef_of(g, 0) * value[g + 1]
                if g > 0:
                    out = out + coef_of(g, 1) * value[g - 1]
                out = out + coef_of(g, 2) * jnp.where(last_row, zero, rolled(v, -1, 0))
                out = out + coef_of(g, 3) * jnp.where(first_row, zero, rolled(v, 1, 0))
                out = out + coef_of(g, 4) * rolled(v, -1, 1)
                out = out + coef_of(g, 5) * rolled(v, 1, 1)
                new.append(out)
            value = new
        found.extend(value)
    refined = exact_dot(jnp.concatenate(found, axis=0), double)
    for e in range(3):
        value = {
            (x, j): before[e][x, j] + refined[(e * gx + x // 2) * gy : (e * gx + x // 2 + 1) * gy] for x, j in cells
        }
        for step in range(2):
            value = {(x, j): sweep2(value, x, e, j) for x, j in cells}
        for x, j in cells:
            error2[pl.ds(place(x + 2, e, j) * (gy + 16) + 8, gy), :] = value[x, j]
    for plane in range(6):
        for e in range(3):
            for step, j, target in ((0, 0, 0), (0, 1, 1), (1, 0, 2), (1, 1, 3), (-1, 0, 6), (-1, 1, 7)):
                start = (((2 * me_x + plane) * 3 + e) * 2 + j) * (gy + 16) + 8 + me_y + step
                rows6[pl.ds((plane * 3 + e) * 8 + target, 1), :] = error2[pl.ds(start, 1), :]
            rows6[pl.ds((plane * 3 + e) * 8 + 4, 2), :] = jnp.zeros((2, LANES), F32)


def finish(gx, gy, place, packed, means, error1, coef1, right1, stat, zlow0, zhigh0, field2, zlow2, zhigh2, out,
           coef2, total2, coef3, error2, rows6, fine2, rows1, fine1):
    coarse_levels(gx, gy, place[0], place[1], packed, means, coef2, total2, coef3, error2, rows6)

    source = lax.broadcasted_iota(jnp.int32, (LANES, LANES), 0)
    target = lax.broadcasted_iota(jnp.int32, (LANES, LANES), 1)
    cell = jnp.where(target >= 96, target - LANES, target)
    wanted = (cell >= -4) & (cell < 68) & ((cell >> 1) + HALO2 == source)
    widened = exact_dot(rows6[...], jnp.where(wanted, F32(1), F32(0)))
    fine2[pl.ds(0, 144, 2), :] = widened
    fine2[pl.ds(1, 144, 2), :] = widened

    row = lax.broadcasted_iota(jnp.int32, (8, LANES), 0)
    for e in range(3):
        get = middle_coef(coef1, right1, e)
        value = {}
        for x in range(-3, 7):
            value[x] = [
                error1[pl.ds(((x + 3) * 3 + e) * 16, 16), :] + fine2[pl.ds(((x // 2 + 2) * 3 + e) * 16, 16), :]
            ]
        value = {x: swept(x, value, get, 1) for x in range(-2, 6)}
        value = {x: swept(x, value, get, 1) for x in range(-1, 5)}
        for x in range(-1, 5):
            whole = value[x][0]
            rows1[pl.ds(((x + 1) * 3 + e) * 8, 8), :] = jnp.where(row == 7, whole[8:], whole[:8])

    inner = jnp.where((target >> 1) == source, F32(1), F32(0))
    outer = jnp.where((target < 2) & (source == 64), F32(1), F32(0))
    outer = jnp.where((target >= 126) & (source == 127), F32(1), outer)
    for tile, matrix in ((0, inner), (1, outer)):
        widened = exact_dot(rows1[...], matrix)
        fine1[pl.ds(288 * tile, 144, 2), :] = widened
        fine1[pl.ds(288 * tile + 1, 144, 2), :] = widened

    for e in range(3):
        get = fine_coef(stat, zlow0, zhigh0, e)
        value = {}
        for x in range(-2, 10):
            start = ((x // 2 + 1) * 3 + e) * 16
            value[x] = [
                field2[pl.ds(((x + 2) * 3 + e) * 16, 16), :] + fine1[pl.ds(start, 16), :],
                side_tile(zlow2, zhigh2, (x + 2) * 16, 2 * e, 2) + fine1[pl.ds(288 + start, 16), :],
            ]
        value = {x: swept(x, value, get, 2) for x in range(-1, 9)}
        for x in range(8):
            out[e, x] = swept(x, value, get, 1)[0][:8]


def both_ways(axis, up, down):
    devices = lax.axis_size(axis)
    pairs = [(i, i + 1) for i in range(devices - 1)]
    return lax.ppermute(up, axis, pairs), lax.ppermute(down, axis, [(b, a) for a, b in pairs])


def per_device(couplings, diagonal, right_side, guess):
    gx, gy = lax.axis_size("gx"), lax.axis_size("gy")
    place = jnp.stack([lax.axis_index("gx"), lax.axis_index("gy")]).astype(jnp.int32)

    stat, field, total, zup, zdown, coef1, scale1, total1 = call(
        prepare_whole, "prepare", [1344, 192, 192, Z_ROWS, Z_ROWS, 288, 48, 48],
        [couplings, diagonal, right_side, guess], scratch=[672, 336, 168, 88, 48],
    )
    zlow, zhigh = both_ways("gz", zup, zdown)
    xup, xdown, shared = call(
        fine_x, "fine_x", [x_rows(FINE), x_rows(FINE), 88], [stat, field, zlow, zhigh, zup]
    )
    means = lax.all_gather(shared, ("gx", "gy"), tiled=True)
    xlow, xhigh = both_ways("gx", xup, xdown)
    yup, ydown = call(
        fine_y, "fine_y", [y_rows(FINE)] * 2, [stat, field, zlow, zhigh, xlow, xhigh]
    )
    ylow, yhigh = both_ways("gy", yup, ydown)
    stat_grown, zlow_grown, zhigh_grown, field2, middle, zup, zdown = call(
        fine_sweeps, "fine_sweeps",
        [FINE[0].grown_rows(), FINE[2].grown_rows(), FINE[3].grown_rows(), 192, 336, 112, 112],
        [stat, field, zlow, zhigh, xlow, xhigh, ylow, yhigh, total, coef1, scale1],
        scratch=[FINE[1].grown_rows(), 96],
    )

    zlow, zhigh = both_ways("gz", zup, zdown)
    coef1, right1, xup, xdown = call(
        middle_x, "middle_x", [288, 48, x_rows(MIDDLE), x_rows(MIDDLE)], [middle, field2, zlow, zhigh]
    )
    xlow, xhigh = both_ways("gx", xup, xdown)
    yup, ydown = call(
        middle_y, "middle_y", [y_rows(MIDDLE)] * 2, [coef1, right1, field2, zlow, zhigh, xlow, xhigh]
    )
    ylow, yhigh = both_ways("gy", yup, ydown)
    coef1, right1, field2, zlow2, zhigh2, error1, coarse = call(
        middle_sweeps, "middle_sweeps", [s.grown_rows() for s in MIDDLE] + [480, 16],
        [coef1, right1, field2, zlow, zhigh, xlow, xhigh, ylow, yhigh, total1], scratch=[32],
    )

    zlow, zhigh = both_ways("gz", coarse, coarse)
    (packed,) = call(spread, "spread", [gx * gy * 8], [coarse, zlow, zhigh], scratch=[16])
    packed = lax.all_to_all(packed.reshape(gx * gy, 8, LANES), ("gx", "gy"), 0, 0).reshape(gx * gy * 8, LANES)

    vmem = pl.BlockSpec(memory_space=pltpu.VMEM)
    args = [packed, means, error1, coef1, right1, stat_grown, zlow_grown, zhigh_grown, field2, zlow2, zhigh2]
    tiles = 12 * gx * gy
    scratch = [tiles * 7, tiles, gx * 21 * gy, (2 * gx + 4) * 6 * (gy + 16), 144, 288, 144, 576]
    return pl.pallas_call(
        lambda *refs: finish(gx, gy, *refs),
        name="finish",
        out_shape=jax.ShapeDtypeStruct(guess.shape, F32),
        in_specs=[pl.BlockSpec(memory_space=pltpu.SMEM)] + [vmem] * len(args),
        out_specs=vmem,
        scratch_shapes=[pltpu.VMEM((rows, LANES), F32) for rows in scratch],
        compiler_params=pltpu.CompilerParams(vmem_limit_bytes=40 * 1024 * 1024),
    )(place, *args)


def solution(mesh):
    spec = P(None, "gx", "gy", "gz")
    return jax.shard_map(per_device, mesh=mesh, in_specs=(spec,) * 4, out_specs=spec, check_vma=False)
```

time: 489 us -> 151 us (0.31)
  the two profiles are of different devices: /device:TPU:220 before, /device:TPU:1 now
where the time goes in v1:
time: 151 us
  waiting for transfers between devices  60.2 us (40%)
  starting transfers between devices  54.9 us (36%)
  between operations  13.6 us (9%)
  Pallas kernels  12.5 us (8%)
  local copies, waits for them, and re-layouts  9.58 us (6%)
    ppermute x7, waiting for transfers between devices, both_ways(): lax.ppermute(down, axis, [(b, a) for a, b in pairs])  30.9 us
    ppermute x7, starting transfers between devices, both_ways(): lax.ppermute(up, axis, pairs)  28.6 us
    ppermute x7, waiting for transfers between devices, both_ways(): lax.ppermute(up, axis, pairs)  15.6 us
    ppermute x7, starting transfers between devices, both_ways(): lax.ppermute(down, axis, [(b, a) for a, b in pairs])  14.6 us
    all_to_all x1, waiting for transfers between devices, per_device(): lax.all_to_all(packed.reshape(gx * gy, 8, LANES), ('gx', 'gy'), 0, 0)  13.7 us
    all_to_all x1, starting transfers between devices, per_device(): lax.all_to_all(packed.reshape(gx * gy, 8, LANES), ('gx', 'gy'), 0, 0)  11.7 us
    unnamed x18, local copies, waits for them, and re-layouts  9.58 us
    pallas_call x1, Pallas kernels, per_device(): pl.pallas_call(lambda *refs: finish(gx, gy, *refs), name='finish', out_sh...  6.62 us
  transfers between devices with their start and end apart: 16, of which 12 were waited for; matrix products, arithmetic and copies ran while one was open for 0% of the time, Pallas kernels for 3%

profile of v1, /device:TPU:1, one launch (start us, length us, event | category | flops | bytes accessed | tf_op | source)
XLA Modules:
  0.0 150.7 jit_solution(11935483690998429953)
XLA Ops:
  11.3 4.5 %collective-permute-start = (f32[152,128]{1,0:T(8,128)S(1)}, f32[152,128]{1,0:T(8,128)S(1)}, u32[]{:S(2)}, u32[]{:S(2)}) collective-permute-start(f32[152,128]{1,0:T(8,128)S(1)} %get-tuple-element.40.zown), channel_id=1, source_target_pairs={{0,1},{1,2},{2,3},{3,4},{4,5},{5,6},{6,7},{8,9},{9,10},{10,11},{11... | collective-permute-start | bytes 233480 | tf_op jit(solution)/shard_map/ppermute | solution.py:567
  15.8 5.6 %collective-permute-start.1 = (f32[152,128]{1,0:T(8,128)S(1)}, f32[152,128]{1,0:T(8,128)S(1)}, u32[]{:S(2)}, u32[]{:S(2)}) collective-permute-start(f32[152,128]{1,0:T(8,128)S(1)} %get-tuple-element.41), channel_id=1, source_target_pairs={{1,0},{2,1},{3,2},{4,3},{5,4},{6,5},{7,6},{9,8},{10,9},{11,10},{12... | collective-permute-start | bytes 233480 | tf_op jit(solution)/shard_map/ppermute | solution.py:567
  23.0 2.5 %collective-permute-start.2 = (f32[456,128]{1,0:T(8,128)S(1)}, f32[456,128]{1,0:T(8,128)S(1)}, u32[]{:S(2)}, u32[]{:S(2)}) collective-permute-start(f32[456,128]{1,0:T(8,128)S(1)} %get-tuple-element.42), channel_id=1, source_target_pairs={{0,64},{64,128},{128,192},{192,256},{256,320},{320,384},{384,448},... | collective-permute-start | bytes 700424 | tf_op jit(solution)/shard_map/ppermute | solution.py:567
  26.8 3.6 %collective-permute-done.2.low = f32[456,128]{1,0:T(8,128)S(1)} collective-permute-done((f32[456,128]{1,0:T(8,128)S(1)}, f32[456,128]{1,0:T(8,128)S(1)}, u32[]{:S(2)}, u32[]{:S(2)}) %collective-permute-start.2) | collective-permute-done | bytes 233504 | tf_op jit(solution)/shard_map/ppermute | solution.py:567
  30.4 4.1 %collective-permute-done.3.high = f32[456,128]{1,0:T(8,128)S(1)} collective-permute-done((f32[456,128]{1,0:T(8,128)S(1)}, f32[456,128]{1,0:T(8,128)S(1)}, u32[]{:S(2)}, u32[]{:S(2)}) %collective-permute-start.3) | collective-permute-done | bytes 233504 | tf_op jit(solution)/shard_map/ppermute | solution.py:567
  34.6 2.6 %collective-permute-start.4 = (f32[528,128]{1,0:T(8,128)S(1)}, f32[528,128]{1,0:T(8,128)S(1)}, u32[]{:S(2)}, u32[]{:S(2)}) collective-permute-start(f32[528,128]{1,0:T(8,128)S(1)} %get-tuple-element.44), channel_id=1, source_target_pairs={{0,8},{8,16},{16,24},{24,32},{32,40},{40,48},{48,56},{1,9},{9,17},... | collective-permute-start | bytes 811016 | tf_op jit(solution)/shard_map/ppermute | solution.py:567
  38.5 4.4 %collective-permute-done.4.below = f32[528,128]{1,0:T(8,128)S(1)} collective-permute-done((f32[528,128]{1,0:T(8,128)S(1)}, f32[528,128]{1,0:T(8,128)S(1)}, u32[]{:S(2)}, u32[]{:S(2)}) %collective-permute-start.4) | collective-permute-done | bytes 270368 | tf_op jit(solution)/shard_map/ppermute | solution.py:567
  42.8 4.9 %collective-permute-done.5.above = f32[528,128]{1,0:T(8,128)S(1)} collective-permute-done((f32[528,128]{1,0:T(8,128)S(1)}, f32[528,128]{1,0:T(8,128)S(1)}, u32[]{:S(2)}, u32[]{:S(2)}) %collective-permute-start.5) | collective-permute-done | bytes 270368 | tf_op jit(solution)/shard_map/ppermute | solution.py:567
  47.8 2.1 %fine_sweeps.1 = (f32[4032,128]{1,0:T(8,128)S(1)}, f32[224,128]{1,0:T(8,128)S(1)}, f32[224,128]{1,0:T(8,128)S(1)}, f32[192,128]{1,0:T(8,128)S(1)}, f32[336,128]{...) custom-call(f32[1344,128]{1,0:T(8,128)S(1)} %get-tuple-element.38.stat.stat0, ...), custom_call_target="tpu_custom_call" | custom-call | tf_op jit(solution)/shard_map/fine_sweeps/pallas_call | solution.py:38
  49.9 5.7 %collective-permute-start.6 = (f32[112,128]{1,0:T(8,128)S(1)}, f32[112,128]{1,0:T(8,128)S(1)}, u32[]{:S(2)}, u32[]{:S(2)}) collective-permute-start(f32[112,128]{1,0:T(8,128)S(1)} %get-tuple-element.51), channel_id=1, source_target_pairs={{0,1},{1,2},{2,3},{3,4},{4,5},{5,6},{6,7},{8,9},{9,10},{10,11},{11... | collective-permute-start | bytes 172040 | tf_op jit(solution)/shard_map/ppermute | solution.py:567
  55.5 1.9 %collective-permute-start.7 = (f32[112,128]{1,0:T(8,128)S(1)}, f32[112,128]{1,0:T(8,128)S(1)}, u32[]{:S(2)}, u32[]{:S(2)}) collective-permute-start(f32[112,128]{1,0:T(8,128)S(1)} %get-tuple-element.52), channel_id=1, source_target_pairs={{1,0},{2,1},{3,2},{4,3},{5,4},{6,5},{7,6},{9,8},{10,9},{11,10},{12... | collective-permute-start | bytes 172040 | tf_op jit(solution)/shard_map/ppermute | solution.py:567
  57.5 4.0 %collective-permute-done.7.zhigh.zhigh0 = f32[112,128]{1,0:T(8,128)S(1)} collective-permute-done((f32[112,128]{1,0:T(8,128)S(1)}, f32[112,128]{1,0:T(8,128)S(1)}, u32[]{:S(2)}, u32[]{:S(2)}) %collective-permute-start.7) | collective-permute-done | bytes 57376 | tf_op jit(solution)/shard_map/ppermute | solution.py:567
  61.6 3.2 %collective-permute-start.8 = (f32[344,128]{1,0:T(8,128)S(1)}, f32[344,128]{1,0:T(8,128)S(1)}, u32[]{:S(2)}, u32[]{:S(2)}) collective-permute-start(f32[344,128]{1,0:T(8,128)S(1)} %get-tuple-element.55), channel_id=1, source_target_pairs={{0,64},{64,128},{128,192},{192,256},{256,320},{320,384},{384,448},... | collective-permute-start | bytes 528392 | tf_op jit(solution)/shard_map/ppermute | solution.py:567
  67.2 4.3 %collective-permute-done.9.high = f32[344,128]{1,0:T(8,128)S(1)} collective-permute-done((f32[344,128]{1,0:T(8,128)S(1)}, f32[344,128]{1,0:T(8,128)S(1)}, u32[]{:S(2)}, u32[]{:S(2)}) %collective-permute-start.9) | collective-permute-done | bytes 176160 | tf_op jit(solution)/shard_map/ppermute | solution.py:567
  71.6 3.5 %collective-permute-start.10 = (f32[632,128]{1,0:T(8,128)S(1)}, f32[632,128]{1,0:T(8,128)S(1)}, u32[]{:S(2)}, u32[]{:S(2)}) collective-permute-start(f32[632,128]{1,0:T(8,128)S(1)} %get-tuple-element.57), channel_id=1, source_target_pairs={{0,8},{8,16},{16,24},{24,32},{32,40},{40,48},{48,56},{1,9},{9,17},... | collective-permute-start | bytes 970760 | tf_op jit(solution)/shard_map/ppermute | solution.py:567
  76.4 6.6 %collective-permute-done.10.below = f32[632,128]{1,0:T(8,128)S(1)} collective-permute-done((f32[632,128]{1,0:T(8,128)S(1)}, f32[632,128]{1,0:T(8,128)S(1)}, u32[]{:S(2)}, u32[]{:S(2)}) %collective-permute-start.10) | collective-permute-done | bytes 323616 | tf_op jit(solution)/shard_map/ppermute | solution.py:567
  83.0 9.2 %collective-permute-done.11.above = f32[632,128]{1,0:T(8,128)S(1)} collective-permute-done((f32[632,128]{1,0:T(8,128)S(1)}, f32[632,128]{1,0:T(8,128)S(1)}, u32[]{:S(2)}, u32[]{:S(2)}) %collective-permute-start.11) | collective-permute-done | bytes 323616 | tf_op jit(solution)/shard_map/ppermute | solution.py:567
  94.8 6.7 %collective-permute-start.12 = (f32[16,128]{1,0:T(8,128)S(1)}, f32[16,128]{1,0:T(8,128)S(1)}, u32[]{:S(2)}, u32[]{:S(2)}) collective-permute-start(f32[16,128]{1,0:T(8,128)S(1)} %get-tuple-element.60.coarse), channel_id=1, source_target_pairs={{0,1},{1,2},{2,3},{3,4},{4,5},{5,6},{6,7},{8,9},{9,10},{10,11},{11... | collective-permute-start | bytes 24584 | tf_op jit(solution)/shard_map/ppermute | solution.py:567
  101.4 1.9 %collective-permute-start.13 = (f32[16,128]{1,0:T(8,128)S(1)}, f32[16,128]{1,0:T(8,128)S(1)}, u32[]{:S(2)}, u32[]{:S(2)}) collective-permute-start(f32[16,128]{1,0:T(8,128)S(1)} %get-tuple-element.60.coarse), channel_id=1, source_target_pairs={{1,0},{2,1},{3,2},{4,3},{5,4},{6,5},{7,6},{9,8},{10,9},{11,10},{12... | collective-permute-start | bytes 24584 | tf_op jit(solution)/shard_map/ppermute | solution.py:567
  103.4 3.4 %collective-permute-done.13.zhigh = f32[16,128]{1,0:T(8,128)S(1)} collective-permute-done((f32[16,128]{1,0:T(8,128)S(1)}, f32[16,128]{1,0:T(8,128)S(1)}, u32[]{:S(2)}, u32[]{:S(2)}) %collective-permute-start.13) | collective-permute-done | bytes 8224 | tf_op jit(solution)/shard_map/ppermute | solution.py:567
  107.7 11.7 %all-to-all-start = ((f32[64,8,128]{2,1,0:T(8,128)}), f32[64,8,128]{2,1,0:T(8,128)S(1)}, u32[]{:S(2)}, u32[]{:S(2)}) async-start(f32[64,8,128]{2,1,0:T(8,128)} %bitcast.2), calls=%async_computation | async-start | bytes 524288 | tf_op jit(solution)/shard_map/all_to_all | solution.py:611
  119.5 13.7 %all-to-all-done = f32[64,8,128]{2,1,0:T(8,128)S(1)} async-done(((f32[64,8,128]{2,1,0:T(8,128)}), f32[64,8,128]{2,1,0:T(8,128)S(1)}, u32[]{:S(2)}, u32[]{:S(2)}) %all-to-all-start) | async-done | bytes 262176 | tf_op jit(solution)/shard_map/all_to_all | solution.py:611
  133.2 1.8 %copy-done = f32[5632,128]{1,0:T(8,128)S(1)} copy-done((f32[5632,128]{1,0:T(8,128)S(1)}, f32[5632,128]{1,0:T(8,128)}, u32[]{:S(2)}) %copy-start) | copy-done | bytes 2883608
  137.2 6.6 %finish.1 = f32[3,8,8,128]{3,2,1,0:T(8,128)} custom-call(s32[2]{0:T(128)S(1)} %pad_add_fusion.refs_0_, f32[512,128]{1,0:T(8,128)S(1)} %bitcast.4, f32[5632,128]{1,0:T(8,128)S(1)} %copy-done, f32[480,128]{1,0:T(8,128)S(1)} %get-tuple-element.62.refs_3_, f32[2880,128]{1,0:T(8,128)S(1)} %copy-done.2, f32[576,128]{1,0:T(8,128)S(1)} %get-tuple-element.64.refs_5_, ...), custom_call_target="tpu_custom_call" | custom-call | tf_op jit(solution)/shard_map/finish/pallas_call | solution.py:617
  (37 shorter events, 18.8 us)
Async XLA Ops:
  6.5 126.6 %all-gather.2.cloned.1.call-start = ((), (), s32[]{:S(2)}) async-start(), calls=%async_computation.1 | async-start | bytes 2928640 | tf_op jit(solution)/shard_map/all_gather | solution.py:582
  6.5 1.1 copy-start.3
  7.6 0.9 copy-start.6
  8.5 0.9 copy-start.7
  9.4 0.9 copy-start.8
  11.3 10.1 %collective-permute-start = (f32[152,128]{1,0:T(8,128)S(1)}, f32[152,128]{1,0:T(8,128)S(1)}, u32[]{:S(2)}, u32[]{:S(2)}) collective-permute-start(f32[152,128]{1,0:T(8,128)S(1)} %get-tuple-element.40.zown), channel_id=1, source_target_pairs={{0,1},{1,2},{2,3},{3,4},{4,5},{5,6},{6,7},{8,9},{9,10},{10,11},{11... | collective-permute-start | bytes 233480 | tf_op jit(solution)/shard_map/ppermute | solution.py:567
  15.8 6.5 %collective-permute-start.1 = (f32[152,128]{1,0:T(8,128)S(1)}, f32[152,128]{1,0:T(8,128)S(1)}, u32[]{:S(2)}, u32[]{:S(2)}) collective-permute-start(f32[152,128]{1,0:T(8,128)S(1)} %get-tuple-element.41), channel_id=1, source_target_pairs={{1,0},{2,1},{3,2},{4,3},{5,4},{6,5},{7,6},{9,8},{10,9},{11,10},{12... | collective-permute-start | bytes 233480 | tf_op jit(solution)/shard_map/ppermute | solution.py:567
  23.0 7.3 %collective-permute-start.2 = (f32[456,128]{1,0:T(8,128)S(1)}, f32[456,128]{1,0:T(8,128)S(1)}, u32[]{:S(2)}, u32[]{:S(2)}) collective-permute-start(f32[456,128]{1,0:T(8,128)S(1)} %get-tuple-element.42), channel_id=1, source_target_pairs={{0,64},{64,128},{128,192},{192,256},{256,320},{320,384},{384,448},... | collective-permute-start | bytes 700424 | tf_op jit(solution)/shard_map/ppermute | solution.py:567
  25.5 9.0 %collective-permute-start.3 = (f32[456,128]{1,0:T(8,128)S(1)}, f32[456,128]{1,0:T(8,128)S(1)}, u32[]{:S(2)}, u32[]{:S(2)}) collective-permute-start(f32[456,128]{1,0:T(8,128)S(1)} %get-tuple-element.43), channel_id=1, source_target_pairs={{64,0},{128,64},{192,128},{256,192},{320,256},{384,320},{448,384},... | collective-permute-start | bytes 700424 | tf_op jit(solution)/shard_map/ppermute | solution.py:567
  34.6 8.2 %collective-permute-start.4 = (f32[528,128]{1,0:T(8,128)S(1)}, f32[528,128]{1,0:T(8,128)S(1)}, u32[]{:S(2)}, u32[]{:S(2)}) collective-permute-start(f32[528,128]{1,0:T(8,128)S(1)} %get-tuple-element.44), channel_id=1, source_target_pairs={{0,8},{8,16},{16,24},{24,32},{32,40},{40,48},{48,56},{1,9},{9,17},... | collective-permute-start | bytes 811016 | tf_op jit(solution)/shard_map/ppermute | solution.py:567
  37.2 10.6 %collective-permute-start.5 = (f32[528,128]{1,0:T(8,128)S(1)}, f32[528,128]{1,0:T(8,128)S(1)}, u32[]{:S(2)}, u32[]{:S(2)}) collective-permute-start(f32[528,128]{1,0:T(8,128)S(1)} %get-tuple-element.45), channel_id=1, source_target_pairs={{8,0},{16,8},{24,16},{32,24},{40,32},{48,40},{56,48},{9,1},{17,9},... | collective-permute-start | bytes 811016 | tf_op jit(solution)/shard_map/ppermute | solution.py:567
  49.9 7.6 %collective-permute-start.6 = (f32[112,128]{1,0:T(8,128)S(1)}, f32[112,128]{1,0:T(8,128)S(1)}, u32[]{:S(2)}, u32[]{:S(2)}) collective-permute-start(f32[112,128]{1,0:T(8,128)S(1)} %get-tuple-element.51), channel_id=1, source_target_pairs={{0,1},{1,2},{2,3},{3,4},{4,5},{5,6},{6,7},{8,9},{9,10},{10,11},{11... | collective-permute-start | bytes 172040 | tf_op jit(solution)/shard_map/ppermute | solution.py:567
  55.5 5.9 %collective-permute-start.7 = (f32[112,128]{1,0:T(8,128)S(1)}, f32[112,128]{1,0:T(8,128)S(1)}, u32[]{:S(2)}, u32[]{:S(2)}) collective-permute-start(f32[112,128]{1,0:T(8,128)S(1)} %get-tuple-element.52), channel_id=1, source_target_pairs={{1,0},{2,1},{3,2},{4,3},{5,4},{6,5},{7,6},{9,8},{10,9},{11,10},{12... | collective-permute-start | bytes 172040 | tf_op jit(solution)/shard_map/ppermute | solution.py:567
  61.6 5.6 %collective-permute-start.8 = (f32[344,128]{1,0:T(8,128)S(1)}, f32[344,128]{1,0:T(8,128)S(1)}, u32[]{:S(2)}, u32[]{:S(2)}) collective-permute-start(f32[344,128]{1,0:T(8,128)S(1)} %get-tuple-element.55), channel_id=1, source_target_pairs={{0,64},{64,128},{128,192},{192,256},{256,320},{320,384},{384,448},... | collective-permute-start | bytes 528392 | tf_op jit(solution)/shard_map/ppermute | solution.py:567
  64.8 6.7 %collective-permute-start.9 = (f32[344,128]{1,0:T(8,128)S(1)}, f32[344,128]{1,0:T(8,128)S(1)}, u32[]{:S(2)}, u32[]{:S(2)}) collective-permute-start(f32[344,128]{1,0:T(8,128)S(1)} %get-tuple-element.56), channel_id=1, source_target_pairs={{64,0},{128,64},{192,128},{256,192},{320,256},{384,320},{448,384},... | collective-permute-start | bytes 528392 | tf_op jit(solution)/shard_map/ppermute | solution.py:567
  71.6 11.4 %collective-permute-start.10 = (f32[632,128]{1,0:T(8,128)S(1)}, f32[632,128]{1,0:T(8,128)S(1)}, u32[]{:S(2)}, u32[]{:S(2)}) collective-permute-start(f32[632,128]{1,0:T(8,128)S(1)} %get-tuple-element.57), channel_id=1, source_target_pairs={{0,8},{8,16},{16,24},{24,32},{32,40},{40,48},{48,56},{1,9},{9,17},... | collective-permute-start | bytes 970760 | tf_op jit(solution)/shard_map/ppermute | solution.py:567
  75.1 17.1 %collective-permute-start.11 = (f32[632,128]{1,0:T(8,128)S(1)}, f32[632,128]{1,0:T(8,128)S(1)}, u32[]{:S(2)}, u32[]{:S(2)}) collective-permute-start(f32[632,128]{1,0:T(8,128)S(1)} %get-tuple-element.58), channel_id=1, source_target_pairs={{8,0},{16,8},{24,16},{32,24},{40,32},{48,40},{56,48},{9,1},{17,9},... | collective-permute-start | bytes 970760 | tf_op jit(solution)/shard_map/ppermute | solution.py:567
  93.0 1.1 copy-start.1
  94.8 8.6 %collective-permute-start.12 = (f32[16,128]{1,0:T(8,128)S(1)}, f32[16,128]{1,0:T(8,128)S(1)}, u32[]{:S(2)}, u32[]{:S(2)}) collective-permute-start(f32[16,128]{1,0:T(8,128)S(1)} %get-tuple-element.60.coarse), channel_id=1, source_target_pairs={{0,1},{1,2},{2,3},{3,4},{4,5},{5,6},{6,7},{8,9},{9,10},{10,11},{11... | collective-permute-start | bytes 24584 | tf_op jit(solution)/shard_map/ppermute | solution.py:567
  101.4 5.4 %collective-permute-start.13 = (f32[16,128]{1,0:T(8,128)S(1)}, f32[16,128]{1,0:T(8,128)S(1)}, u32[]{:S(2)}, u32[]{:S(2)}) collective-permute-start(f32[16,128]{1,0:T(8,128)S(1)} %get-tuple-element.60.coarse), channel_id=1, source_target_pairs={{1,0},{2,1},{3,2},{4,3},{5,4},{6,5},{7,6},{9,8},{10,9},{11,10},{12... | collective-permute-start | bytes 24584 | tf_op jit(solution)/shard_map/ppermute | solution.py:567
  107.7 25.4 %all-to-all-start = ((f32[64,8,128]{2,1,0:T(8,128)}), f32[64,8,128]{2,1,0:T(8,128)S(1)}, u32[]{:S(2)}, u32[]{:S(2)}) async-start(f32[64,8,128]{2,1,0:T(8,128)} %bitcast.2), calls=%async_computation | async-start | bytes 524288 | tf_op jit(solution)/shard_map/all_to_all | solution.py:611
  133.2 1.8 %copy-start = (f32[5632,128]{1,0:T(8,128)S(1)}, f32[5632,128]{1,0:T(8,128)}, u32[]{:S(2)}) copy-start(f32[5632,128]{1,0:T(8,128)} %all-gather.2.cloned.1.call-done.refs_2_) | copy-start | bytes 8650756
  135.0 1.4 copy-start.2
  136.3 0.9 copy-start.5
  (1 other events, 0.6 us)
Sparse Core Ops, SparseCore 0:
  23.2 85.5 all-gather.1

commit v2 on v1

--- a/solution.py
+++ b/solution.py
@@ -8,8 +8,11 @@
 
 F32 = jnp.float32
 LANES = 128
+GRANT = 40 * 1024 * 1024
+FAR = 49152
 STATIC = 21
 HALO2 = 20
+SHARED = 64
 MEANS = 84
 
 
@@ -32,18 +35,19 @@
     return jnp.dot(left, right, precision=lax.Precision.HIGHEST, preferred_element_type=F32)
 
 
-def call(body, name, outs, args, scratch=(), scalars=()):
+def call(body, name, outs, args, scratch=(), far_args=(), far_outs=(), copies=0, grant=GRANT):
     vmem = pl.BlockSpec(memory_space=pltpu.VMEM)
-    smem = pl.BlockSpec(memory_space=pltpu.SMEM)
+    far = pl.BlockSpec(memory_space=pltpu.HBM)
+    semaphores = [pltpu.SemaphoreType.DMA((copies,))] if copies else []
     return pl.pallas_call(
         body,
         name=name,
-        out_shape=[jax.ShapeDtypeStruct((rows, LANES), F32) for rows in outs],
-        in_specs=[smem] * len(scalars) + [vmem] * len(args),
-        out_specs=[vmem] * len(outs),
-        scratch_shapes=[pltpu.VMEM((rows, LANES), F32) for rows in scratch],
-        compiler_params=pltpu.CompilerParams(vmem_limit_bytes=40 * 1024 * 1024),
-    )(*scalars, *args)
+        out_shape=[jax.ShapeDtypeStruct((rows, LANES), F32) for rows in (*outs, *far_outs)],
+        in_specs=[far] * len(far_args) + [vmem] * len(args),
+        out_specs=[vmem] * len(outs) + [far] * len(far_outs),
+        scratch_shapes=[pltpu.VMEM(r if isinstance(r, tuple) else (r, LANES), F32) for r in scratch] + semaphores,
+        compiler_params=pltpu.CompilerParams(vmem_limit_bytes=grant),
+    )(*far_args, *args)
 
 
 class Stream:
@@ -199,18 +203,30 @@
     zdown[pl.ds(64, MEANS), :] = sum2[pl.ds(0, MEANS), :]
 
 
-def prepare_whole(c, d, b, g, stat, field, total, zup, zdown, coef1, scale1, total1, summed, means1, half2, sum2, sum3):
+def prepare_whole(c_far, d_far, b_far, g_far, stat, field, total, zup, zdown, coef1, scale1, total1,
+                  c, d, b, g, summed, means1, half2, sum2, sum3, arrived):
+    copies = [
+        pltpu.make_async_copy(far, near, arrived.at[i])
+        for i, (far, near) in enumerate(((c_far, c), (d_far, d), (b_far, b), (g_far, g)))
+    ]
+    for copy in copies:
+        copy.start()
     sum2[pl.ds(80, 8), :] = jnp.zeros((8, LANES), F32)
+    for out in (zup, zdown):
+        out[pl.ds(144, 8), :] = jnp.zeros((8, LANES), F32)
+    for copy in copies:
+        copy.wait()
     prepare(c, d, b, g, stat, field, total, zup, zdown, coef1, scale1, total1, summed, means1, half2, sum2, sum3)
-    for out in (zup, zdown):
-        out[pl.ds(148, 4), :] = jnp.zeros((4, LANES), F32)
 
 
 Z_ROWS = 152
 
 
-def fine_x(stat, field, zlow, zhigh, zown, up, down, gathered):
+def fine_x(stat, field, zlow, zhigh, up, down):
     pack_x(FINE, [stat, field, zlow, zhigh], up, down)
+
+
+def share(zlow, zhigh, zown, shared, wide):
     lane = lanes_of(MEANS)
     low, own, high = (ref[pl.ds(64, MEANS), :] for ref in (zlow, zown, zhigh))
     value = jnp.zeros((MEANS, LANES), F32)
@@ -223,8 +239,23 @@
         (high, 66, 98, 108),
     ):
         value = jnp.where((lane >= first) & (lane < last), rolled(source, shift, 1), value)
-    gathered[pl.ds(0, MEANS), :] = value
-    gathered[pl.ds(MEANS, 4), :] = jnp.zeros((4, LANES), F32)
+    wide[pl.ds(80, 16), :] = jnp.zeros((16, LANES), F32)
+    wide[pl.ds(0, MEANS), :] = value
+    lane = lanes_of(48)
+    body = jnp.where(lane < 64, wide[pl.ds(0, 48), :], rolled(wide[pl.ds(42, 48), :], 64, 1))
+    lane = lanes_of(8)
+    tail = jnp.zeros((8, LANES), F32)
+    third = jnp.zeros((8, LANES), F32)
+    for group in range(11):
+        value = wide[pl.ds(8 * group, 8), :]
+        inside = (lane >= 8 * group) & (lane < 8 * group + 8)
+        tail = jnp.where(inside, rolled(value, 8 * group - 64, 1), tail)
+        if group < 3:
+            inside = (lane >= 36 * group) & (lane < 36 * group + 36)
+            third = jnp.where(inside, rolled(value, 36 * group - 72, 1), third)
+    shared[pl.ds(0, 48), :] = body
+    shared[pl.ds(48, 8), :] = tail
+    shared[pl.ds(56, 8), :] = third
 
 
 def fine_y(stat, field, zlow, zhigh, low, high, up, down):
@@ -254,14 +285,21 @@
     return out
 
 
-def side_tile(zlow, zhigh, row, base, width):
+def both_sides(zlow, zhigh, sides):
+    for tile in range(sides.shape[0] // 16):
+        rows = pl.ds(tile * 16, 16)
+        sides[rows, :] = jnp.where(lanes_of(16) < 64, zhigh[rows, :], rolled(zlow[rows, :], 64, 1))
+
+
+def side_tile(sides, row, base, width):
     lane = lanes_of(16)
-    high = rolled(zhigh[pl.ds(row, 16), :], -base, 1)
-    low = rolled(zlow[pl.ds(row, 16), :], -width - base, 1)
+    packed = sides[pl.ds(row, 16), :]
+    high = rolled(packed, -base, 1)
+    low = rolled(packed, -width - base - 64, 1)
     return jnp.where(lane < width, high, jnp.where(lane >= LANES - width, low, F32(0)))
 
 
-def fine_coef(stat, zlow, zhigh, e):
+def fine_coef(stat, sides, e):
     cache = {}
 
     def coef(x, k, t):
@@ -269,22 +307,25 @@
         if t == 0:
             return stat[pl.ds(((x + 2) * STATIC + a) * 16, 16), :]
         if (x, k) not in cache:
-            cache[x, k] = side_tile(zlow, zhigh, (x + 3) * 16, 2 * a, 2)
+            cache[x, k] = side_tile(sides, (x + 3) * 16, 2 * a, 2)
         return cache[x, k]
 
     return coef
 
 
 def fine_sweeps(stat0, field0, zlow0, zhigh0, low, high, below, above, total, coef1, scale1,
-                stat, zlow, zhigh, field2, middle, zup, zdown, field, sums):
+                sides, field2, middle, zup, zdown, stat_far, stat, field, zlow, zhigh, sums, left):
     grow(FINE, [stat0, field0, zlow0, zhigh0], low, high, below, above, [stat, field, zlow, zhigh])
+    keep = pltpu.make_async_copy(stat, stat_far.at[pl.ds(0, stat.shape[0]), :], left.at[0])
+    keep.start()
+    both_sides(zlow, zhigh, sides)
     for e in range(3):
-        coef = fine_coef(stat, zlow, zhigh, e)
+        coef = fine_coef(stat, sides, e)
         value = {}
         for x in range(-3, 11):
             value[x] = [
                 field[pl.ds(((x + 3) * 3 + e) * 16, 16), :],
-                side_tile(zlow, zhigh, (x + 3) * 16, 42 + 3 * e, 3),
+                side_tile(sides, (x + 3) * 16, 42 + 3 * e, 3),
             ]
         value = {x: swept(x, value, coef, 2) for x in range(-2, 10)}
         value = {x: swept(x, value, coef, 2) for x in range(-1, 9)}
@@ -320,6 +361,7 @@
             down = jnp.where(inside, rolled(value, 2 * e, 1), down)
         zup[pl.ds(x * 8, 8), :] = up
         zdown[pl.ds(x * 8, 8), :] = down
+    keep.wait()
 
 
 def middle_x(middle, field, zlow, zhigh, coef, right, up, down):
@@ -350,8 +392,11 @@
 
 
 def middle_sweeps(coef0, right0, field0, zlow0, zhigh0, low, high, below, above, total1,
-                  coef, right, field, zlow, zhigh, error, coarse, sums):
+                  right, field, sides, error, coarse, coef_far, coef, zlow, zhigh, sums, left):
     grow(MIDDLE, [coef0, right0, field0, zlow0, zhigh0], low, high, below, above, [coef, right, field, zlow, zhigh])
+    keep = pltpu.make_async_copy(coef, coef_far.at[pl.ds(0, coef.shape[0]), :], left.at[0])
+    keep.start()
+    both_sides(zlow, zhigh, sides)
     for e in range(3):
         get = middle_coef(coef, right, e)
         value = {x: [get(x, 6, 0)] for x in range(-4, 8)}
@@ -366,6 +411,7 @@
             sums[pl.ds((i * 3 + e) * 4, 4), :] = resid[2 * i] + resid[2 * i + 1]
     sums[pl.ds(24, 8), :] = jnp.zeros((8, LANES), F32)
     coarse[...] = exact_dot(sums[pl.ds(0, 16, 2), :] + sums[pl.ds(1, 16, 2), :], pair_matrix(0.125))
+    keep.wait()
 
 
 def spread(coarse, zlow, zhigh, out, wide):
@@ -388,52 +434,75 @@
         out[pl.ds(copy * 8, 8), :] = block
 
 
-def coarse_levels(gx, gy, me_x, me_y, packed, means, coef, total, coef3, error2, rows6):
+def coarse_place(x, e, j):
+    return (x * 3 + e) * 2 + j
+
+
+def coarse_coefs(gx, gy, shared, arrivals, coef, scale, total, coef3):
+    lane = lanes_of(gy)
+    used = lane < 72
+    for g in range(gx):
+        arrivals[g].wait()
+
+        def rows(r):
+            return shared[pl.ds(g * gy * SHARED + r, gy, SHARED), :]
+
+        tails = [rows(48 + r) for r in range(8)]
+        thirds = [rows(56 + r) for r in range(8)]
+
+        def settle(w, d):
+            tot = d + (((w[0] + w[1]) + (w[2] + w[3])) + (w[4] + w[5]))
+            tot = jnp.where(tot > 0, tot, F32(1))
+            return tot, 0.8 / tot
+
+        for e in range(3):
+            for j in range(2):
+                pairs = {a: rows(a * 2 + j) for a in [6 * e + k for k in range(6)] + [18 + e]}
+                for i in range(2):
+
+                    def mean(a):
+                        r = i * 42 + a * 2 + j
+                        value = pairs[a] if i == 0 else rolled(pairs[a], 64, 1)
+                        value = jnp.where(lane < 64, value, rolled(tails[r % 8], 64 - 8 * (r // 8), 1))
+                        return jnp.where(used, value, F32(0))
+
+                    w = [mean(6 * e + k) * 0.0625 for k in range(6)]
+                    tot, inverse = settle(w, mean(18 + e))
+                    base = coarse_place(2 * g + i, e, j)
+                    for k in range(6):
+                        coef[pl.ds((base * 6 + k) * gy, gy), :] = w[k] * inverse
+                    scale[pl.ds(base * gy, gy), :] = inverse
+                    total[pl.ds(base * gy, gy), :] = tot * 1.25
+
+            def mean3(a):
+                return jnp.where(lane < 36, rolled(thirds[a % 8], -36 * (a // 8), 1), F32(0))
+
+            w = [mean3(6 * e + k) * 0.015625 for k in range(6)]
+            tot, inverse = settle(w, mean3(18 + e))
+            for k in range(6):
+                coef3[pl.ds(((g * 3 + e) * 7 + k) * gy, gy), :] = w[k] * inverse
+            coef3[pl.ds(((g * 3 + e) * 7 + 6) * gy, gy), :] = inverse
+
+
+def coarse_levels(gx, gy, me_x, me_y, packed, coef, scale, total, coef3, right2, error2, rows6):
     planes = 2 * gx
+    place = coarse_place
     lane = lanes_of(gy)
     used = lane < 72
     row = lax.broadcasted_iota(jnp.int32, (gy, LANES), 0)
     first_row, last_row = row == 0, row == gy - 1
     zero = jnp.zeros((gy, LANES), F32)
 
-    def place(x, e, j):
-        return (x * 3 + e) * 2 + j
-
     for g in range(gx):
         blocks = [packed[pl.ds(g * gy * 8 + r, gy, 8), :] for r in range(7)]
         for i in range(2):
-            x = 2 * g + i
             for e in range(3):
                 for j in range(2):
-
-                    def mean(a):
-                        return jnp.where(used, means[pl.ds(g * gy * 88 + i * 42 + a * 2 + j, gy, 88), :], F32(0))
-
-                    w = [mean(6 * e + k) * 0.0625 for k in range(6)]
-                    tot = mean(18 + e) + (((w[0] + w[1]) + (w[2] + w[3])) + (w[4] + w[5]))
-                    tot = jnp.where(tot > 0, tot, F32(1))
-                    inverse = 0.8 / tot
                     r = (i * 3 + e) * 2 + j
                     right = blocks[r] if r < 6 else rolled(blocks[r - 6], 64, 1)
                     right = jnp.where(lane < 64, right, rolled(blocks[6], 64 - 8 * r, 1))
-                    right = jnp.where(used, right, F32(0))
-                    base = place(x, e, j)
-                    for k in range(6):
-                        coef[pl.ds((base * 7 + k) * gy, gy), :] = w[k] * inverse
-                    coef[pl.ds((base * 7 + 6) * gy, gy), :] = right * inverse
-                    total[pl.ds(base * gy, gy), :] = tot * 1.25
-        for e in range(3):
-
-            def mean3(a):
-                value = rolled(means[pl.ds(g * gy * 88 + a, gy, 88), :], -72, 1)
-                return jnp.where(lane < 36, value, F32(0))
-
-            w = [mean3(6 * e + k) * 0.015625 for k in range(6)]
-            tot = mean3(18 + e) + (((w[0] + w[1]) + (w[2] + w[3])) + (w[4] + w[5]))
-            inverse = 0.8 / jnp.where(tot > 0, tot, F32(1))
-            for k in range(6):
-                coef3[pl.ds(((g * 3 + e) * 7 + k) * gy, gy), :] = w[k] * inverse
-            coef3[pl.ds(((g * 3 + e) * 7 + 6) * gy, gy), :] = inverse
+                    base = place(2 * g + i, e, j) * gy
+                    right2[pl.ds(base, gy), :] = jnp.where(used, right, F32(0)) * scale[pl.ds(base, gy), :]
 
     def sweep2(value, x, e, j):
         base = place(x, e, j)
@@ -446,22 +515,21 @@
             rolled(v, -1, 1),
             rolled(v, 1, 1),
         ]
-        out = 0.2 * v + coef[pl.ds((base * 7 + 6) * gy, gy), :]
+        out = 0.2 * v + right2[pl.ds(base * gy, gy), :]
         for k in range(6):
             if near[k] is not None:
-                out = out + coef[pl.ds((base * 7 + k) * gy, gy), :] * near[k]
+                out = out + coef[pl.ds((base * 6 + k) * gy, gy), :] * near[k]
         return out
 
     cells = [(x, j) for x in range(planes) for j in range(2)]
-    halve, double = pair_matrix(0.125), None
+    halve = pair_matrix(0.125)
     fine = lax.broadcasted_iota(jnp.int32, (LANES, LANES), 1)
     coarse = lax.broadcasted_iota(jnp.int32, (LANES, LANES), 0)
     double = jnp.where((fine >> 1) == coarse, F32(1), F32(0))
-    for ref in (error2,):
-        ref[...] = jnp.zeros(ref.shape, F32)
+    error2[...] = jnp.zeros(error2.shape, F32)
     before, sums = [], []
     for e in range(3):
-        value = {(x, j): coef[pl.ds((place(x, e, j) * 7 + 6) * gy, gy), :] for x, j in cells}
+        value = {(x, j): right2[pl.ds(place(x, e, j) * gy, gy), :] for x, j in cells}
         value = {(x, j): sweep2(value, x, e, j) for x, j in cells}
         before.append(value)
         resid = {
@@ -513,9 +581,24 @@
             rows6[pl.ds((plane * 3 + e) * 8 + 4, 2), :] = jnp.zeros((2, LANES), F32)
 
 
-def finish(gx, gy, place, packed, means, error1, coef1, right1, stat, zlow0, zhigh0, field2, zlow2, zhigh2, out,
-           coef2, total2, coef3, error2, rows6, fine2, rows1, fine1):
-    coarse_levels(gx, gy, place[0], place[1], packed, means, coef2, total2, coef3, error2, rows6)
+def finish(gx, gy, shared_far, coef1_far, stat_far, packed, error1, right1, sides0, field2, sides2, out,
+           shared, coef1, stat, coef2, scale2, total2, coef3, right2, error2, rows6, fine2, rows1, fine1, arrived):
+    chunk = gy * SHARED
+    arrivals = [
+        pltpu.make_async_copy(shared_far.at[pl.ds(g * chunk, chunk), :], shared.at[pl.ds(g * chunk, chunk), :], arrived.at[g])
+        for g in range(gx)
+    ]
+    later = [
+        pltpu.make_async_copy(coef1_far.at[pl.ds(0, coef1.shape[0]), :], coef1, arrived.at[gx]),
+        pltpu.make_async_copy(stat_far.at[pl.ds(0, stat.shape[0]), :], stat, arrived.at[gx + 1]),
+    ]
+    for copy in arrivals + later:
+        copy.start()
+    coarse_coefs(gx, gy, shared, arrivals, coef2, scale2, total2, coef3)
+    me_x, me_y = lax.axis_index("gx"), lax.axis_index("gy")
+    coarse_levels(gx, gy, me_x, me_y, packed, coef2, scale2, total2, coef3, right2, error2, rows6)
+    for copy in later:
+        copy.wait()
 
     source = lax.broadcasted_iota(jnp.int32, (LANES, LANES), 0)
     target = lax.broadcasted_iota(jnp.int32, (LANES, LANES), 1)
@@ -548,13 +631,13 @@
         fine1[pl.ds(288 * tile + 1, 144, 2), :] = widened
 
     for e in range(3):
-        get = fine_coef(stat, zlow0, zhigh0, e)
+        get = fine_coef(stat, sides0, e)
         value = {}
         for x in range(-2, 10):
             start = ((x // 2 + 1) * 3 + e) * 16
             value[x] = [
                 field2[pl.ds(((x + 2) * 3 + e) * 16, 16), :] + fine1[pl.ds(start, 16), :],
-                side_tile(zlow2, zhigh2, (x + 2) * 16, 2 * e, 2) + fine1[pl.ds(288 + start, 16), :],
+                side_tile(sides2, (x + 2) * 16, 2 * e, 2) + fine1[pl.ds(288 + start, 16), :],
             ]
         value = {x: swept(x, value, get, 2) for x in range(-1, 9)}
         for x in range(8):
@@ -567,29 +650,30 @@
     return lax.ppermute(up, axis, pairs), lax.ppermute(down, axis, [(b, a) for a, b in pairs])
 
 
+def to_all(value, devices):
+    blocks = value.reshape(devices, value.shape[0] // devices, LANES)
+    return lax.all_to_all(blocks, ("gx", "gy"), 0, 0).reshape(value.shape)
+
+
 def per_device(couplings, diagonal, right_side, guess):
     gx, gy = lax.axis_size("gx"), lax.axis_size("gy")
-    place = jnp.stack([lax.axis_index("gx"), lax.axis_index("gy")]).astype(jnp.int32)
+    inputs = (couplings, diagonal, right_side, guess)
 
     stat, field, total, zup, zdown, coef1, scale1, total1 = call(
-        prepare_whole, "prepare", [1344, 192, 192, Z_ROWS, Z_ROWS, 288, 48, 48],
-        [couplings, diagonal, right_side, guess], scratch=[672, 336, 168, 88, 48],
+        prepare_whole, "prepare", [1344, 192, 192, Z_ROWS, Z_ROWS, 288, 48, 48], [], far_args=inputs,
+        scratch=[value.shape for value in inputs] + [672, 336, 168, 88, 48], copies=4,
     )
     zlow, zhigh = both_ways("gz", zup, zdown)
-    xup, xdown, shared = call(
-        fine_x, "fine_x", [x_rows(FINE), x_rows(FINE), 88], [stat, field, zlow, zhigh, zup]
-    )
-    means = lax.all_gather(shared, ("gx", "gy"), tiled=True)
+    xup, xdown = call(fine_x, "fine_x", [x_rows(FINE)] * 2, [stat, field, zlow, zhigh])
+    (shared,) = call(share, "share", [SHARED], [zlow, zhigh, zup], scratch=[96])
+    shared = to_all(jnp.broadcast_to(shared[None], (gx * gy, SHARED, LANES)).reshape(-1, LANES), gx * gy)
     xlow, xhigh = both_ways("gx", xup, xdown)
-    yup, ydown = call(
-        fine_y, "fine_y", [y_rows(FINE)] * 2, [stat, field, zlow, zhigh, xlow, xhigh]
-    )
+    yup, ydown = call(fine_y, "fine_y", [y_rows(FINE)] * 2, [stat, field, zlow, zhigh, xlow, xhigh])
     ylow, yhigh = both_ways("gy", yup, ydown)
-    stat_grown, zlow_grown, zhigh_grown, field2, middle, zup, zdown = call(
-        fine_sweeps, "fine_sweeps",
-        [FINE[0].grown_rows(), FINE[2].grown_rows(), FINE[3].grown_rows(), 192, 336, 112, 112],
+    sides0, field2, middle, zup, zdown, stat = call(
+        fine_sweeps, "fine_sweeps", [FINE[2].grown_rows(), 192, 336, 112, 112],
         [stat, field, zlow, zhigh, xlow, xhigh, ylow, yhigh, total, coef1, scale1],
-        scratch=[FINE[1].grown_rows(), 96],
+        far_outs=[FAR], scratch=[s.grown_rows() for s in FINE] + [96], copies=1,
     )
 
     zlow, zhigh = both_ways("gz", zup, zdown)
@@ -601,28 +685,32 @@
         middle_y, "middle_y", [y_rows(MIDDLE)] * 2, [coef1, right1, field2, zlow, zhigh, xlow, xhigh]
     )
     ylow, yhigh = both_ways("gy", yup, ydown)
-    coef1, right1, field2, zlow2, zhigh2, error1, coarse = call(
-        middle_sweeps, "middle_sweeps", [s.grown_rows() for s in MIDDLE] + [480, 16],
-        [coef1, right1, field2, zlow, zhigh, xlow, xhigh, ylow, yhigh, total1], scratch=[32],
+    right1, field2, sides2, error1, coarse, coef1 = call(
+        middle_sweeps, "middle_sweeps", [s.grown_rows() for s in MIDDLE[1:4]] + [480, 16],
+        [coef1, right1, field2, zlow, zhigh, xlow, xhigh, ylow, yhigh, total1],
+        far_outs=[FAR], scratch=[MIDDLE[i].grown_rows() for i in (0, 3, 4)] + [32], copies=1,
     )
 
     zlow, zhigh = both_ways("gz", coarse, coarse)
     (packed,) = call(spread, "spread", [gx * gy * 8], [coarse, zlow, zhigh], scratch=[16])
-    packed = lax.all_to_all(packed.reshape(gx * gy, 8, LANES), ("gx", "gy"), 0, 0).reshape(gx * gy * 8, LANES)
-
+    packed, shared = lax.optimization_barrier((packed, shared))
+    packed = to_all(packed, gx * gy)
+
+    tiles = 12 * gx * gy
     vmem = pl.BlockSpec(memory_space=pltpu.VMEM)
-    args = [packed, means, error1, coef1, right1, stat_grown, zlow_grown, zhigh_grown, field2, zlow2, zhigh2]
-    tiles = 12 * gx * gy
-    scratch = [tiles * 7, tiles, gx * 21 * gy, (2 * gx + 4) * 6 * (gy + 16), 144, 288, 144, 576]
+    far = pl.BlockSpec(memory_space=pltpu.HBM)
+    near = [packed, error1, right1, sides0, field2, sides2]
+    scratch = [gx * gy * SHARED, MIDDLE[0].grown_rows(), FINE[0].grown_rows(), tiles * 6, tiles, tiles, gx * 21 * gy]
+    scratch += [tiles, (2 * gx + 4) * 6 * (gy + 16), 144, 288, 144, 576]
     return pl.pallas_call(
         lambda *refs: finish(gx, gy, *refs),
         name="finish",
         out_shape=jax.ShapeDtypeStruct(guess.shape, F32),
-        in_specs=[pl.BlockSpec(memory_space=pltpu.SMEM)] + [vmem] * len(args),
+        in_specs=[far] * 3 + [vmem] * len(near),
         out_specs=vmem,
-        scratch_shapes=[pltpu.VMEM((rows, LANES), F32) for rows in scratch],
-        compiler_params=pltpu.CompilerParams(vmem_limit_bytes=40 * 1024 * 1024),
-    )(place, *args)
+        scratch_shapes=[pltpu.VMEM((rows, LANES), F32) for rows in scratch] + [pltpu.SemaphoreType.DMA((gx + 2,))],
+        compiler_params=pltpu.CompilerParams(vmem_limit_bytes=GRANT),
+    )(shared, coef1, stat, *near)
 
 
 def solution(mesh):

time: 151 us -> 178 us (1.18)
  blocking collectives: 0 us -> 19.7 us
  waiting for transfers between devices: 60.2 us -> 79.8 us
  between operations: 13.6 us -> 0.38 us
  local copies, waits for them, and re-layouts: 9.58 us -> 5.3 us
  starting transfers between devices: 54.9 us -> 58 us
  Pallas kernels: 12.5 us -> 14.3 us
    ppermute x7, waiting for transfers between devices: 15.6 us -> 60.3 us  [both_ways(): lax.ppermute(up, axis, pairs)]
    all_to_all x0 -> x1, blocking collectives: none -> 19.7 us  [to_all(): return lax.all_to_all(blocks, ('gx', 'gy'), 0, 0).reshape(value.shape)]
    all_to_all x1, waiting for transfers between devices: 13.7 us -> 0.01 us  [to_all(): return lax.all_to_all(blocks, ('gx', 'gy'), 0, 0).reshape(value.shape)]
    ppermute x7, waiting for transfers between devices: 30.9 us -> 19.6 us  [both_ways(): lax.ppermute(down, axis, [(b, a) for a, b in pairs])]
    unnamed x18 -> x8, local copies, waits for them, and re-layouts: 9.58 us -> 3.74 us
    ppermute x7, starting transfers between devices: 14.6 us -> 18.8 us  [both_ways(): lax.ppermute(down, axis, [(b, a) for a, b in pairs])]
    pallas_call x8 -> x9, Pallas kernels: 5.83 us -> 7.42 us  [call(): pl.pallas_call(body, name=name, out_shape=[jax.ShapeDtypeStruct((rows, LA...]
  transfers between devices with their start and end apart: 16 -> 15, of which waited for: 12 -> 11; matrix products, arithmetic and copies ran while one was open for 0% -> 0% of each run, Pallas kernels for 3% -> 3%
where the time goes in v2:
time: 178 us
  waiting for transfers between devices  79.8 us (45%)
  starting transfers between devices  58 us (33%)
  blocking collectives  19.7 us (11%)
  Pallas kernels  14.3 us (8%)
  local copies, waits for them, and re-layouts  5.3 us (3%)
    ppermute x7, waiting for transfers between devices, both_ways(): lax.ppermute(up, axis, pairs)  60.3 us
    ppermute x7, starting transfers between devices, both_ways(): lax.ppermute(up, axis, pairs)  27.2 us
    all_to_all x1, blocking collectives, to_all(): return lax.all_to_all(blocks, ('gx', 'gy'), 0, 0).reshape(value.shape)  19.7 us
    ppermute x7, waiting for transfers between devices, both_ways(): lax.ppermute(down, axis, [(b, a) for a, b in pairs])  19.6 us
    ppermute x7, starting transfers between devices, both_ways(): lax.ppermute(down, axis, [(b, a) for a, b in pairs])  18.8 us
    all_to_all x1, starting transfers between devices, to_all(): return lax.all_to_all(blocks, ('gx', 'gy'), 0, 0).reshape(value.shape)  12 us
    pallas_call x9, Pallas kernels, call(): pl.pallas_call(body, name=name, out_shape=[jax.ShapeDtypeStruct((rows, LA...  7.42 us
    pallas_call x1, Pallas kernels, per_device(): pl.pallas_call(lambda *refs: finish(gx, gy, *refs), name='finish', out_sh...  6.93 us
  transfers between devices with their start and end apart: 15, of which 11 were waited for; matrix products, arithmetic and copies ran while one was open for 0% of the time, Pallas kernels for 3%

profile of v2, /device:TPU:1, one launch (start us, length us, event | category | flops | bytes accessed | tf_op | source)
XLA Modules:
  0.0 177.6 jit_solution(8786833736698132)
XLA Ops:
  5.3 8.8 %collective-permute-start.1 = (f32[152,128]{1,0:T(8,128)S(1)}, f32[152,128]{1,0:T(8,128)S(1)}, u32[]{:S(2)}, u32[]{:S(2)}) collective-permute-start(f32[152,128]{1,0:T(8,128)S(1)} %get-tuple-element.40), channel_id=1, source_target_pairs={{1,0},{2,1},{3,2},{4,3},{5,4},{6,5},{7,6},{9,8},{10,9},{11,10},{12... | collective-permute-start | bytes 233480 | tf_op jit(solution)/shard_map/ppermute | solution.py:650
  14.1 1.9 %collective-permute-start = (f32[152,128]{1,0:T(8,128)S(1)}, f32[152,128]{1,0:T(8,128)S(1)}, u32[]{:S(2)}, u32[]{:S(2)}) collective-permute-start(f32[152,128]{1,0:T(8,128)S(1)} %get-tuple-element.39.zown), channel_id=1, source_target_pairs={{0,1},{1,2},{2,3},{3,4},{4,5},{5,6},{6,7},{8,9},{9,10},{10,11},{11... | collective-permute-start | bytes 233480 | tf_op jit(solution)/shard_map/ppermute | solution.py:650
  17.7 1.6 broadcast_in_dim.2
  19.2 12.0 %all-to-all-start = ((f32[64,64,128]{2,1,0:T(8,128)}), f32[64,64,128]{2,1,0:T(8,128)S(1)}, u32[]{:S(2)}, u32[]{:S(2)}) async-start(f32[64,64,128]{2,1,0:T(8,128)} %broadcast_in_dim.2), calls=%async_computation | async-start | bytes 4194304 | tf_op jit(solution)/shard_map/all_to_all | solution.py:655
  31.3 2.9 %collective-permute-start.2 = (f32[456,128]{1,0:T(8,128)S(1)}, f32[456,128]{1,0:T(8,128)S(1)}, u32[]{:S(2)}, u32[]{:S(2)}) collective-permute-start(f32[456,128]{1,0:T(8,128)S(1)} %get-tuple-element.41), channel_id=1, source_target_pairs={{0,64},{64,128},{128,192},{192,256},{256,320},{320,384},{384,448},... | collective-permute-start | bytes 700424 | tf_op jit(solution)/shard_map/ppermute | solution.py:650
  35.5 45.7 %collective-permute-done.2.low = f32[456,128]{1,0:T(8,128)S(1)} collective-permute-done((f32[456,128]{1,0:T(8,128)S(1)}, f32[456,128]{1,0:T(8,128)S(1)}, u32[]{:S(2)}, u32[]{:S(2)}) %collective-permute-start.2) | collective-permute-done | bytes 233504 | tf_op jit(solution)/shard_map/ppermute | solution.py:650
  82.7 3.1 %collective-permute-start.4 = (f32[528,128]{1,0:T(8,128)S(1)}, f32[528,128]{1,0:T(8,128)S(1)}, u32[]{:S(2)}, u32[]{:S(2)}) collective-permute-start(f32[528,128]{1,0:T(8,128)S(1)} %get-tuple-element.43), channel_id=1, source_target_pairs={{0,8},{8,16},{16,24},{24,32},{32,40},{40,48},{48,56},{1,9},{9,17},... | collective-permute-start | bytes 811016 | tf_op jit(solution)/shard_map/ppermute | solution.py:650
  87.1 4.5 %collective-permute-done.4.below = f32[528,128]{1,0:T(8,128)S(1)} collective-permute-done((f32[528,128]{1,0:T(8,128)S(1)}, f32[528,128]{1,0:T(8,128)S(1)}, u32[]{:S(2)}, u32[]{:S(2)}) %collective-permute-start.4) | collective-permute-done | bytes 270368 | tf_op jit(solution)/shard_map/ppermute | solution.py:650
  91.6 5.1 %collective-permute-done.5.above = f32[528,128]{1,0:T(8,128)S(1)} collective-permute-done((f32[528,128]{1,0:T(8,128)S(1)}, f32[528,128]{1,0:T(8,128)S(1)}, u32[]{:S(2)}, u32[]{:S(2)}) %collective-permute-start.5) | collective-permute-done | bytes 270368 | tf_op jit(solution)/shard_map/ppermute | solution.py:650
  96.7 3.3 %fine_sweeps.1 = (f32[224,128]{1,0:T(8,128)S(1)}, f32[192,128]{1,0:T(8,128)S(1)}, f32[336,128]{1,0:T(8,128)S(1)}, f32[112,128]{1,0:T(8,128)S(1)}, f32[112,128]{1,0:T(8,128)S(1)}, /*index=5*/f32[49152,128]{1,0:T(8,128)}) custom-call(f32[1344,128]{1,0:T(8,128)S(1)} %get-tuple-element.37.stat.stat0, f32[192,128]{1,0:T(8,128)S(1)} %get-tuple-element.38.field.field0, ...), custom_call_target="tpu_custom_call" | custom-call | tf_op jit(solution)/shard_map/fine_sweeps/pallas_call | solution.py:42
  100.0 2.3 %collective-permute-start.6 = (f32[112,128]{1,0:T(8,128)S(1)}, f32[112,128]{1,0:T(8,128)S(1)}, u32[]{:S(2)}, u32[]{:S(2)}) collective-permute-start(f32[112,128]{1,0:T(8,128)S(1)} %get-tuple-element.50), channel_id=1, source_target_pairs={{0,1},{1,2},{2,3},{3,4},{4,5},{5,6},{6,7},{8,9},{9,10},{10,11},{11... | collective-permute-start | bytes 172040 | tf_op jit(solution)/shard_map/ppermute | solution.py:650
  102.3 2.1 %collective-permute-start.7 = (f32[112,128]{1,0:T(8,128)S(1)}, f32[112,128]{1,0:T(8,128)S(1)}, u32[]{:S(2)}, u32[]{:S(2)}) collective-permute-start(f32[112,128]{1,0:T(8,128)S(1)} %get-tuple-element.51), channel_id=1, source_target_pairs={{1,0},{2,1},{3,2},{4,3},{5,4},{6,5},{7,6},{9,8},{10,9},{11,10},{12... | collective-permute-start | bytes 172040 | tf_op jit(solution)/shard_map/ppermute | solution.py:650
  104.4 3.4 %collective-permute-done.7.zhigh.zhigh0 = f32[112,128]{1,0:T(8,128)S(1)} collective-permute-done((f32[112,128]{1,0:T(8,128)S(1)}, f32[112,128]{1,0:T(8,128)S(1)}, u32[]{:S(2)}, u32[]{:S(2)}) %collective-permute-start.7) | collective-permute-done | bytes 57376 | tf_op jit(solution)/shard_map/ppermute | solution.py:650
  108.0 8.9 %collective-permute-start.8 = (f32[344,128]{1,0:T(8,128)S(1)}, f32[344,128]{1,0:T(8,128)S(1)}, u32[]{:S(2)}, u32[]{:S(2)}) collective-permute-start(f32[344,128]{1,0:T(8,128)S(1)} %get-tuple-element.54), channel_id=1, source_target_pairs={{0,64},{64,128},{128,192},{192,256},{256,320},{320,384},{384,448},... | collective-permute-start | bytes 528392 | tf_op jit(solution)/shard_map/ppermute | solution.py:650
  118.2 2.0 %collective-permute-done.8.low = f32[344,128]{1,0:T(8,128)S(1)} collective-permute-done((f32[344,128]{1,0:T(8,128)S(1)}, f32[344,128]{1,0:T(8,128)S(1)}, u32[]{:S(2)}, u32[]{:S(2)}) %collective-permute-start.8) | collective-permute-done | bytes 176160 | tf_op jit(solution)/shard_map/ppermute | solution.py:650
  120.2 5.8 %collective-permute-done.9.high = f32[344,128]{1,0:T(8,128)S(1)} collective-permute-done((f32[344,128]{1,0:T(8,128)S(1)}, f32[344,128]{1,0:T(8,128)S(1)}, u32[]{:S(2)}, u32[]{:S(2)}) %collective-permute-start.9) | collective-permute-done | bytes 176160 | tf_op jit(solution)/shard_map/ppermute | solution.py:650
  126.1 5.2 %collective-permute-start.10 = (f32[632,128]{1,0:T(8,128)S(1)}, f32[632,128]{1,0:T(8,128)S(1)}, u32[]{:S(2)}, u32[]{:S(2)}) collective-permute-start(f32[632,128]{1,0:T(8,128)S(1)} %get-tuple-element.56), channel_id=1, source_target_pairs={{0,8},{8,16},{16,24},{24,32},{32,40},{40,48},{48,56},{1,9},{9,17},... | collective-permute-start | bytes 970760 | tf_op jit(solution)/shard_map/ppermute | solution.py:650
  132.5 6.0 %collective-permute-done.10.below = f32[632,128]{1,0:T(8,128)S(1)} collective-permute-done((f32[632,128]{1,0:T(8,128)S(1)}, f32[632,128]{1,0:T(8,128)S(1)}, u32[]{:S(2)}, u32[]{:S(2)}) %collective-permute-start.10) | collective-permute-done | bytes 323616 | tf_op jit(solution)/shard_map/ppermute | solution.py:650
  138.5 3.9 %collective-permute-done.11.above = f32[632,128]{1,0:T(8,128)S(1)} collective-permute-done((f32[632,128]{1,0:T(8,128)S(1)}, f32[632,128]{1,0:T(8,128)S(1)}, u32[]{:S(2)}, u32[]{:S(2)}) %collective-permute-start.11) | collective-permute-done | bytes 323616 | tf_op jit(solution)/shard_map/ppermute | solution.py:650
  142.4 1.8 %middle_sweeps.1 = (f32[576,128]{1,0:T(8,128)S(1)}, f32[576,128]{1,0:T(8,128)S(1)}, f32[192,128]{1,0:T(8,128)S(1)}, f32[480,128]{1,0:T(8,128)S(1)}, f32[16,128]{1,0:T(8,128)S(1)}, /*index=5*/f32[49152,128]{1,0:T(8,128)}) custom-call(f32[288,128]{1,0:T(8,128)S(1)} %get-tuple-element.52.coef.coef0, f32[48,128]{1,0:T(8,128)S(1)} %get-tuple-element.53.right.right0, ...), custom_call_target="tpu_custom_call" | custom-call | tf_op jit(solution)/shard_map/middle_sweeps/pallas_call | solution.py:42
  144.2 2.7 %collective-permute-start.13 = (f32[16,128]{1,0:T(8,128)S(1)}, f32[16,128]{1,0:T(8,128)S(1)}, u32[]{:S(2)}, u32[]{:S(2)}) collective-permute-start(f32[16,128]{1,0:T(8,128)S(1)} %get-tuple-element.59.coarse), channel_id=1, source_target_pairs={{1,0},{2,1},{3,2},{4,3},{5,4},{6,5},{7,6},{9,8},{10,9},{11,10},{12... | collective-permute-start | bytes 24584 | tf_op jit(solution)/shard_map/ppermute | solution.py:650
  146.9 2.9 %collective-permute-start.12 = (f32[16,128]{1,0:T(8,128)S(1)}, f32[16,128]{1,0:T(8,128)S(1)}, u32[]{:S(2)}, u32[]{:S(2)}) collective-permute-start(f32[16,128]{1,0:T(8,128)S(1)} %get-tuple-element.59.coarse), channel_id=1, source_target_pairs={{0,1},{1,2},{2,3},{3,4},{4,5},{5,6},{6,7},{8,9},{9,10},{10,11},{11... | collective-permute-start | bytes 24584 | tf_op jit(solution)/shard_map/ppermute | solution.py:650
  150.8 19.7 %all_to_all.10 = f32[64,8,128]{2,1,0:T(8,128)S(1)} all-to-all(f32[64,8,128]{2,1,0:T(8,128)S(1)} %bitcast.5), channel_id=1, replica_groups=mesh['gx'=8,'gy'=8,'gz'=8] {'gx','gy'}, dimensions={0} | all-to-all | bytes 524288 | tf_op jit(solution)/shard_map/all_to_all | solution.py:655
  170.5 6.9 %finish.1 = f32[3,8,8,128]{3,2,1,0:T(8,128)} custom-call(f32[4096,128]{1,0:T(8,128)S(1)} %bitcast.3, f32[49152,128]{1,0:T(8,128)} %get-tuple-element.61.refs_1_, f32[49152,128]{1,0:T(8,128)} %get-tuple-element.62.refs_2_, f32[512,128]{1,0:T(8,128)S(1)} %bitcast.4, f32[480,128]{1,0:T(8,128)S(1)} %get-tuple-element.64.refs_4_, ...), custom_call_target="tpu_custom_call" | custom-call | tf_op jit(solution)/shard_map/finish/pallas_call | solution.py:705
  (26 shorter events, 14.8 us)
Async XLA Ops:
  0.0 1.1 copy-start
  1.1 0.9 copy-start.1
  2.0 0.9 copy-start.2
  2.9 0.9 copy-start.3
  5.3 10.7 %collective-permute-start.1 = (f32[152,128]{1,0:T(8,128)S(1)}, f32[152,128]{1,0:T(8,128)S(1)}, u32[]{:S(2)}, u32[]{:S(2)}) collective-permute-start(f32[152,128]{1,0:T(8,128)S(1)} %get-tuple-element.40), channel_id=1, source_target_pairs={{1,0},{2,1},{3,2},{4,3},{5,4},{6,5},{7,6},{9,8},{10,9},{11,10},{12... | collective-permute-start | bytes 233480 | tf_op jit(solution)/shard_map/ppermute | solution.py:650
  14.1 3.4 %collective-permute-start = (f32[152,128]{1,0:T(8,128)S(1)}, f32[152,128]{1,0:T(8,128)S(1)}, u32[]{:S(2)}, u32[]{:S(2)}) collective-permute-start(f32[152,128]{1,0:T(8,128)S(1)} %get-tuple-element.39.zown), channel_id=1, source_target_pairs={{0,1},{1,2},{2,3},{3,4},{4,5},{5,6},{6,7},{8,9},{9,10},{10,11},{11... | collective-permute-start | bytes 233480 | tf_op jit(solution)/shard_map/ppermute | solution.py:650
  19.2 131.5 %all-to-all-start = ((f32[64,64,128]{2,1,0:T(8,128)}), f32[64,64,128]{2,1,0:T(8,128)S(1)}, u32[]{:S(2)}, u32[]{:S(2)}) async-start(f32[64,64,128]{2,1,0:T(8,128)} %broadcast_in_dim.2), calls=%async_computation | async-start | bytes 4194304 | tf_op jit(solution)/shard_map/all_to_all | solution.py:655
  31.3 49.9 %collective-permute-start.2 = (f32[456,128]{1,0:T(8,128)S(1)}, f32[456,128]{1,0:T(8,128)S(1)}, u32[]{:S(2)}, u32[]{:S(2)}) collective-permute-start(f32[456,128]{1,0:T(8,128)S(1)} %get-tuple-element.41), channel_id=1, source_target_pairs={{0,64},{64,128},{128,192},{192,256},{256,320},{320,384},{384,448},... | collective-permute-start | bytes 700424 | tf_op jit(solution)/shard_map/ppermute | solution.py:650
  34.2 48.4 %collective-permute-start.3 = (f32[456,128]{1,0:T(8,128)S(1)}, f32[456,128]{1,0:T(8,128)S(1)}, u32[]{:S(2)}, u32[]{:S(2)}) collective-permute-start(f32[456,128]{1,0:T(8,128)S(1)} %get-tuple-element.42), channel_id=1, source_target_pairs={{64,0},{128,64},{192,128},{256,192},{320,256},{384,320},{448,384},... | collective-permute-start | bytes 700424 | tf_op jit(solution)/shard_map/ppermute | solution.py:650
  82.7 8.9 %collective-permute-start.4 = (f32[528,128]{1,0:T(8,128)S(1)}, f32[528,128]{1,0:T(8,128)S(1)}, u32[]{:S(2)}, u32[]{:S(2)}) collective-permute-start(f32[528,128]{1,0:T(8,128)S(1)} %get-tuple-element.43), channel_id=1, source_target_pairs={{0,8},{8,16},{16,24},{24,32},{32,40},{40,48},{48,56},{1,9},{9,17},... | collective-permute-start | bytes 811016 | tf_op jit(solution)/shard_map/ppermute | solution.py:650
  85.8 10.8 %collective-permute-start.5 = (f32[528,128]{1,0:T(8,128)S(1)}, f32[528,128]{1,0:T(8,128)S(1)}, u32[]{:S(2)}, u32[]{:S(2)}) collective-permute-start(f32[528,128]{1,0:T(8,128)S(1)} %get-tuple-element.44), channel_id=1, source_target_pairs={{8,0},{16,8},{24,16},{32,24},{40,32},{48,40},{56,48},{9,1},{17,9},... | collective-permute-start | bytes 811016 | tf_op jit(solution)/shard_map/ppermute | solution.py:650
  100.0 4.4 %collective-permute-start.6 = (f32[112,128]{1,0:T(8,128)S(1)}, f32[112,128]{1,0:T(8,128)S(1)}, u32[]{:S(2)}, u32[]{:S(2)}) collective-permute-start(f32[112,128]{1,0:T(8,128)S(1)} %get-tuple-element.50), channel_id=1, source_target_pairs={{0,1},{1,2},{2,3},{3,4},{4,5},{5,6},{6,7},{8,9},{9,10},{10,11},{11... | collective-permute-start | bytes 172040 | tf_op jit(solution)/shard_map/ppermute | solution.py:650
  102.3 5.5 %collective-permute-start.7 = (f32[112,128]{1,0:T(8,128)S(1)}, f32[112,128]{1,0:T(8,128)S(1)}, u32[]{:S(2)}, u32[]{:S(2)}) collective-permute-start(f32[112,128]{1,0:T(8,128)S(1)} %get-tuple-element.51), channel_id=1, source_target_pairs={{1,0},{2,1},{3,2},{4,3},{5,4},{6,5},{7,6},{9,8},{10,9},{11,10},{12... | collective-permute-start | bytes 172040 | tf_op jit(solution)/shard_map/ppermute | solution.py:650
  108.0 12.2 %collective-permute-start.8 = (f32[344,128]{1,0:T(8,128)S(1)}, f32[344,128]{1,0:T(8,128)S(1)}, u32[]{:S(2)}, u32[]{:S(2)}) collective-permute-start(f32[344,128]{1,0:T(8,128)S(1)} %get-tuple-element.54), channel_id=1, source_target_pairs={{0,64},{64,128},{128,192},{192,256},{256,320},{320,384},{384,448},... | collective-permute-start | bytes 528392 | tf_op jit(solution)/shard_map/ppermute | solution.py:650
  116.9 9.1 %collective-permute-start.9 = (f32[344,128]{1,0:T(8,128)S(1)}, f32[344,128]{1,0:T(8,128)S(1)}, u32[]{:S(2)}, u32[]{:S(2)}) collective-permute-start(f32[344,128]{1,0:T(8,128)S(1)} %get-tuple-element.55), channel_id=1, source_target_pairs={{64,0},{128,64},{192,128},{256,192},{320,256},{384,320},{448,384},... | collective-permute-start | bytes 528392 | tf_op jit(solution)/shard_map/ppermute | solution.py:650
  126.1 12.4 %collective-permute-start.10 = (f32[632,128]{1,0:T(8,128)S(1)}, f32[632,128]{1,0:T(8,128)S(1)}, u32[]{:S(2)}, u32[]{:S(2)}) collective-permute-start(f32[632,128]{1,0:T(8,128)S(1)} %get-tuple-element.56), channel_id=1, source_target_pairs={{0,8},{8,16},{16,24},{24,32},{32,40},{40,48},{48,56},{1,9},{9,17},... | collective-permute-start | bytes 970760 | tf_op jit(solution)/shard_map/ppermute | solution.py:650
  131.2 11.1 %collective-permute-start.11 = (f32[632,128]{1,0:T(8,128)S(1)}, f32[632,128]{1,0:T(8,128)S(1)}, u32[]{:S(2)}, u32[]{:S(2)}) collective-permute-start(f32[632,128]{1,0:T(8,128)S(1)} %get-tuple-element.57), channel_id=1, source_target_pairs={{8,0},{16,8},{24,16},{32,24},{40,32},{48,40},{56,48},{9,1},{17,9},... | collective-permute-start | bytes 970760 | tf_op jit(solution)/shard_map/ppermute | solution.py:650
  144.2 5.6 %collective-permute-start.13 = (f32[16,128]{1,0:T(8,128)S(1)}, f32[16,128]{1,0:T(8,128)S(1)}, u32[]{:S(2)}, u32[]{:S(2)}) collective-permute-start(f32[16,128]{1,0:T(8,128)S(1)} %get-tuple-element.59.coarse), channel_id=1, source_target_pairs={{1,0},{2,1},{3,2},{4,3},{5,4},{6,5},{7,6},{9,8},{10,9},{11,10},{12... | collective-permute-start | bytes 24584 | tf_op jit(solution)/shard_map/ppermute | solution.py:650
  146.9 3.6 %collective-permute-start.12 = (f32[16,128]{1,0:T(8,128)S(1)}, f32[16,128]{1,0:T(8,128)S(1)}, u32[]{:S(2)}, u32[]{:S(2)}) collective-permute-start(f32[16,128]{1,0:T(8,128)S(1)} %get-tuple-element.59.coarse), channel_id=1, source_target_pairs={{0,1},{1,2},{2,3},{3,4},{4,5},{5,6},{6,7},{8,9},{9,10},{10,11},{11... | collective-permute-start | bytes 24584 | tf_op jit(solution)/shard_map/ppermute | solution.py:650

commit v3 on v2

--- a/solution.py
+++ b/solution.py
@@ -11,6 +11,7 @@
 GRANT = 40 * 1024 * 1024
 FAR = 49152
 STATIC = 21
+WIDE = 42
 HALO2 = 20
 SHARED = 64
 MEANS = 84
@@ -66,6 +67,7 @@
 
 FINE = [Stream(STATIC, 8, 8, 2, 2), Stream(3, 8, 8, 3, 3), Stream(1, 8, 8, 3, 3), Stream(1, 8, 8, 3, 3)]
 MIDDLE = [Stream(18, 4, 4, 3, 4), Stream(3, 4, 4, 4, 5), Stream(3, 8, 8, 2, 2), Stream(1, 8, 8, 2, 2), Stream(1, 8, 8, 2, 2)]
+MIDDLE += [Stream(18, 4, 4, 1, 1), Stream(3, 4, 4, 2, 2)]
 
 
 def x_rows(streams):
@@ -313,11 +315,9 @@
     return coef
 
 
-def fine_sweeps(stat0, field0, zlow0, zhigh0, low, high, below, above, total, coef1, scale1,
-                sides, field2, middle, zup, zdown, stat_far, stat, field, zlow, zhigh, sums, left):
+def fine_sweeps(stat0, field0, zlow0, zhigh0, low, high, below, above, total, coef1, scale1, total1,
+                stat, sides, field2, middle, zup, zdown, field, zlow, zhigh, sums):
     grow(FINE, [stat0, field0, zlow0, zhigh0], low, high, below, above, [stat, field, zlow, zhigh])
-    keep = pltpu.make_async_copy(stat, stat_far.at[pl.ds(0, stat.shape[0]), :], left.at[0])
-    keep.start()
     both_sides(zlow, zhigh, sides)
     for e in range(3):
         coef = fine_coef(stat, sides, e)
@@ -340,16 +340,17 @@
     right = exact_dot(sums[pl.ds(0, 48, 2), :] + sums[pl.ds(1, 48, 2), :], pair_matrix(0.125))
     middle[pl.ds(0, 288), :] = coef1[...]
     middle[pl.ds(288, 48), :] = right * scale1[...]
-    lane = lanes_of(48)
-    up = jnp.zeros((48, LANES), F32)
-    down = jnp.zeros((48, LANES), F32)
-    for group in range(7):
-        value = middle[pl.ds(48 * group, 48), :]
-        inside = (lane >= 4 * group) & (lane < 4 * group + 4)
-        up = jnp.where(inside, rolled(value, 4 * group - 60, 1), up)
-        down = jnp.where(inside, rolled(value, 4 * group, 1), down)
-    zup[pl.ds(64, 48), :] = up
-    zdown[pl.ds(64, 48), :] = down
+    middle[pl.ds(336, 48), :] = total1[...]
+    lane = lanes_of(128)
+    up = jnp.zeros((128, LANES), F32)
+    down = jnp.zeros((128, LANES), F32)
+    for group in range(3):
+        value = middle[pl.ds(128 * group, 128), :]
+        inside = (lane >= WIDE * group) & (lane < WIDE * group + WIDE)
+        up = jnp.where(inside, rolled(value, WIDE * group + WIDE - 64, 1), up)
+        down = jnp.where(inside, rolled(value, WIDE * group, 1), down)
+    zup[pl.ds(64, 128), :] = up
+    zdown[pl.ds(64, 128), :] = down
     lane = lanes_of(8)
     for x in range(8):
         up = jnp.zeros((8, LANES), F32)
@@ -361,25 +362,33 @@
             down = jnp.where(inside, rolled(value, 2 * e, 1), down)
         zup[pl.ds(x * 8, 8), :] = up
         zdown[pl.ds(x * 8, 8), :] = down
-    keep.wait()
-
-
-def middle_x(middle, field, zlow, zhigh, coef, right, up, down):
-    lane = lanes_of(48)
-    low, high = zlow[pl.ds(64, 48), :], zhigh[pl.ds(64, 48), :]
-    for group in range(7):
-        value = middle[pl.ds(48 * group, 48), :]
-        value = jnp.where((lane >= 64) & (lane < 68), rolled(high, 64 - 4 * group, 1), value)
-        value = jnp.where(lane >= 124, rolled(low, 124 - 4 * group, 1), value)
-        if group < 6:
-            coef[pl.ds(48 * group, 48), :] = value
+
+
+def middle_x(middle, field, zlow, zhigh, coef, right, side_coef, side_right, side_total, up, down):
+    lane = lanes_of(128)
+    low, high = zlow[pl.ds(64, 128), :], zhigh[pl.ds(64, 128), :]
+    for group in range(3):
+        own = middle[pl.ds(128 * group, 128), :]
+        main = jnp.where((lane >= 64) & (lane < 68), rolled(high, 64 - WIDE * group, 1), own)
+        main = jnp.where(lane >= 124, rolled(low, 128 - WIDE - WIDE * group, 1), main)
+        side = jnp.where(lane < 2, rolled(own, -62, 1), F32(0))
+        side = jnp.where((lane >= 2) & (lane < 2 + WIDE), rolled(high, 2 - WIDE * group, 1), side)
+        side = jnp.where((lane >= 64) & (lane < 64 + WIDE), rolled(low, 64 - WIDE * group, 1), side)
+        side = jnp.where((lane >= 106) & (lane < 108), rolled(own, 106, 1), side)
+        if group < 2:
+            coef[pl.ds(128 * group, 128), :] = main
+            side_coef[pl.ds(128 * group, 128), :] = side
         else:
-            right[...] = value
-    pack_x(MIDDLE, [coef, right, field, zlow, zhigh], up, down)
-
-
-def middle_y(coef, right, field, zlow, zhigh, low, high, up, down):
-    pack_y(MIDDLE, [coef, right, field, zlow, zhigh], low, high, up, down)
+            coef[pl.ds(256, 32), :] = main[:32]
+            side_coef[pl.ds(256, 32), :] = side[:32]
+            right[...] = main[32:80]
+            side_right[...] = side[32:80]
+            side_total[...] = side[80:]
+    pack_x(MIDDLE, [coef, right, field, zlow, zhigh, side_coef, side_right], up, down)
+
+
+def middle_y(coef, right, field, zlow, zhigh, side_coef, side_right, low, high, up, down):
+    pack_y(MIDDLE, [coef, right, field, zlow, zhigh, side_coef, side_right], low, high, up, down)
 
 
 def middle_coef(coef, right, e):
@@ -391,35 +400,52 @@
     return get
 
 
-def middle_sweeps(coef0, right0, field0, zlow0, zhigh0, low, high, below, above, total1,
-                  right, field, sides, error, coarse, coef_far, coef, zlow, zhigh, sums, left):
-    grow(MIDDLE, [coef0, right0, field0, zlow0, zhigh0], low, high, below, above, [coef, right, field, zlow, zhigh])
-    keep = pltpu.make_async_copy(coef, coef_far.at[pl.ds(0, coef.shape[0]), :], left.at[0])
+def middle_sweeps(coef0, right0, field0, zlow0, zhigh0, side_coef0, side_right0, low, high, below, above, total1, side_total,
+                  right, field, sides, error, packed, coef_far, coef, zlow, zhigh, side_coef, side_right, sums, side_sums,
+                  wide, left):
+    grow(MIDDLE, [coef0, right0, field0, zlow0, zhigh0, side_coef0, side_right0], low, high, below, above,
+         [coef, right, field, zlow, zhigh, side_coef, side_right])
+    inner = pl.ds(18 * 16, 8 * 18 * 16)
+    keep = pltpu.make_async_copy(coef.at[inner, :], coef_far.at[inner, :], left.at[0])
     keep.start()
     both_sides(zlow, zhigh, sides)
     for e in range(3):
+
+        def side_get(x, k, t):
+            if k < 6:
+                return side_coef[pl.ds(((x + 1) * 18 + 6 * e + k) * 16, 16), :]
+            return side_right[pl.ds(((x + 2) * 3 + e) * 16, 16), :]
+
         get = middle_coef(coef, right, e)
-        value = {x: [get(x, 6, 0)] for x in range(-4, 8)}
-        value = {x: swept(x, value, get, 1) for x in range(-3, 7)}
+        value = {x: swept(x, {y: [get(y, 6, 0)] for y in (x - 1, x, x + 1)}, get, 1) for x in range(-3, 7)}
         for x in range(-3, 7):
             error[pl.ds(((x + 3) * 3 + e) * 16, 16), :] = value[x][0]
-        resid = []
-        for x in range(4):
-            change = swept(x, value, get, 1)[0] - value[x][0]
-            resid.append(change[:4] * total1[pl.ds((x * 3 + e) * 4, 4), :])
-        for i in range(2):
-            sums[pl.ds((i * 3 + e) * 4, 4), :] = resid[2 * i] + resid[2 * i + 1]
+        beside = {x: swept(x, {y: [side_get(y, 6, 0)] for y in (x - 1, x, x + 1)}, side_get, 1) for x in range(-1, 5)}
+        for known, coef_of, weight, out in ((value, get, total1, sums), (beside, side_get, side_total, side_sums)):
+            resid = []
+            for x in range(4):
+                change = swept(x, known, coef_of, 1)[0] - known[x][0]
+                resid.append(change[:4] * weight[pl.ds((x * 3 + e) * 4, 4), :])
+            for i in range(2):
+                out[pl.ds((i * 3 + e) * 4, 4), :] = resid[2 * i] + resid[2 * i + 1]
     sums[pl.ds(24, 8), :] = jnp.zeros((8, LANES), F32)
-    coarse[...] = exact_dot(sums[pl.ds(0, 16, 2), :] + sums[pl.ds(1, 16, 2), :], pair_matrix(0.125))
+    side_sums[pl.ds(24, 8), :] = jnp.zeros((8, LANES), F32)
+    fine = lax.broadcasted_iota(jnp.int32, (LANES, LANES), 0)
+    coarse = lax.broadcasted_iota(jnp.int32, (LANES, LANES), 1)
+    own = (fine < 64) & ((fine >> 1) + HALO2 == coarse)
+    above_own = (fine >= 2) & (fine < 42) & ((fine >> 1) + 51 == coarse)
+    below_own = (fine >= 66) & (fine < 106) & ((fine >> 1) - 33 == coarse)
+    wide[...] = exact_dot(
+        sums[pl.ds(0, 16, 2), :] + sums[pl.ds(1, 16, 2), :], jnp.where(own, F32(0.125), F32(0))
+    ) + exact_dot(
+        side_sums[pl.ds(0, 16, 2), :] + side_sums[pl.ds(1, 16, 2), :],
+        jnp.where(above_own | below_own, F32(0.125), F32(0)),
+    )
+    spread(wide, packed)
     keep.wait()
 
 
-def spread(coarse, zlow, zhigh, out, wide):
-    lane = lanes_of(16)
-    value = jnp.where(lane < HALO2, rolled(zlow[...], -12, 1), F32(0))
-    value = jnp.where((lane >= 20) & (lane < 52), rolled(coarse[...], 20, 1), value)
-    value = jnp.where((lane >= 52) & (lane < 72), rolled(zhigh[...], 52, 1), value)
-    wide[...] = value
+def spread(wide, out):
     lane = lanes_of(8)
     first, second = wide[pl.ds(0, 8), :], wide[pl.ds(6, 8), :]
     block = jnp.where(lane < 64, first, rolled(second, 64, 1))
@@ -581,16 +607,16 @@
             rows6[pl.ds((plane * 3 + e) * 8 + 4, 2), :] = jnp.zeros((2, LANES), F32)
 
 
-def finish(gx, gy, shared_far, coef1_far, stat_far, packed, error1, right1, sides0, field2, sides2, out,
-           shared, coef1, stat, coef2, scale2, total2, coef3, right2, error2, rows6, fine2, rows1, fine1, arrived):
+def finish(gx, gy, shared_far, coef1_far, packed, error1, right1, stat, sides0, field2, sides2, out,
+           shared, coef1, coef2, scale2, total2, coef3, right2, error2, rows6, fine2, rows1, fine1, arrived):
     chunk = gy * SHARED
     arrivals = [
         pltpu.make_async_copy(shared_far.at[pl.ds(g * chunk, chunk), :], shared.at[pl.ds(g * chunk, chunk), :], arrived.at[g])
         for g in range(gx)
     ]
+    inner = pl.ds(18 * 16, 8 * 18 * 16)
     later = [
-        pltpu.make_async_copy(coef1_far.at[pl.ds(0, coef1.shape[0]), :], coef1, arrived.at[gx]),
-        pltpu.make_async_copy(stat_far.at[pl.ds(0, stat.shape[0]), :], stat, arrived.at[gx + 1]),
+        pltpu.make_async_copy(coef1_far.at[inner, :], coef1.at[inner, :], arrived.at[gx]),
     ]
     for copy in arrivals + later:
         copy.start()
@@ -666,51 +692,46 @@
     zlow, zhigh = both_ways("gz", zup, zdown)
     xup, xdown = call(fine_x, "fine_x", [x_rows(FINE)] * 2, [stat, field, zlow, zhigh])
     (shared,) = call(share, "share", [SHARED], [zlow, zhigh, zup], scratch=[96])
-    shared = to_all(jnp.broadcast_to(shared[None], (gx * gy, SHARED, LANES)).reshape(-1, LANES), gx * gy)
+    shared = lax.all_gather(shared, ("gx", "gy"), tiled=True)
     xlow, xhigh = both_ways("gx", xup, xdown)
     yup, ydown = call(fine_y, "fine_y", [y_rows(FINE)] * 2, [stat, field, zlow, zhigh, xlow, xhigh])
     ylow, yhigh = both_ways("gy", yup, ydown)
-    sides0, field2, middle, zup, zdown, stat = call(
-        fine_sweeps, "fine_sweeps", [FINE[2].grown_rows(), 192, 336, 112, 112],
-        [stat, field, zlow, zhigh, xlow, xhigh, ylow, yhigh, total, coef1, scale1],
-        far_outs=[FAR], scratch=[s.grown_rows() for s in FINE] + [96], copies=1,
+    stat, sides0, field2, middle, zup, zdown = call(
+        fine_sweeps, "fine_sweeps", [FINE[0].grown_rows(), FINE[2].grown_rows(), 192, 384, 192, 192],
+        [stat, field, zlow, zhigh, xlow, xhigh, ylow, yhigh, total, coef1, scale1, total1],
+        scratch=[s.grown_rows() for s in FINE[1:]] + [96],
     )
 
     zlow, zhigh = both_ways("gz", zup, zdown)
-    coef1, right1, xup, xdown = call(
-        middle_x, "middle_x", [288, 48, x_rows(MIDDLE), x_rows(MIDDLE)], [middle, field2, zlow, zhigh]
+    coef1, right1, side_coef, side_right, side_total, xup, xdown = call(
+        middle_x, "middle_x", [288, 48, 288, 48, 48, x_rows(MIDDLE), x_rows(MIDDLE)], [middle, field2, zlow, zhigh]
     )
     xlow, xhigh = both_ways("gx", xup, xdown)
-    yup, ydown = call(
-        middle_y, "middle_y", [y_rows(MIDDLE)] * 2, [coef1, right1, field2, zlow, zhigh, xlow, xhigh]
+    level1 = [coef1, right1, field2, zlow, zhigh, side_coef, side_right]
+    yup, ydown = call(middle_y, "middle_y", [y_rows(MIDDLE)] * 2, [*level1, xlow, xhigh])
+    ylow, yhigh = both_ways("gy", yup, ydown)
+    right1, field2, sides2, error1, packed, coef1 = call(
+        middle_sweeps, "middle_sweeps", [s.grown_rows() for s in MIDDLE[1:4]] + [480, gx * gy * 8],
+        [*level1, xlow, xhigh, ylow, yhigh, total1, side_total],
+        far_outs=[FAR], scratch=[MIDDLE[i].grown_rows() for i in (0, 3, 4, 5, 6)] + [32, 32, 16], copies=1,
     )
-    ylow, yhigh = both_ways("gy", yup, ydown)
-    right1, field2, sides2, error1, coarse, coef1 = call(
-        middle_sweeps, "middle_sweeps", [s.grown_rows() for s in MIDDLE[1:4]] + [480, 16],
-        [coef1, right1, field2, zlow, zhigh, xlow, xhigh, ylow, yhigh, total1],
-        far_outs=[FAR], scratch=[MIDDLE[i].grown_rows() for i in (0, 3, 4)] + [32], copies=1,
-    )
-
-    zlow, zhigh = both_ways("gz", coarse, coarse)
-    (packed,) = call(spread, "spread", [gx * gy * 8], [coarse, zlow, zhigh], scratch=[16])
-    packed, shared = lax.optimization_barrier((packed, shared))
     packed = to_all(packed, gx * gy)
 
     tiles = 12 * gx * gy
     vmem = pl.BlockSpec(memory_space=pltpu.VMEM)
     far = pl.BlockSpec(memory_space=pltpu.HBM)
-    near = [packed, error1, right1, sides0, field2, sides2]
-    scratch = [gx * gy * SHARED, MIDDLE[0].grown_rows(), FINE[0].grown_rows(), tiles * 6, tiles, tiles, gx * 21 * gy]
+    near = [packed, error1, right1, stat, sides0, field2, sides2]
+    scratch = [gx * gy * SHARED, MIDDLE[0].grown_rows(), tiles * 6, tiles, tiles, gx * 21 * gy]
     scratch += [tiles, (2 * gx + 4) * 6 * (gy + 16), 144, 288, 144, 576]
     return pl.pallas_call(
         lambda *refs: finish(gx, gy, *refs),
         name="finish",
         out_shape=jax.ShapeDtypeStruct(guess.shape, F32),
-        in_specs=[far] * 3 + [vmem] * len(near),
+        in_specs=[far] * 2 + [vmem] * len(near),
         out_specs=vmem,
-        scratch_shapes=[pltpu.VMEM((rows, LANES), F32) for rows in scratch] + [pltpu.SemaphoreType.DMA((gx + 2,))],
+        scratch_shapes=[pltpu.VMEM((rows, LANES), F32) for rows in scratch] + [pltpu.SemaphoreType.DMA((gx + 1,))],
         compiler_params=pltpu.CompilerParams(vmem_limit_bytes=GRANT),
-    )(shared, coef1, stat, *near)
+    )(shared, coef1, *near)
 
 
 def solution(mesh):

time: 178 us -> 143 us (0.80)
  the two profiles are of different devices: /device:TPU:1 before, /device:TPU:2 now
where the time goes in v3:
time: 143 us; the launch traced here: 142 us
  waiting for transfers between devices  48.9 us (34%)
  starting transfers between devices  31.6 us (22%)
  blocking collectives  28.8 us (20%)
  Pallas kernels  14.1 us (10%)
  between operations  13.6 us (10%)
  local copies, waits for them, and re-layouts  5.33 us (4%)
    all_to_all x1, blocking collectives, to_all(): return lax.all_to_all(blocks, ('gx', 'gy'), 0, 0).reshape(value.shape)  28.8 us
    ppermute x6, waiting for transfers between devices, both_ways(): lax.ppermute(down, axis, [(b, a) for a, b in pairs])  25.3 us
    ppermute x6, waiting for transfers between devices, both_ways(): lax.ppermute(up, axis, pairs)  23.6 us
    ppermute x6, starting transfers between devices, both_ways(): lax.ppermute(up, axis, pairs)  19.1 us
    ppermute x6, starting transfers between devices, both_ways(): lax.ppermute(down, axis, [(b, a) for a, b in pairs])  12.5 us
    pallas_call x8, Pallas kernels, call(): pl.pallas_call(body, name=name, out_shape=[jax.ShapeDtypeStruct((rows, LA...  7.2 us
    pallas_call x1, Pallas kernels, per_device(): pl.pallas_call(lambda *refs: finish(gx, gy, *refs), name='finish', out_sh...  6.9 us
    unnamed x10, local copies, waits for them, and re-layouts  5.33 us
  transfers between devices with their start and end apart: 13, of which 12 were waited for; matrix products, arithmetic and copies ran while one was open for 0% of the time, Pallas kernels for 3%

profile of v3, /device:TPU:2, one launch (start us, length us, event | category | flops | bytes accessed | tf_op | source)
XLA Modules:
  0.0 142.2 jit_solution(6310352772046598544)
XLA Ops:
  10.3 1.5 %prepare.1 = (f32[1344,128]{1,0:T(8,128)S(1)}, f32[192,128]{1,0:T(8,128)S(1)}, f32[192,128]{1,0:T(8,128)S(1)}, f32[152,128]{1,0:T(8,128)S(1)}, f32[152,128]{1,0:...) custom-call(f32[18,8,8,128]{3,2,1,0:T(8,128)S(1)} %copy-done.1, ...), custom_call_target="tpu_custom_call" | custom-call | tf_op jit(solution)/shard_map/prepare/pallas_call | solution.py:43
  11.8 1.9 %collective-permute-start = (f32[152,128]{1,0:T(8,128)S(1)}, f32[152,128]{1,0:T(8,128)S(1)}, u32[]{:S(2)}, u32[]{:S(2)}) collective-permute-start(f32[152,128]{1,0:T(8,128)S(1)} %get-tuple-element.38.zown), channel_id=1, source_target_pairs={{0,1},{1,2},{2,3},{3,4},{4,5},{5,6},{6,7},{8,9},{9,10},{10,11},{11... | collective-permute-start | bytes 233480 | tf_op jit(solution)/shard_map/ppermute | solution.py:676
  13.8 3.6 %collective-permute-start.1 = (f32[152,128]{1,0:T(8,128)S(1)}, f32[152,128]{1,0:T(8,128)S(1)}, u32[]{:S(2)}, u32[]{:S(2)}) collective-permute-start(f32[152,128]{1,0:T(8,128)S(1)} %get-tuple-element.39), channel_id=1, source_target_pairs={{1,0},{2,1},{3,2},{4,3},{5,4},{6,5},{7,6},{9,8},{10,9},{11,10},{12... | collective-permute-start | bytes 233480 | tf_op jit(solution)/shard_map/ppermute | solution.py:676
  17.5 1.9 %collective-permute-done.1.zhigh.zhigh0 = f32[152,128]{1,0:T(8,128)S(1)} collective-permute-done((f32[152,128]{1,0:T(8,128)S(1)}, f32[152,128]{1,0:T(8,128)S(1)}, u32[]{:S(2)}, u32[]{:S(2)}) %collective-permute-start.1) | collective-permute-done | bytes 77856 | tf_op jit(solution)/shard_map/ppermute | solution.py:676
  20.3 3.5 %collective-permute-start.2 = (f32[456,128]{1,0:T(8,128)S(1)}, f32[456,128]{1,0:T(8,128)S(1)}, u32[]{:S(2)}, u32[]{:S(2)}) collective-permute-start(f32[456,128]{1,0:T(8,128)S(1)} %get-tuple-element.42), channel_id=1, source_target_pairs={{0,64},{64,128},{128,192},{192,256},{256,320},{320,384},{384,448},... | collective-permute-start | bytes 700424 | tf_op jit(solution)/shard_map/ppermute | solution.py:676
  25.1 4.1 %collective-permute-done.2.low = f32[456,128]{1,0:T(8,128)S(1)} collective-permute-done((f32[456,128]{1,0:T(8,128)S(1)}, f32[456,128]{1,0:T(8,128)S(1)}, u32[]{:S(2)}, u32[]{:S(2)}) %collective-permute-start.2) | collective-permute-done | bytes 233504 | tf_op jit(solution)/shard_map/ppermute | solution.py:676
  29.2 4.7 %collective-permute-done.3.high = f32[456,128]{1,0:T(8,128)S(1)} collective-permute-done((f32[456,128]{1,0:T(8,128)S(1)}, f32[456,128]{1,0:T(8,128)S(1)}, u32[]{:S(2)}, u32[]{:S(2)}) %collective-permute-start.3) | collective-permute-done | bytes 233504 | tf_op jit(solution)/shard_map/ppermute | solution.py:676
  34.1 4.3 %collective-permute-start.4 = (f32[528,128]{1,0:T(8,128)S(1)}, f32[528,128]{1,0:T(8,128)S(1)}, u32[]{:S(2)}, u32[]{:S(2)}) collective-permute-start(f32[528,128]{1,0:T(8,128)S(1)} %get-tuple-element.44), channel_id=1, source_target_pairs={{0,8},{8,16},{16,24},{24,32},{32,40},{40,48},{48,56},{1,9},{9,17},... | collective-permute-start | bytes 811016 | tf_op jit(solution)/shard_map/ppermute | solution.py:676
  39.7 4.9 %collective-permute-done.4.below = f32[528,128]{1,0:T(8,128)S(1)} collective-permute-done((f32[528,128]{1,0:T(8,128)S(1)}, f32[528,128]{1,0:T(8,128)S(1)}, u32[]{:S(2)}, u32[]{:S(2)}) %collective-permute-start.4) | collective-permute-done | bytes 270368 | tf_op jit(solution)/shard_map/ppermute | solution.py:676
  44.6 4.9 %collective-permute-done.5.above = f32[528,128]{1,0:T(8,128)S(1)} collective-permute-done((f32[528,128]{1,0:T(8,128)S(1)}, f32[528,128]{1,0:T(8,128)S(1)}, u32[]{:S(2)}, u32[]{:S(2)}) %collective-permute-start.5) | collective-permute-done | bytes 270368 | tf_op jit(solution)/shard_map/ppermute | solution.py:676
  49.5 2.2 %fine_sweeps.1 = (f32[4032,128]{1,0:T(8,128)S(1)}, f32[224,128]{1,0:T(8,128)S(1)}, f32[192,128]{1,0:T(8,128)S(1)}, f32[384,128]{1,0:T(8,128)S(1)}, f32[192,128]{1,0:T(8,128)S(1)}, /*index=5*/f32[192,128]{1,0:T(8,128)S(1)}) custom-call(f32[1344,128]{1,0:T(8,128)S(1)} %get-tuple-element.40.stat.stat0, f32[192,128]{1,0:T(8,128)S(1)} %get-tuple-element.41.field.field0, ...), custom_call_target="tpu_custom_call" | custom-call | tf_op jit(solution)/shard_map/fine_sweeps/pallas_call | solution.py:43
  51.7 1.9 %collective-permute-start.6 = (f32[192,128]{1,0:T(8,128)S(1)}, f32[192,128]{1,0:T(8,128)S(1)}, u32[]{:S(2)}, u32[]{:S(2)}) collective-permute-start(f32[192,128]{1,0:T(8,128)S(1)} %get-tuple-element.52), channel_id=1, source_target_pairs={{0,1},{1,2},{2,3},{3,4},{4,5},{5,6},{6,7},{8,9},{9,10},{10,11},{11... | collective-permute-start | bytes 294920 | tf_op jit(solution)/shard_map/ppermute | solution.py:676
  53.6 3.6 %collective-permute-start.7 = (f32[192,128]{1,0:T(8,128)S(1)}, f32[192,128]{1,0:T(8,128)S(1)}, u32[]{:S(2)}, u32[]{:S(2)}) collective-permute-start(f32[192,128]{1,0:T(8,128)S(1)} %get-tuple-element.53), channel_id=1, source_target_pairs={{1,0},{2,1},{3,2},{4,3},{5,4},{6,5},{7,6},{9,8},{10,9},{11,10},{12... | collective-permute-start | bytes 294920 | tf_op jit(solution)/shard_map/ppermute | solution.py:676
  57.6 1.8 %collective-permute-done.7.zhigh.zhigh0 = f32[192,128]{1,0:T(8,128)S(1)} collective-permute-done((f32[192,128]{1,0:T(8,128)S(1)}, f32[192,128]{1,0:T(8,128)S(1)}, u32[]{:S(2)}, u32[]{:S(2)}) %collective-permute-start.7) | collective-permute-done | bytes 98336 | tf_op jit(solution)/shard_map/ppermute | solution.py:676
  59.8 3.5 %collective-permute-start.8 = (f32[440,128]{1,0:T(8,128)S(1)}, f32[440,128]{1,0:T(8,128)S(1)}, u32[]{:S(2)}, u32[]{:S(2)}) collective-permute-start(f32[440,128]{1,0:T(8,128)S(1)} %get-tuple-element.58), channel_id=1, source_target_pairs={{0,64},{64,128},{128,192},{192,256},{256,320},{320,384},{384,448},... | collective-permute-start | bytes 675848 | tf_op jit(solution)/shard_map/ppermute | solution.py:676
  64.6 3.3 %collective-permute-done.8.low = f32[440,128]{1,0:T(8,128)S(1)} collective-permute-done((f32[440,128]{1,0:T(8,128)S(1)}, f32[440,128]{1,0:T(8,128)S(1)}, u32[]{:S(2)}, u32[]{:S(2)}) %collective-permute-start.8) | collective-permute-done | bytes 225312 | tf_op jit(solution)/shard_map/ppermute | solution.py:676
  67.9 5.1 %collective-permute-done.9.high = f32[440,128]{1,0:T(8,128)S(1)} collective-permute-done((f32[440,128]{1,0:T(8,128)S(1)}, f32[440,128]{1,0:T(8,128)S(1)}, u32[]{:S(2)}, u32[]{:S(2)}) %collective-permute-start.9) | collective-permute-done | bytes 225312 | tf_op jit(solution)/shard_map/ppermute | solution.py:676
  73.1 4.0 %collective-permute-start.10 = (f32[736,128]{1,0:T(8,128)S(1)}, f32[736,128]{1,0:T(8,128)S(1)}, u32[]{:S(2)}, u32[]{:S(2)}) collective-permute-start(f32[736,128]{1,0:T(8,128)S(1)} %get-tuple-element.60), channel_id=1, source_target_pairs={{0,8},{8,16},{16,24},{24,32},{32,40},{40,48},{48,56},{1,9},{9,17},... | collective-permute-start | bytes 1130504 | tf_op jit(solution)/shard_map/ppermute | solution.py:676
  78.4 10.8 %collective-permute-done.10.below = f32[736,128]{1,0:T(8,128)S(1)} collective-permute-done((f32[736,128]{1,0:T(8,128)S(1)}, f32[736,128]{1,0:T(8,128)S(1)}, u32[]{:S(2)}, u32[]{:S(2)}) %collective-permute-start.10) | collective-permute-done | bytes 376864 | tf_op jit(solution)/shard_map/ppermute | solution.py:676
  89.2 6.8 %collective-permute-done.11.above = f32[736,128]{1,0:T(8,128)S(1)} collective-permute-done((f32[736,128]{1,0:T(8,128)S(1)}, f32[736,128]{1,0:T(8,128)S(1)}, u32[]{:S(2)}, u32[]{:S(2)}) %collective-permute-start.11) | collective-permute-done | bytes 376864 | tf_op jit(solution)/shard_map/ppermute | solution.py:676
  96.0 2.0 %middle_sweeps.1 = (f32[576,128]{1,0:T(8,128)S(1)}, f32[576,128]{1,0:T(8,128)S(1)}, f32[192,128]{1,0:T(8,128)S(1)}, f32[480,128]{1,0:T(8,128)S(1)}, f32[512,128]{1,0:T(8,128)S(1)}, /*index=5*/f32[49152,128]{1,0:T(8,128)}) custom-call(f32[288,128]{1,0:T(8,128)S(1)} %get-tuple-element.54.coef.coef0, f32[48,128]{1,0:T(8,128)S(1)} %get-tuple-element.55.right.right0, ...), custom_call_target="tpu_custom_call" | custom-call | tf_op jit(solution)/shard_map/middle_sweeps/pallas_call | solution.py:43
  98.1 28.8 %all_to_all.5 = f32[64,8,128]{2,1,0:T(8,128)S(1)} all-to-all(f32[64,8,128]{2,1,0:T(8,128)S(1)} %bitcast.3), channel_id=1, replica_groups=mesh['gx'=8,'gy'=8,'gz'=8] {'gx','gy'}, dimensions={0} | all-to-all | bytes 524288 | tf_op jit(solution)/shard_map/all_to_all | solution.py:681
  126.8 1.6 %copy-done = f32[4096,128]{1,0:T(8,128)S(1)} copy-done((f32[4096,128]{1,0:T(8,128)S(1)}, f32[4096,128]{1,0:T(8,128)}, u32[]{:S(2)}) %copy-start) | copy-done | bytes 2097176
  128.4 6.9 %finish.1 = f32[3,8,8,128]{3,2,1,0:T(8,128)} custom-call(f32[4096,128]{1,0:T(8,128)S(1)} %copy-done, f32[49152,128]{1,0:T(8,128)} %get-tuple-element.63.refs_1_, f32[512,128]{1,0:T(8,128)S(1)} %bitcast.2, f32[480,128]{1,0:T(8,128)S(1)} %get-tuple-element.65.refs_3_, f32[576,128]{1,0:T(8,128)S(1)} %get-tuple-element.66.refs_4_, ...), custom_call_target="tpu_custom_call" | custom-call | tf_op jit(solution)/shard_map/finish/pallas_call | solution.py:726
  (23 shorter events, 10.9 us)
Async XLA Ops:
  6.5 120.3 %all-gather.2.cloned.1.call-start = ((), (), s32[]{:S(2)}) async-start(), calls=%async_computation.1 | async-start | bytes 2129920 | tf_op jit(solution)/shard_map/all_gather | solution.py:695
  6.5 1.1 copy-start.1
  7.6 0.9 copy-start.2
  8.5 0.9 copy-start.3
  9.4 0.9 copy-start.4
  11.8 5.7 %collective-permute-start = (f32[152,128]{1,0:T(8,128)S(1)}, f32[152,128]{1,0:T(8,128)S(1)}, u32[]{:S(2)}, u32[]{:S(2)}) collective-permute-start(f32[152,128]{1,0:T(8,128)S(1)} %get-tuple-element.38.zown), channel_id=1, source_target_pairs={{0,1},{1,2},{2,3},{3,4},{4,5},{5,6},{6,7},{8,9},{9,10},{10,11},{11... | collective-permute-start | bytes 233480 | tf_op jit(solution)/shard_map/ppermute | solution.py:676
  13.8 5.6 %collective-permute-start.1 = (f32[152,128]{1,0:T(8,128)S(1)}, f32[152,128]{1,0:T(8,128)S(1)}, u32[]{:S(2)}, u32[]{:S(2)}) collective-permute-start(f32[152,128]{1,0:T(8,128)S(1)} %get-tuple-element.39), channel_id=1, source_target_pairs={{1,0},{2,1},{3,2},{4,3},{5,4},{6,5},{7,6},{9,8},{10,9},{11,10},{12... | collective-permute-start | bytes 233480 | tf_op jit(solution)/shard_map/ppermute | solution.py:676
  20.3 8.9 %collective-permute-start.2 = (f32[456,128]{1,0:T(8,128)S(1)}, f32[456,128]{1,0:T(8,128)S(1)}, u32[]{:S(2)}, u32[]{:S(2)}) collective-permute-start(f32[456,128]{1,0:T(8,128)S(1)} %get-tuple-element.42), channel_id=1, source_target_pairs={{0,64},{64,128},{128,192},{192,256},{256,320},{320,384},{384,448},... | collective-permute-start | bytes 700424 | tf_op jit(solution)/shard_map/ppermute | solution.py:676
  23.8 10.1 %collective-permute-start.3 = (f32[456,128]{1,0:T(8,128)S(1)}, f32[456,128]{1,0:T(8,128)S(1)}, u32[]{:S(2)}, u32[]{:S(2)}) collective-permute-start(f32[456,128]{1,0:T(8,128)S(1)} %get-tuple-element.43), channel_id=1, source_target_pairs={{64,0},{128,64},{192,128},{256,192},{320,256},{384,320},{448,384},... | collective-permute-start | bytes 700424 | tf_op jit(solution)/shard_map/ppermute | solution.py:676
  34.1 10.5 %collective-permute-start.4 = (f32[528,128]{1,0:T(8,128)S(1)}, f32[528,128]{1,0:T(8,128)S(1)}, u32[]{:S(2)}, u32[]{:S(2)}) collective-permute-start(f32[528,128]{1,0:T(8,128)S(1)} %get-tuple-element.44), channel_id=1, source_target_pairs={{0,8},{8,16},{16,24},{24,32},{32,40},{40,48},{48,56},{1,9},{9,17},... | collective-permute-start | bytes 811016 | tf_op jit(solution)/shard_map/ppermute | solution.py:676
  38.4 11.1 %collective-permute-start.5 = (f32[528,128]{1,0:T(8,128)S(1)}, f32[528,128]{1,0:T(8,128)S(1)}, u32[]{:S(2)}, u32[]{:S(2)}) collective-permute-start(f32[528,128]{1,0:T(8,128)S(1)} %get-tuple-element.45), channel_id=1, source_target_pairs={{8,0},{16,8},{24,16},{32,24},{40,32},{48,40},{56,48},{9,1},{17,9},... | collective-permute-start | bytes 811016 | tf_op jit(solution)/shard_map/ppermute | solution.py:676
  51.7 5.9 %collective-permute-start.6 = (f32[192,128]{1,0:T(8,128)S(1)}, f32[192,128]{1,0:T(8,128)S(1)}, u32[]{:S(2)}, u32[]{:S(2)}) collective-permute-start(f32[192,128]{1,0:T(8,128)S(1)} %get-tuple-element.52), channel_id=1, source_target_pairs={{0,1},{1,2},{2,3},{3,4},{4,5},{5,6},{6,7},{8,9},{9,10},{10,11},{11... | collective-permute-start | bytes 294920 | tf_op jit(solution)/shard_map/ppermute | solution.py:676
  53.6 5.8 %collective-permute-start.7 = (f32[192,128]{1,0:T(8,128)S(1)}, f32[192,128]{1,0:T(8,128)S(1)}, u32[]{:S(2)}, u32[]{:S(2)}) collective-permute-start(f32[192,128]{1,0:T(8,128)S(1)} %get-tuple-element.53), channel_id=1, source_target_pairs={{1,0},{2,1},{3,2},{4,3},{5,4},{6,5},{7,6},{9,8},{10,9},{11,10},{12... | collective-permute-start | bytes 294920 | tf_op jit(solution)/shard_map/ppermute | solution.py:676
  59.8 8.1 %collective-permute-start.8 = (f32[440,128]{1,0:T(8,128)S(1)}, f32[440,128]{1,0:T(8,128)S(1)}, u32[]{:S(2)}, u32[]{:S(2)}) collective-permute-start(f32[440,128]{1,0:T(8,128)S(1)} %get-tuple-element.58), channel_id=1, source_target_pairs={{0,64},{64,128},{128,192},{192,256},{256,320},{320,384},{384,448},... | collective-permute-start | bytes 675848 | tf_op jit(solution)/shard_map/ppermute | solution.py:676
  63.3 9.7 %collective-permute-start.9 = (f32[440,128]{1,0:T(8,128)S(1)}, f32[440,128]{1,0:T(8,128)S(1)}, u32[]{:S(2)}, u32[]{:S(2)}) collective-permute-start(f32[440,128]{1,0:T(8,128)S(1)} %get-tuple-element.59), channel_id=1, source_target_pairs={{64,0},{128,64},{192,128},{256,192},{320,256},{384,320},{448,384},... | collective-permute-start | bytes 675848 | tf_op jit(solution)/shard_map/ppermute | solution.py:676
  73.1 16.1 %collective-permute-start.10 = (f32[736,128]{1,0:T(8,128)S(1)}, f32[736,128]{1,0:T(8,128)S(1)}, u32[]{:S(2)}, u32[]{:S(2)}) collective-permute-start(f32[736,128]{1,0:T(8,128)S(1)} %get-tuple-element.60), channel_id=1, source_target_pairs={{0,8},{8,16},{16,24},{24,32},{32,40},{40,48},{48,56},{1,9},{9,17},... | collective-permute-start | bytes 1130504 | tf_op jit(solution)/shard_map/ppermute | solution.py:676
  77.1 18.9 %collective-permute-start.11 = (f32[736,128]{1,0:T(8,128)S(1)}, f32[736,128]{1,0:T(8,128)S(1)}, u32[]{:S(2)}, u32[]{:S(2)}) collective-permute-start(f32[736,128]{1,0:T(8,128)S(1)} %get-tuple-element.61), channel_id=1, source_target_pairs={{8,0},{16,8},{24,16},{32,24},{40,32},{48,40},{56,48},{9,1},{17,9},... | collective-permute-start | bytes 1130504 | tf_op jit(solution)/shard_map/ppermute | solution.py:676
  126.8 1.6 %copy-start = (f32[4096,128]{1,0:T(8,128)S(1)}, f32[4096,128]{1,0:T(8,128)}, u32[]{:S(2)}) copy-start(f32[4096,128]{1,0:T(8,128)} %all-gather.2.cloned.1.call-done.refs_0_) | copy-start | bytes 6291460
Sparse Core Ops, SparseCore 0:
  20.4 90.5 all-gather.1

commit v4 on v3

--- a/solution.py
+++ b/solution.py
@@ -205,19 +205,11 @@
     zdown[pl.ds(64, MEANS), :] = sum2[pl.ds(0, MEANS), :]
 
 
-def prepare_whole(c_far, d_far, b_far, g_far, stat, field, total, zup, zdown, coef1, scale1, total1,
-                  c, d, b, g, summed, means1, half2, sum2, sum3, arrived):
-    copies = [
-        pltpu.make_async_copy(far, near, arrived.at[i])
-        for i, (far, near) in enumerate(((c_far, c), (d_far, d), (b_far, b), (g_far, g)))
-    ]
-    for copy in copies:
-        copy.start()
+def prepare_whole(inputs, stat, field, total, zup, zdown, coef1, scale1, total1, summed, means1, half2, sum2, sum3):
     sum2[pl.ds(80, 8), :] = jnp.zeros((8, LANES), F32)
     for out in (zup, zdown):
         out[pl.ds(144, 8), :] = jnp.zeros((8, LANES), F32)
-    for copy in copies:
-        copy.wait()
+    c, d, b, g = (inputs.at[pl.ds(first, number)] for first, number in ((0, 18), (18, 3), (21, 3), (24, 3)))
     prepare(c, d, b, g, stat, field, total, zup, zdown, coef1, scale1, total1, summed, means1, half2, sum2, sum3)
 
 
@@ -460,15 +452,17 @@
         out[pl.ds(copy * 8, 8), :] = block
 
 
-def coarse_place(x, e, j):
-    return (x * 3 + e) * 2 + j
-
-
-def coarse_coefs(gx, gy, shared, arrivals, coef, scale, total, coef3):
+def coarse_parts(gx, gy):
+    each = 4 * gx * gy
+    sizes = [3 * each, 3 * each, 6 * each, 6 * each, 6 * each, 21 * gx * gy]
+    return [(sum(sizes[:i]), size) for i, size in enumerate(sizes)]
+
+
+def coarse_coefs(gx, gy, shared, table_far, table, left):
+    (scale_at, _), (total_at, _), (coef_at, _), _, _, (coef3_at, size3) = coarse_parts(gx, gy)
     lane = lanes_of(gy)
     used = lane < 72
     for g in range(gx):
-        arrivals[g].wait()
 
         def rows(r):
             return shared[pl.ds(g * gy * SHARED + r, gy, SHARED), :]
@@ -494,11 +488,11 @@
 
                     w = [mean(6 * e + k) * 0.0625 for k in range(6)]
                     tot, inverse = settle(w, mean(18 + e))
-                    base = coarse_place(2 * g + i, e, j)
+                    base = (e * 2 * gx + 2 * g + i) * 2 + j
                     for k in range(6):
-                        coef[pl.ds((base * 6 + k) * gy, gy), :] = w[k] * inverse
-                    scale[pl.ds(base * gy, gy), :] = inverse
-                    total[pl.ds(base * gy, gy), :] = tot * 1.25
+                        table[pl.ds(coef_at + (base * 6 + k) * gy, gy), :] = w[k] * inverse
+                    table[pl.ds(scale_at + base * gy, gy), :] = inverse
+                    table[pl.ds(total_at + base * gy, gy), :] = tot * 1.25
 
             def mean3(a):
                 return jnp.where(lane < 36, rolled(thirds[a % 8], -36 * (a // 8), 1), F32(0))
@@ -506,13 +500,22 @@
             w = [mean3(6 * e + k) * 0.015625 for k in range(6)]
             tot, inverse = settle(w, mean3(18 + e))
             for k in range(6):
-                coef3[pl.ds(((g * 3 + e) * 7 + k) * gy, gy), :] = w[k] * inverse
-            coef3[pl.ds(((g * 3 + e) * 7 + 6) * gy, gy), :] = inverse
-
-
-def coarse_levels(gx, gy, me_x, me_y, packed, coef, scale, total, coef3, right2, error2, rows6):
+                table[pl.ds(coef3_at + ((g * 3 + e) * 7 + k) * gy, gy), :] = w[k] * inverse
+            table[pl.ds(coef3_at + ((g * 3 + e) * 7 + 6) * gy, gy), :] = inverse
+    keep = pltpu.make_async_copy(table, table_far.at[pl.ds(0, coef3_at + size3), :], left.at[0])
+    keep.start()
+    keep.wait()
+
+
+def coarse_levels(gx, gy, me_x, me_y, packed, table, arrivals, right2, error2, rows6):
     planes = 2 * gx
-    place = coarse_place
+    (scale_at, _), (total_at, _), (coef_at, _), _, _, (coef3_at, _) = coarse_parts(gx, gy)
+
+    def place(x, e, j):
+        return (e * 2 * gx + x) * 2 + j
+
+    error2[...] = jnp.zeros(error2.shape, F32)
+    arrivals[0].wait()
     lane = lanes_of(gy)
     used = lane < 72
     row = lax.broadcasted_iota(jnp.int32, (gy, LANES), 0)
@@ -528,7 +531,7 @@
                     right = blocks[r] if r < 6 else rolled(blocks[r - 6], 64, 1)
                     right = jnp.where(lane < 64, right, rolled(blocks[6], 64 - 8 * r, 1))
                     base = place(2 * g + i, e, j) * gy
-                    right2[pl.ds(base, gy), :] = jnp.where(used, right, F32(0)) * scale[pl.ds(base, gy), :]
+                    right2[pl.ds(base, gy), :] = jnp.where(used, right, F32(0)) * table[pl.ds(scale_at + base, gy), :]
 
     def sweep2(value, x, e, j):
         base = place(x, e, j)
@@ -544,7 +547,7 @@
         out = 0.2 * v + right2[pl.ds(base * gy, gy), :]
         for k in range(6):
             if near[k] is not None:
-                out = out + coef[pl.ds((base * 6 + k) * gy, gy), :] * near[k]
+                out = out + table[pl.ds(coef_at + (base * 6 + k) * gy, gy), :] * near[k]
         return out
 
     cells = [(x, j) for x in range(planes) for j in range(2)]
@@ -552,25 +555,28 @@
     fine = lax.broadcasted_iota(jnp.int32, (LANES, LANES), 1)
     coarse = lax.broadcasted_iota(jnp.int32, (LANES, LANES), 0)
     double = jnp.where((fine >> 1) == coarse, F32(1), F32(0))
-    error2[...] = jnp.zeros(error2.shape, F32)
     before, sums = [], []
     for e in range(3):
+        if e == 0:
+            arrivals[1].wait()
+        arrivals[2 + e].wait()
         value = {(x, j): right2[pl.ds(place(x, e, j) * gy, gy), :] for x, j in cells}
         value = {(x, j): sweep2(value, x, e, j) for x, j in cells}
         before.append(value)
         resid = {
-            (x, j): (sweep2(value, x, e, j) - value[x, j]) * total[pl.ds(place(x, e, j) * gy, gy), :] for x, j in cells
+            (x, j): (sweep2(value, x, e, j) - value[x, j]) * table[pl.ds(total_at + place(x, e, j) * gy, gy), :] for x, j in cells
         }
         for g in range(gx):
             sums.append(
                 (resid[2 * g, 0] + resid[2 * g, 1]) + (resid[2 * g + 1, 0] + resid[2 * g + 1, 1])
             )
+    arrivals[5].wait()
     right3 = exact_dot(jnp.concatenate(sums, axis=0), halve)
     found = []
     for e in range(3):
 
         def coef_of(g, k):
-            return coef3[pl.ds(((g * 3 + e) * 7 + k) * gy, gy), :]
+            return table[pl.ds(coef3_at + ((g * 3 + e) * 7 + k) * gy, gy), :]
 
         right = [right3[(e * gx + g) * gy : (e * gx + g + 1) * gy] * coef_of(g, 6) for g in range(gx)]
         value = right
@@ -598,7 +604,7 @@
         for step in range(2):
             value = {(x, j): sweep2(value, x, e, j) for x, j in cells}
         for x, j in cells:
-            error2[pl.ds(place(x + 2, e, j) * (gy + 16) + 8, gy), :] = value[x, j]
+            error2[pl.ds((((x + 2) * 3 + e) * 2 + j) * (gy + 16) + 8, gy), :] = value[x, j]
     for plane in range(6):
         for e in range(3):
             for step, j, target in ((0, 0, 0), (0, 1, 1), (1, 0, 2), (1, 1, 3), (-1, 0, 6), (-1, 1, 7)):
@@ -607,24 +613,20 @@
             rows6[pl.ds((plane * 3 + e) * 8 + 4, 2), :] = jnp.zeros((2, LANES), F32)
 
 
-def finish(gx, gy, shared_far, coef1_far, packed, error1, right1, stat, sides0, field2, sides2, out,
-           shared, coef1, coef2, scale2, total2, coef3, right2, error2, rows6, fine2, rows1, fine1, arrived):
-    chunk = gy * SHARED
+def finish(gx, gy, table_far, coef1_far, packed, error1, right1, stat, sides0, field2, sides2, out,
+           table, coef1, right2, error2, rows6, fine2, rows1, fine1, arrived):
+    inner = pl.ds(18 * 16, 8 * 18 * 16)
+    pieces = [(table_far, table, pl.ds(first, size)) for first, size in coarse_parts(gx, gy)]
+    pieces.append((coef1_far, coef1, inner))
     arrivals = [
-        pltpu.make_async_copy(shared_far.at[pl.ds(g * chunk, chunk), :], shared.at[pl.ds(g * chunk, chunk), :], arrived.at[g])
-        for g in range(gx)
+        pltpu.make_async_copy(far.at[rows, :], near.at[rows, :], arrived.at[i])
+        for i, (far, near, rows) in enumerate(pieces)
     ]
-    inner = pl.ds(18 * 16, 8 * 18 * 16)
-    later = [
-        pltpu.make_async_copy(coef1_far.at[inner, :], coef1.at[inner, :], arrived.at[gx]),
-    ]
-    for copy in arrivals + later:
+    for copy in arrivals:
         copy.start()
-    coarse_coefs(gx, gy, shared, arrivals, coef2, scale2, total2, coef3)
     me_x, me_y = lax.axis_index("gx"), lax.axis_index("gy")
-    coarse_levels(gx, gy, me_x, me_y, packed, coef2, scale2, total2, coef3, right2, error2, rows6)
-    for copy in later:
-        copy.wait()
+    coarse_levels(gx, gy, me_x, me_y, packed, table, arrivals, right2, error2, rows6)
+    arrivals[6].wait()
 
     source = lax.broadcasted_iota(jnp.int32, (LANES, LANES), 0)
     target = lax.broadcasted_iota(jnp.int32, (LANES, LANES), 1)
@@ -683,11 +685,10 @@
 
 def per_device(couplings, diagonal, right_side, guess):
     gx, gy = lax.axis_size("gx"), lax.axis_size("gy")
-    inputs = (couplings, diagonal, right_side, guess)
+    inputs = jnp.concatenate([couplings, diagonal, right_side, guess])
 
     stat, field, total, zup, zdown, coef1, scale1, total1 = call(
-        prepare_whole, "prepare", [1344, 192, 192, Z_ROWS, Z_ROWS, 288, 48, 48], [], far_args=inputs,
-        scratch=[value.shape for value in inputs] + [672, 336, 168, 88, 48], copies=4,
+        prepare_whole, "prepare", [1344, 192, 192, Z_ROWS, Z_ROWS, 288, 48, 48], [inputs], scratch=[672, 336, 168, 88, 48]
     )
     zlow, zhigh = both_ways("gz", zup, zdown)
     xup, xdown = call(fine_x, "fine_x", [x_rows(FINE)] * 2, [stat, field, zlow, zhigh])
@@ -717,21 +718,24 @@
     )
     packed = to_all(packed, gx * gy)
 
-    tiles = 12 * gx * gy
+    rows = sum(coarse_parts(gx, gy)[-1])
+    (table,) = call(
+        lambda *refs: coarse_coefs(gx, gy, *refs), "coarse_coefs", [], [shared], far_outs=[FAR], scratch=[rows], copies=1
+    )
+
     vmem = pl.BlockSpec(memory_space=pltpu.VMEM)
     far = pl.BlockSpec(memory_space=pltpu.HBM)
     near = [packed, error1, right1, stat, sides0, field2, sides2]
-    scratch = [gx * gy * SHARED, MIDDLE[0].grown_rows(), tiles * 6, tiles, tiles, gx * 21 * gy]
-    scratch += [tiles, (2 * gx + 4) * 6 * (gy + 16), 144, 288, 144, 576]
+    scratch = [rows, MIDDLE[0].grown_rows(), 12 * gx * gy, (2 * gx + 4) * 6 * (gy + 16), 144, 288, 144, 576]
     return pl.pallas_call(
         lambda *refs: finish(gx, gy, *refs),
         name="finish",
         out_shape=jax.ShapeDtypeStruct(guess.shape, F32),
         in_specs=[far] * 2 + [vmem] * len(near),
         out_specs=vmem,
-        scratch_shapes=[pltpu.VMEM((rows, LANES), F32) for rows in scratch] + [pltpu.SemaphoreType.DMA((gx + 1,))],
+        scratch_shapes=[pltpu.VMEM((rows, LANES), F32) for rows in scratch] + [pltpu.SemaphoreType.DMA((7,))],
         compiler_params=pltpu.CompilerParams(vmem_limit_bytes=GRANT),
-    )(shared, coef1, *near)
+    )(table, coef1, *near)
 
 
 def solution(mesh):

time: 143 us -> 133 us (0.930)
  blocking collectives: 28.8 us -> 0 us
  waiting for transfers between devices: 48.9 us -> 61.6 us
  starting transfers between devices: 31.6 us -> 38.3 us
  local copies, waits for them, and re-layouts: 5.33 us -> 1.59 us
  Pallas kernels: 14.1 us -> 16.3 us
    all_to_all x1 -> x0, blocking collectives: 28.8 us -> none  [to_all(): return lax.all_to_all(blocks, ('gx', 'gy'), 0, 0).reshape(value.shape)]
    all_to_all x0 -> x1, starting transfers between devices: none -> 11.9 us  [to_all(): return lax.all_to_all(blocks, ('gx', 'gy'), 0, 0).reshape(value.shape)]
    all_to_all x0 -> x1, waiting for transfers between devices: none -> 8.57 us  [to_all(): return lax.all_to_all(blocks, ('gx', 'gy'), 0, 0).reshape(value.shape)]
    unnamed x10 -> x2, local copies, waits for them, and re-layouts: 5.33 us -> 1.59 us
    pallas_call x8 -> x9, Pallas kernels: 7.2 us -> 10.7 us  [call(): pl.pallas_call(body, name=name, out_shape=[jax.ShapeDtypeStruct((rows, LA...]
    ppermute x6, starting transfers between devices: 19.1 us -> 15.7 us  [both_ways(): lax.ppermute(up, axis, pairs)]
    ppermute x6, waiting for transfers between devices: 23.6 us -> 25.7 us  [both_ways(): lax.ppermute(up, axis, pairs)]
    all_gather x1, waiting for transfers between devices: 0.01 us -> 1.75 us  [per_device(): shared = lax.all_gather(shared, ('gx', 'gy'), tiled=True)]
  transfers between devices with their start and end apart: 13 -> 14, of which waited for: 12 -> 13; matrix products, arithmetic and copies ran while one was open for 0% -> 0% of each run, Pallas kernels for 3% -> 7%
where the time goes in v4:
time: 133 us
  waiting for transfers between devices  61.6 us (46%)
  starting transfers between devices  38.3 us (29%)
  Pallas kernels  16.3 us (12%)
  between operations  13.6 us (10%)
  local copies, waits for them, and re-layouts  1.59 us (1%)
    ppermute x6, waiting for transfers between devices, both_ways(): lax.ppermute(up, axis, pairs)  25.7 us
    ppermute x6, waiting for transfers between devices, both_ways(): lax.ppermute(down, axis, [(b, a) for a, b in pairs])  25.6 us
    ppermute x6, starting transfers between devices, both_ways(): lax.ppermute(up, axis, pairs)  15.7 us
    all_to_all x1, starting transfers between devices, to_all(): return lax.all_to_all(blocks, ('gx', 'gy'), 0, 0).reshape(value.shape)  11.9 us
    ppermute x6, starting transfers between devices, both_ways(): lax.ppermute(down, axis, [(b, a) for a, b in pairs])  10.7 us
    pallas_call x9, Pallas kernels, call(): pl.pallas_call(body, name=name, out_shape=[jax.ShapeDtypeStruct((rows, LA...  10.7 us
    all_to_all x1, waiting for transfers between devices, to_all(): return lax.all_to_all(blocks, ('gx', 'gy'), 0, 0).reshape(value.shape)  8.57 us
    pallas_call x1, Pallas kernels, per_device(): pl.pallas_call(lambda *refs: finish(gx, gy, *refs), name='finish', out_sh...  5.61 us
  transfers between devices with their start and end apart: 14, of which 13 were waited for; matrix products, arithmetic and copies ran while one was open for 0% of the time, Pallas kernels for 7%

profile of v4, /device:TPU:2, one launch (start us, length us, event | category | flops | bytes accessed | tf_op | source)
XLA Modules:
  0.0 132.7 jit_solution(6274076454380562674)
XLA Ops:
  8.9 1.9 %collective-permute-start.1 = (f32[152,128]{1,0:T(8,128)S(1)}, f32[152,128]{1,0:T(8,128)S(1)}, u32[]{:S(2)}, u32[]{:S(2)}) collective-permute-start(f32[152,128]{1,0:T(8,128)S(1)} %get-tuple-element.39), channel_id=1, source_target_pairs={{1,0},{2,1},{3,2},{4,3},{5,4},{6,5},{7,6},{9,8},{10,9},{11,10},{12... | collective-permute-start | bytes 233480 | tf_op jit(solution)/shard_map/ppermute | solution.py:678
  10.8 2.4 %collective-permute-start = (f32[152,128]{1,0:T(8,128)S(1)}, f32[152,128]{1,0:T(8,128)S(1)}, u32[]{:S(2)}, u32[]{:S(2)}) collective-permute-start(f32[152,128]{1,0:T(8,128)S(1)} %get-tuple-element.38.zown), channel_id=1, source_target_pairs={{0,1},{1,2},{2,3},{3,4},{4,5},{5,6},{6,7},{8,9},{9,10},{10,11},{11... | collective-permute-start | bytes 233480 | tf_op jit(solution)/shard_map/ppermute | solution.py:678
  13.2 7.6 %collective-permute-done.zlow.zlow0 = f32[152,128]{1,0:T(8,128)S(1)} collective-permute-done((f32[152,128]{1,0:T(8,128)S(1)}, f32[152,128]{1,0:T(8,128)S(1)}, u32[]{:S(2)}, u32[]{:S(2)}) %collective-permute-start) | collective-permute-done | bytes 77856 | tf_op jit(solution)/shard_map/ppermute | solution.py:678
  24.3 2.3 %collective-permute-done.2.low = f32[456,128]{1,0:T(8,128)S(1)} collective-permute-done((f32[456,128]{1,0:T(8,128)S(1)}, f32[456,128]{1,0:T(8,128)S(1)}, u32[]{:S(2)}, u32[]{:S(2)}) %collective-permute-start.2) | collective-permute-done | bytes 233504 | tf_op jit(solution)/shard_map/ppermute | solution.py:678
  26.5 4.4 %collective-permute-done.3.high = f32[456,128]{1,0:T(8,128)S(1)} collective-permute-done((f32[456,128]{1,0:T(8,128)S(1)}, f32[456,128]{1,0:T(8,128)S(1)}, u32[]{:S(2)}, u32[]{:S(2)}) %collective-permute-start.3) | collective-permute-done | bytes 233504 | tf_op jit(solution)/shard_map/ppermute | solution.py:678
  31.1 2.7 %collective-permute-start.4 = (f32[528,128]{1,0:T(8,128)S(1)}, f32[528,128]{1,0:T(8,128)S(1)}, u32[]{:S(2)}, u32[]{:S(2)}) collective-permute-start(f32[528,128]{1,0:T(8,128)S(1)} %get-tuple-element.44), channel_id=1, source_target_pairs={{0,8},{8,16},{16,24},{24,32},{32,40},{40,48},{48,56},{1,9},{9,17},... | collective-permute-start | bytes 811016 | tf_op jit(solution)/shard_map/ppermute | solution.py:678
  35.1 2.6 %collective-permute-done.4.below = f32[528,128]{1,0:T(8,128)S(1)} collective-permute-done((f32[528,128]{1,0:T(8,128)S(1)}, f32[528,128]{1,0:T(8,128)S(1)}, u32[]{:S(2)}, u32[]{:S(2)}) %collective-permute-start.4) | collective-permute-done | bytes 270368 | tf_op jit(solution)/shard_map/ppermute | solution.py:678
  37.7 4.9 %collective-permute-done.5.above = f32[528,128]{1,0:T(8,128)S(1)} collective-permute-done((f32[528,128]{1,0:T(8,128)S(1)}, f32[528,128]{1,0:T(8,128)S(1)}, u32[]{:S(2)}, u32[]{:S(2)}) %collective-permute-start.5) | collective-permute-done | bytes 270368 | tf_op jit(solution)/shard_map/ppermute | solution.py:678
  42.6 2.2 %fine_sweeps.1 = (f32[4032,128]{1,0:T(8,128)S(1)}, f32[224,128]{1,0:T(8,128)S(1)}, f32[192,128]{1,0:T(8,128)S(1)}, f32[384,128]{1,0:T(8,128)S(1)}, f32[192,128]{1,0:T(8,128)S(1)}, /*index=5*/f32[192,128]{1,0:T(8,128)S(1)}) custom-call(f32[1344,128]{1,0:T(8,128)S(1)} %get-tuple-element.40.stat.stat0, f32[192,128]{1,0:T(8,128)S(1)} %get-tuple-element.41.field.field0, ...), custom_call_target="tpu_custom_call" | custom-call | tf_op jit(solution)/shard_map/fine_sweeps/pallas_call | solution.py:43
  44.9 1.9 %collective-permute-start.6 = (f32[192,128]{1,0:T(8,128)S(1)}, f32[192,128]{1,0:T(8,128)S(1)}, u32[]{:S(2)}, u32[]{:S(2)}) collective-permute-start(f32[192,128]{1,0:T(8,128)S(1)} %get-tuple-element.52), channel_id=1, source_target_pairs={{0,1},{1,2},{2,3},{3,4},{4,5},{5,6},{6,7},{8,9},{9,10},{10,11},{11... | collective-permute-start | bytes 294920 | tf_op jit(solution)/shard_map/ppermute | solution.py:678
  46.8 3.6 %collective-permute-start.7 = (f32[192,128]{1,0:T(8,128)S(1)}, f32[192,128]{1,0:T(8,128)S(1)}, u32[]{:S(2)}, u32[]{:S(2)}) collective-permute-start(f32[192,128]{1,0:T(8,128)S(1)} %get-tuple-element.53), channel_id=1, source_target_pairs={{1,0},{2,1},{3,2},{4,3},{5,4},{6,5},{7,6},{9,8},{10,9},{11,10},{12... | collective-permute-start | bytes 294920 | tf_op jit(solution)/shard_map/ppermute | solution.py:678
  50.8 1.8 %collective-permute-done.7.zhigh.zhigh0 = f32[192,128]{1,0:T(8,128)S(1)} collective-permute-done((f32[192,128]{1,0:T(8,128)S(1)}, f32[192,128]{1,0:T(8,128)S(1)}, u32[]{:S(2)}, u32[]{:S(2)}) %collective-permute-start.7) | collective-permute-done | bytes 98336 | tf_op jit(solution)/shard_map/ppermute | solution.py:678
  53.0 3.5 %collective-permute-start.8 = (f32[440,128]{1,0:T(8,128)S(1)}, f32[440,128]{1,0:T(8,128)S(1)}, u32[]{:S(2)}, u32[]{:S(2)}) collective-permute-start(f32[440,128]{1,0:T(8,128)S(1)} %get-tuple-element.58), channel_id=1, source_target_pairs={{0,64},{64,128},{128,192},{192,256},{256,320},{320,384},{384,448},... | collective-permute-start | bytes 675848 | tf_op jit(solution)/shard_map/ppermute | solution.py:678
  57.8 3.7 %collective-permute-done.8.low = f32[440,128]{1,0:T(8,128)S(1)} collective-permute-done((f32[440,128]{1,0:T(8,128)S(1)}, f32[440,128]{1,0:T(8,128)S(1)}, u32[]{:S(2)}, u32[]{:S(2)}) %collective-permute-start.8) | collective-permute-done | bytes 225312 | tf_op jit(solution)/shard_map/ppermute | solution.py:678
  61.5 5.7 %collective-permute-done.9.high = f32[440,128]{1,0:T(8,128)S(1)} collective-permute-done((f32[440,128]{1,0:T(8,128)S(1)}, f32[440,128]{1,0:T(8,128)S(1)}, u32[]{:S(2)}, u32[]{:S(2)}) %collective-permute-start.9) | collective-permute-done | bytes 225312 | tf_op jit(solution)/shard_map/ppermute | solution.py:678
  67.3 3.9 %collective-permute-start.10 = (f32[736,128]{1,0:T(8,128)S(1)}, f32[736,128]{1,0:T(8,128)S(1)}, u32[]{:S(2)}, u32[]{:S(2)}) collective-permute-start(f32[736,128]{1,0:T(8,128)S(1)} %get-tuple-element.60), channel_id=1, source_target_pairs={{0,8},{8,16},{16,24},{24,32},{32,40},{40,48},{48,56},{1,9},{9,17},... | collective-permute-start | bytes 1130504 | tf_op jit(solution)/shard_map/ppermute | solution.py:678
  72.4 9.1 %collective-permute-done.10.below = f32[736,128]{1,0:T(8,128)S(1)} collective-permute-done((f32[736,128]{1,0:T(8,128)S(1)}, f32[736,128]{1,0:T(8,128)S(1)}, u32[]{:S(2)}, u32[]{:S(2)}) %collective-permute-start.10) | collective-permute-done | bytes 376864 | tf_op jit(solution)/shard_map/ppermute | solution.py:678
  81.5 8.8 %collective-permute-done.11.above = f32[736,128]{1,0:T(8,128)S(1)} collective-permute-done((f32[736,128]{1,0:T(8,128)S(1)}, f32[736,128]{1,0:T(8,128)S(1)}, u32[]{:S(2)}, u32[]{:S(2)}) %collective-permute-start.11) | collective-permute-done | bytes 376864 | tf_op jit(solution)/shard_map/ppermute | solution.py:678
  90.3 2.7 %middle_sweeps.1 = (f32[576,128]{1,0:T(8,128)S(1)}, f32[576,128]{1,0:T(8,128)S(1)}, f32[192,128]{1,0:T(8,128)S(1)}, f32[480,128]{1,0:T(8,128)S(1)}, f32[512,128]{1,0:T(8,128)}, /*index=5*/f32[49152,128]{1,0:T(8,128)}) custom-call(f32[288,128]{1,0:T(8,128)S(1)} %get-tuple-element.54.coef.coef0, f32[48,128]{1,0:T(8,128)S(1)} %get-tuple-element.55.right.right0, ...), custom_call_target="tpu_custom_call" | custom-call | tf_op jit(solution)/shard_map/middle_sweeps/pallas_call | solution.py:43
  93.1 11.9 %all-to-all-start = ((f32[64,8,128]{2,1,0:T(8,128)}), f32[64,8,128]{2,1,0:T(8,128)S(1)}, u32[]{:S(2)}, u32[]{:S(2)}) async-start(f32[64,8,128]{2,1,0:T(8,128)} %bitcast), calls=%async_computation | async-start | bytes 524288 | tf_op jit(solution)/shard_map/all_to_all | solution.py:683
  105.0 1.8 %all-gather.2.cloned.1.call-done.refs_0_ = f32[4096,128]{1,0:T(8,128)} async-done(((f32[64,128]{1,0:T(8,128)}), f32[4096,128]{1,0:T(8,128)}) %all-gather.2.cloned.1.call-update) | async-done | bytes 2097168 | tf_op jit(solution)/shard_map/all_gather | solution.py:696
  108.3 3.3 %coarse_coefs.1.refs_0_ = f32[49152,128]{1,0:T(8,128)} custom-call(f32[4096,128]{1,0:T(8,128)S(1)} %copy-done), custom_call_target="tpu_custom_call" | custom-call | tf_op jit(solution)/shard_map/coarse_coefs/pallas_call | solution.py:43
  111.6 8.6 %all-to-all-done = f32[64,8,128]{2,1,0:T(8,128)S(1)} async-done(((f32[64,8,128]{2,1,0:T(8,128)}), f32[64,8,128]{2,1,0:T(8,128)S(1)}, u32[]{:S(2)}, u32[]{:S(2)}) %all-to-all-start) | async-done | bytes 262176 | tf_op jit(solution)/shard_map/all_to_all | solution.py:683
  120.2 5.6 %finish.1 = f32[3,8,8,128]{3,2,1,0:T(8,128)} custom-call(f32[49152,128]{1,0:T(8,128)} %coarse_coefs.1.refs_0_, f32[49152,128]{1,0:T(8,128)} %get-tuple-element.63.refs_1_, f32[512,128]{1,0:T(8,128)S(1)} %bitcast.2, f32[480,128]{1,0:T(8,128)S(1)} %get-tuple-element.65.refs_3_, f32[576,128]{1,0:T(8,128)S(1)} %get-tuple-element.66.refs_4_, ...), custom_call_target="tpu_custom_call" | custom-call | tf_op jit(solution)/shard_map/finish/pallas_call | solution.py:730
  (18 shorter events, 12.2 us)
Async XLA Ops:
  6.5 100.2 %all-gather.2.cloned.1.call-start = ((), (), s32[]{:S(2)}) async-start(), calls=%async_computation.1 | async-start | bytes 2129920 | tf_op jit(solution)/shard_map/all_gather | solution.py:696
  8.9 4.3 %collective-permute-start.1 = (f32[152,128]{1,0:T(8,128)S(1)}, f32[152,128]{1,0:T(8,128)S(1)}, u32[]{:S(2)}, u32[]{:S(2)}) collective-permute-start(f32[152,128]{1,0:T(8,128)S(1)} %get-tuple-element.39), channel_id=1, source_target_pairs={{1,0},{2,1},{3,2},{4,3},{5,4},{6,5},{7,6},{9,8},{10,9},{11,10},{12... | collective-permute-start | bytes 233480 | tf_op jit(solution)/shard_map/ppermute | solution.py:678
  10.8 10.0 %collective-permute-start = (f32[152,128]{1,0:T(8,128)S(1)}, f32[152,128]{1,0:T(8,128)S(1)}, u32[]{:S(2)}, u32[]{:S(2)}) collective-permute-start(f32[152,128]{1,0:T(8,128)S(1)} %get-tuple-element.38.zown), channel_id=1, source_target_pairs={{0,1},{1,2},{2,3},{3,4},{4,5},{5,6},{6,7},{8,9},{9,10},{10,11},{11... | collective-permute-start | bytes 233480 | tf_op jit(solution)/shard_map/ppermute | solution.py:678
  21.7 4.9 %collective-permute-start.2 = (f32[456,128]{1,0:T(8,128)S(1)}, f32[456,128]{1,0:T(8,128)S(1)}, u32[]{:S(2)}, u32[]{:S(2)}) collective-permute-start(f32[456,128]{1,0:T(8,128)S(1)} %get-tuple-element.42), channel_id=1, source_target_pairs={{0,64},{64,128},{128,192},{192,256},{256,320},{320,384},{384,448},... | collective-permute-start | bytes 700424 | tf_op jit(solution)/shard_map/ppermute | solution.py:678
  23.0 8.0 %collective-permute-start.3 = (f32[456,128]{1,0:T(8,128)S(1)}, f32[456,128]{1,0:T(8,128)S(1)}, u32[]{:S(2)}, u32[]{:S(2)}) collective-permute-start(f32[456,128]{1,0:T(8,128)S(1)} %get-tuple-element.43), channel_id=1, source_target_pairs={{64,0},{128,64},{192,128},{256,192},{320,256},{384,320},{448,384},... | collective-permute-start | bytes 700424 | tf_op jit(solution)/shard_map/ppermute | solution.py:678
  31.1 6.6 %collective-permute-start.4 = (f32[528,128]{1,0:T(8,128)S(1)}, f32[528,128]{1,0:T(8,128)S(1)}, u32[]{:S(2)}, u32[]{:S(2)}) collective-permute-start(f32[528,128]{1,0:T(8,128)S(1)} %get-tuple-element.44), channel_id=1, source_target_pairs={{0,8},{8,16},{16,24},{24,32},{32,40},{40,48},{48,56},{1,9},{9,17},... | collective-permute-start | bytes 811016 | tf_op jit(solution)/shard_map/ppermute | solution.py:678
  33.8 8.9 %collective-permute-start.5 = (f32[528,128]{1,0:T(8,128)S(1)}, f32[528,128]{1,0:T(8,128)S(1)}, u32[]{:S(2)}, u32[]{:S(2)}) collective-permute-start(f32[528,128]{1,0:T(8,128)S(1)} %get-tuple-element.45), channel_id=1, source_target_pairs={{8,0},{16,8},{24,16},{32,24},{40,32},{48,40},{56,48},{9,1},{17,9},... | collective-permute-start | bytes 811016 | tf_op jit(solution)/shard_map/ppermute | solution.py:678
  44.9 5.9 %collective-permute-start.6 = (f32[192,128]{1,0:T(8,128)S(1)}, f32[192,128]{1,0:T(8,128)S(1)}, u32[]{:S(2)}, u32[]{:S(2)}) collective-permute-start(f32[192,128]{1,0:T(8,128)S(1)} %get-tuple-element.52), channel_id=1, source_target_pairs={{0,1},{1,2},{2,3},{3,4},{4,5},{5,6},{6,7},{8,9},{9,10},{10,11},{11... | collective-permute-start | bytes 294920 | tf_op jit(solution)/shard_map/ppermute | solution.py:678
  46.8 5.8 %collective-permute-start.7 = (f32[192,128]{1,0:T(8,128)S(1)}, f32[192,128]{1,0:T(8,128)S(1)}, u32[]{:S(2)}, u32[]{:S(2)}) collective-permute-start(f32[192,128]{1,0:T(8,128)S(1)} %get-tuple-element.53), channel_id=1, source_target_pairs={{1,0},{2,1},{3,2},{4,3},{5,4},{6,5},{7,6},{9,8},{10,9},{11,10},{12... | collective-permute-start | bytes 294920 | tf_op jit(solution)/shard_map/ppermute | solution.py:678
  53.0 8.5 %collective-permute-start.8 = (f32[440,128]{1,0:T(8,128)S(1)}, f32[440,128]{1,0:T(8,128)S(1)}, u32[]{:S(2)}, u32[]{:S(2)}) collective-permute-start(f32[440,128]{1,0:T(8,128)S(1)} %get-tuple-element.58), channel_id=1, source_target_pairs={{0,64},{64,128},{128,192},{192,256},{256,320},{320,384},{384,448},... | collective-permute-start | bytes 675848 | tf_op jit(solution)/shard_map/ppermute | solution.py:678
  56.5 10.7 %collective-permute-start.9 = (f32[440,128]{1,0:T(8,128)S(1)}, f32[440,128]{1,0:T(8,128)S(1)}, u32[]{:S(2)}, u32[]{:S(2)}) collective-permute-start(f32[440,128]{1,0:T(8,128)S(1)} %get-tuple-element.59), channel_id=1, source_target_pairs={{64,0},{128,64},{192,128},{256,192},{320,256},{384,320},{448,384},... | collective-permute-start | bytes 675848 | tf_op jit(solution)/shard_map/ppermute | solution.py:678
  67.3 14.3 %collective-permute-start.10 = (f32[736,128]{1,0:T(8,128)S(1)}, f32[736,128]{1,0:T(8,128)S(1)}, u32[]{:S(2)}, u32[]{:S(2)}) collective-permute-start(f32[736,128]{1,0:T(8,128)S(1)} %get-tuple-element.60), channel_id=1, source_target_pairs={{0,8},{8,16},{16,24},{24,32},{32,40},{40,48},{48,56},{1,9},{9,17},... | collective-permute-start | bytes 1130504 | tf_op jit(solution)/shard_map/ppermute | solution.py:678
  71.1 19.2 %collective-permute-start.11 = (f32[736,128]{1,0:T(8,128)S(1)}, f32[736,128]{1,0:T(8,128)S(1)}, u32[]{:S(2)}, u32[]{:S(2)}) collective-permute-start(f32[736,128]{1,0:T(8,128)S(1)} %get-tuple-element.61), channel_id=1, source_target_pairs={{8,0},{16,8},{24,16},{32,24},{40,32},{48,40},{56,48},{9,1},{17,9},... | collective-permute-start | bytes 1130504 | tf_op jit(solution)/shard_map/ppermute | solution.py:678
  93.1 27.1 %all-to-all-start = ((f32[64,8,128]{2,1,0:T(8,128)}), f32[64,8,128]{2,1,0:T(8,128)S(1)}, u32[]{:S(2)}, u32[]{:S(2)}) async-start(f32[64,8,128]{2,1,0:T(8,128)} %bitcast), calls=%async_computation | async-start | bytes 524288 | tf_op jit(solution)/shard_map/all_to_all | solution.py:683
  106.7 1.6 %copy-start = (f32[4096,128]{1,0:T(8,128)S(1)}, f32[4096,128]{1,0:T(8,128)}, u32[]{:S(2)}) copy-start(f32[4096,128]{1,0:T(8,128)} %all-gather.2.cloned.1.call-done.refs_0_) | copy-start | bytes 6291460
Sparse Core Ops, SparseCore 0:
  21.8 84.9 all-gather.1

commit v5 on v4

--- a/solution.py
+++ b/solution.py
@@ -65,8 +65,8 @@
         return (self.planes + 2 * self.halo) * self.count * 16
 
 
-FINE = [Stream(STATIC, 8, 8, 2, 2), Stream(3, 8, 8, 3, 3), Stream(1, 8, 8, 3, 3), Stream(1, 8, 8, 3, 3)]
-MIDDLE = [Stream(18, 4, 4, 3, 4), Stream(3, 4, 4, 4, 5), Stream(3, 8, 8, 2, 2), Stream(1, 8, 8, 2, 2), Stream(1, 8, 8, 2, 2)]
+FINE = [Stream(STATIC, 8, 8, 2, 2), Stream(3, 8, 8, 3, 3), Stream(1, 8, 8, 3, 3)]
+MIDDLE = [Stream(18, 4, 4, 3, 4), Stream(3, 4, 4, 4, 5), Stream(3, 8, 8, 2, 2), Stream(1, 8, 8, 2, 2)]
 MIDDLE += [Stream(18, 4, 4, 1, 1), Stream(3, 4, 4, 2, 2)]
 
 
@@ -77,12 +77,10 @@
 def y_pieces(streams):
     offset = 0
     pieces = []
-    for depth in range(1, 1 + max(s.halo for s in streams)):
-        for index, s in enumerate(streams):
-            if depth <= s.halo:
-                planes = s.planes + 2 * s.extent(depth)
-                pieces.append((index, depth, offset))
-                offset += planes * s.count
+    for index, s in enumerate(streams):
+        for depth in range(1, 1 + s.halo):
+            pieces.append((index, depth, offset))
+            offset += (s.planes + 2 * s.extent(depth)) * s.count
     return pieces, offset
 
 
@@ -216,8 +214,14 @@
 Z_ROWS = 152
 
 
-def fine_x(stat, field, zlow, zhigh, up, down):
-    pack_x(FINE, [stat, field, zlow, zhigh], up, down)
+def both_sides(zlow, zhigh, side):
+    rows = pl.ds(0, 64)
+    side[...] = jnp.where(lanes_of(64) < 64, zhigh[rows, :], rolled(zlow[rows, :], 64, 1))
+
+
+def fine_x(stat, field, zlow, zhigh, side, up, down):
+    both_sides(zlow, zhigh, side)
+    pack_x(FINE, [stat, field, side], up, down)
 
 
 def share(zlow, zhigh, zown, shared, wide):
@@ -252,8 +256,8 @@
     shared[pl.ds(56, 8), :] = third
 
 
-def fine_y(stat, field, zlow, zhigh, low, high, up, down):
-    pack_y(FINE, [stat, field, zlow, zhigh], low, high, up, down)
+def fine_y(stat, field, side, low, high, up, down):
+    pack_y(FINE, [stat, field, side], low, high, up, down)
 
 
 def z_near(tiles):
@@ -279,12 +283,6 @@
     return out
 
 
-def both_sides(zlow, zhigh, sides):
-    for tile in range(sides.shape[0] // 16):
-        rows = pl.ds(tile * 16, 16)
-        sides[rows, :] = jnp.where(lanes_of(16) < 64, zhigh[rows, :], rolled(zlow[rows, :], 64, 1))
-
-
 def side_tile(sides, row, base, width):
     lane = lanes_of(16)
     packed = sides[pl.ds(row, 16), :]
@@ -307,10 +305,9 @@
     return coef
 
 
-def fine_sweeps(stat0, field0, zlow0, zhigh0, low, high, below, above, total, coef1, scale1, total1,
-                stat, sides, field2, middle, zup, zdown, field, zlow, zhigh, sums):
-    grow(FINE, [stat0, field0, zlow0, zhigh0], low, high, below, above, [stat, field, zlow, zhigh])
-    both_sides(zlow, zhigh, sides)
+def fine_sweeps(stat0, field0, side0, low, high, below, above, total, coef1, scale1, total1,
+                stat, sides, field2, middle, zup, zdown, field, sums):
+    grow(FINE, [stat0, field0, side0], low, high, below, above, [stat, field, sides])
     for e in range(3):
         coef = fine_coef(stat, sides, e)
         value = {}
@@ -356,31 +353,81 @@
         zdown[pl.ds(x * 8, 8), :] = down
 
 
-def middle_x(middle, field, zlow, zhigh, coef, right, side_coef, side_right, side_total, up, down):
+def middle_x(middle, field, zlow, zhigh, coef, right, side, side_coef, side_right, side_total, up, down, up_full, down_full):
     lane = lanes_of(128)
     low, high = zlow[pl.ds(64, 128), :], zhigh[pl.ds(64, 128), :]
     for group in range(3):
         own = middle[pl.ds(128 * group, 128), :]
         main = jnp.where((lane >= 64) & (lane < 68), rolled(high, 64 - WIDE * group, 1), own)
         main = jnp.where(lane >= 124, rolled(low, 128 - WIDE - WIDE * group, 1), main)
-        side = jnp.where(lane < 2, rolled(own, -62, 1), F32(0))
-        side = jnp.where((lane >= 2) & (lane < 2 + WIDE), rolled(high, 2 - WIDE * group, 1), side)
-        side = jnp.where((lane >= 64) & (lane < 64 + WIDE), rolled(low, 64 - WIDE * group, 1), side)
-        side = jnp.where((lane >= 106) & (lane < 108), rolled(own, 106, 1), side)
+        wide = jnp.where(lane < 2, rolled(own, -62, 1), F32(0))
+        wide = jnp.where((lane >= 2) & (lane < 2 + WIDE), rolled(high, 2 - WIDE * group, 1), wide)
+        wide = jnp.where((lane >= 64) & (lane < 64 + WIDE), rolled(low, 64 - WIDE * group, 1), wide)
+        wide = jnp.where((lane >= 106) & (lane < 108), rolled(own, 106, 1), wide)
         if group < 2:
             coef[pl.ds(128 * group, 128), :] = main
-            side_coef[pl.ds(128 * group, 128), :] = side
+            side_coef[pl.ds(128 * group, 128), :] = wide
         else:
             coef[pl.ds(256, 32), :] = main[:32]
-            side_coef[pl.ds(256, 32), :] = side[:32]
+            side_coef[pl.ds(256, 32), :] = wide[:32]
             right[...] = main[32:80]
-            side_right[...] = side[32:80]
-            side_total[...] = side[80:]
-    pack_x(MIDDLE, [coef, right, field, zlow, zhigh, side_coef, side_right], up, down)
-
-
-def middle_y(coef, right, field, zlow, zhigh, side_coef, side_right, low, high, up, down):
-    pack_y(MIDDLE, [coef, right, field, zlow, zhigh, side_coef, side_right], low, high, up, down)
+            side_right[...] = wide[32:80]
+            side_total[...] = wide[80:]
+    both_sides(zlow, zhigh, side)
+    pack_x(MIDDLE, [coef, right, field, side, side_coef, side_right], up_full, down_full)
+    squeeze(X_SQUEEZE, up_full, up)
+    squeeze(X_SQUEEZE, down_full, down)
+
+
+X_SQUEEZE = (216, 112, 16)
+Y_SQUEEZE = (432, 216, 32)
+
+
+def squeezed(total, plan):
+    return total - plan[0] + plan[1] + plan[2]
+
+
+def squeeze(plan, full, out):
+    number, half, size = plan
+    lane = lanes_of(half)
+    out[pl.ds(0, half), :] = jnp.where(lane < 64, full[pl.ds(0, half), :], rolled(full[pl.ds(half, half), :], 64, 1))
+    lane = lanes_of(size)
+    tail = jnp.zeros((size, LANES), F32)
+    for group in range(-(-number // size)):
+        value = full[pl.ds(group * size, size), :]
+        at = 8 * group
+        tail = jnp.where((lane >= at) & (lane < at + 4), rolled(value, at - 64, 1), tail)
+        tail = jnp.where((lane >= at + 4) & (lane < at + 8), rolled(value, at + 4 - 124, 1), tail)
+    out[pl.ds(half, size), :] = tail
+    rest = full.shape[0] - number
+    out[pl.ds(half + size, rest), :] = full[pl.ds(number, rest), :]
+
+
+def unsqueeze(plan, packed, full):
+    number, half, size = plan
+    lane = lanes_of(half)
+    both = packed[pl.ds(0, half), :]
+    full[pl.ds(0, half), :] = jnp.where(lane < 64, both, F32(0))
+    full[pl.ds(half, number - half), :] = jnp.where(lane < 64, rolled(both, 64, 1), F32(0))[: number - half]
+    for group in range(-(-number // size)):
+        at = 8 * group
+        rows = min(size, number - group * size)
+        tail = packed[pl.ds(half, rows), :]
+        lane = lanes_of(rows)
+        value = full[pl.ds(group * size, rows), :]
+        value = jnp.where((lane >= 64) & (lane < 68), rolled(tail, 64 - at, 1), value)
+        value = jnp.where(lane >= 124, rolled(tail, 124 - at - 4, 1), value)
+        full[pl.ds(group * size, rows), :] = value
+    rest = full.shape[0] - number
+    full[pl.ds(number, rest), :] = packed[pl.ds(half + size, rest), :]
+
+
+def middle_y(coef, right, field, side, side_coef, side_right, low_packed, high_packed, low, high, up, down, up_full, down_full):
+    unsqueeze(X_SQUEEZE, low_packed, low)
+    unsqueeze(X_SQUEEZE, high_packed, high)
+    pack_y(MIDDLE, [coef, right, field, side, side_coef, side_right], low, high, up_full, down_full)
+    squeeze(Y_SQUEEZE, up_full, up)
+    squeeze(Y_SQUEEZE, down_full, down)
 
 
 def middle_coef(coef, right, e):
@@ -392,15 +439,16 @@
     return get
 
 
-def middle_sweeps(coef0, right0, field0, zlow0, zhigh0, side_coef0, side_right0, low, high, below, above, total1, side_total,
-                  right, field, sides, error, packed, coef_far, coef, zlow, zhigh, side_coef, side_right, sums, side_sums,
-                  wide, left):
-    grow(MIDDLE, [coef0, right0, field0, zlow0, zhigh0, side_coef0, side_right0], low, high, below, above,
-         [coef, right, field, zlow, zhigh, side_coef, side_right])
+def middle_sweeps(coef0, right0, field0, side0, side_coef0, side_right0, low, high, below_packed, above_packed, total1, side_total,
+                  right, field, sides, error, packed, coef_far, coef, side_coef, side_right, sums, side_sums, wide,
+                  below, above, left):
+    unsqueeze(Y_SQUEEZE, below_packed, below)
+    unsqueeze(Y_SQUEEZE, above_packed, above)
+    grow(MIDDLE, [coef0, right0, field0, side0, side_coef0, side_right0], low, high, below, above,
+         [coef, right, field, sides, side_coef, side_right])
     inner = pl.ds(18 * 16, 8 * 18 * 16)
     keep = pltpu.make_async_copy(coef.at[inner, :], coef_far.at[inner, :], left.at[0])
     keep.start()
-    both_sides(zlow, zhigh, sides)
     for e in range(3):
 
         def side_get(x, k, t):
@@ -691,30 +739,34 @@
         prepare_whole, "prepare", [1344, 192, 192, Z_ROWS, Z_ROWS, 288, 48, 48], [inputs], scratch=[672, 336, 168, 88, 48]
     )
     zlow, zhigh = both_ways("gz", zup, zdown)
-    xup, xdown = call(fine_x, "fine_x", [x_rows(FINE)] * 2, [stat, field, zlow, zhigh])
+    side, xup, xdown = call(fine_x, "fine_x", [64, x_rows(FINE), x_rows(FINE)], [stat, field, zlow, zhigh])
     (shared,) = call(share, "share", [SHARED], [zlow, zhigh, zup], scratch=[96])
     shared = lax.all_gather(shared, ("gx", "gy"), tiled=True)
     xlow, xhigh = both_ways("gx", xup, xdown)
-    yup, ydown = call(fine_y, "fine_y", [y_rows(FINE)] * 2, [stat, field, zlow, zhigh, xlow, xhigh])
+    yup, ydown = call(fine_y, "fine_y", [y_rows(FINE)] * 2, [stat, field, side, xlow, xhigh])
     ylow, yhigh = both_ways("gy", yup, ydown)
     stat, sides0, field2, middle, zup, zdown = call(
         fine_sweeps, "fine_sweeps", [FINE[0].grown_rows(), FINE[2].grown_rows(), 192, 384, 192, 192],
-        [stat, field, zlow, zhigh, xlow, xhigh, ylow, yhigh, total, coef1, scale1, total1],
-        scratch=[s.grown_rows() for s in FINE[1:]] + [96],
+        [stat, field, side, xlow, xhigh, ylow, yhigh, total, coef1, scale1, total1],
+        scratch=[FINE[1].grown_rows(), 96],
     )
 
     zlow, zhigh = both_ways("gz", zup, zdown)
-    coef1, right1, side_coef, side_right, side_total, xup, xdown = call(
-        middle_x, "middle_x", [288, 48, 288, 48, 48, x_rows(MIDDLE), x_rows(MIDDLE)], [middle, field2, zlow, zhigh]
+    x_full, y_full = x_rows(MIDDLE), y_rows(MIDDLE)
+    x_sent, y_sent = squeezed(x_full, X_SQUEEZE), squeezed(y_full, Y_SQUEEZE)
+    coef1, right1, side, side_coef, side_right, side_total, xup, xdown = call(
+        middle_x, "middle_x", [288, 48, 64, 288, 48, 48, x_sent, x_sent], [middle, field2, zlow, zhigh], scratch=[x_full] * 2
     )
     xlow, xhigh = both_ways("gx", xup, xdown)
-    level1 = [coef1, right1, field2, zlow, zhigh, side_coef, side_right]
-    yup, ydown = call(middle_y, "middle_y", [y_rows(MIDDLE)] * 2, [*level1, xlow, xhigh])
+    level1 = [coef1, right1, field2, side, side_coef, side_right]
+    xlow, xhigh, yup, ydown = call(
+        middle_y, "middle_y", [x_full, x_full, y_sent, y_sent], [*level1, xlow, xhigh], scratch=[y_full] * 2
+    )
     ylow, yhigh = both_ways("gy", yup, ydown)
     right1, field2, sides2, error1, packed, coef1 = call(
         middle_sweeps, "middle_sweeps", [s.grown_rows() for s in MIDDLE[1:4]] + [480, gx * gy * 8],
-        [*level1, xlow, xhigh, ylow, yhigh, total1, side_total],
-        far_outs=[FAR], scratch=[MIDDLE[i].grown_rows() for i in (0, 3, 4, 5, 6)] + [32, 32, 16], copies=1,
+        [*level1, xlow, xhigh, ylow, yhigh, total1, side_total], far_outs=[FAR],
+        scratch=[MIDDLE[i].grown_rows() for i in (0, 4, 5)] + [32, 32, 16, y_full, y_full], copies=1,
     )
     packed = to_all(packed, gx * gy)
 

time: 133 us -> 130 us (0.977)
  waiting for transfers between devices: 61.6 us -> 56.2 us
    all_to_all x1, waiting for transfers between devices: 8.57 us -> 3.96 us  [to_all(): return lax.all_to_all(blocks, ('gx', 'gy'), 0, 0).reshape(value.shape)]
    all_gather x1, waiting for transfers between devices: 1.75 us -> 6.24 us  [per_device(): shared = lax.all_gather(shared, ('gx', 'gy'), tiled=True)]
    ppermute x6, waiting for transfers between devices: 25.7 us -> 21.4 us  [both_ways(): lax.ppermute(up, axis, pairs)]
    all_to_all x1, starting transfers between devices: 11.9 us -> 13.2 us  [to_all(): return lax.all_to_all(blocks, ('gx', 'gy'), 0, 0).reshape(value.shape)]
where the time goes in v5:
time: 130 us; the launch traced here: 129 us
  waiting for transfers between devices  56.2 us (43%)
  starting transfers between devices  39.6 us (30%)
  Pallas kernels  17.1 us (13%)
  between operations  13.6 us (10%)
  local copies, waits for them, and re-layouts  1.59 us (1%)
  other arithmetic  1.3 us (1%)
    ppermute x6, waiting for transfers between devices, both_ways(): lax.ppermute(down, axis, [(b, a) for a, b in pairs])  24.6 us
    ppermute x6, waiting for transfers between devices, both_ways(): lax.ppermute(up, axis, pairs)  21.4 us
    ppermute x6, starting transfers between devices, both_ways(): lax.ppermute(up, axis, pairs)  15.6 us
    all_to_all x1, starting transfers between devices, to_all(): return lax.all_to_all(blocks, ('gx', 'gy'), 0, 0).reshape(value.shape)  13.2 us
    pallas_call x9, Pallas kernels, call(): pl.pallas_call(body, name=name, out_shape=[jax.ShapeDtypeStruct((rows, LA...  11.4 us
    ppermute x6, starting transfers between devices, both_ways(): lax.ppermute(down, axis, [(b, a) for a, b in pairs])  10.7 us
    all_gather x1, waiting for transfers between devices, per_device(): shared = lax.all_gather(shared, ('gx', 'gy'), tiled=True)  6.24 us
    pallas_call x1, Pallas kernels, per_device(): pl.pallas_call(lambda *refs: finish(gx, gy, *refs), name='finish', out_sh...  5.62 us
  transfers between devices with their start and end apart: 14, of which 13 were waited for; matrix products, arithmetic and copies ran while one was open for 0% of the time, Pallas kernels for 7%

profile of v5, /device:TPU:2, one launch (start us, length us, event | category | flops | bytes accessed | tf_op | source)
XLA Modules:
  0.0 129.3 jit_solution(5743676447399304636)
XLA Ops:
  8.9 1.9 %collective-permute-start.1 = (f32[152,128]{1,0:T(8,128)S(1)}, f32[152,128]{1,0:T(8,128)S(1)}, u32[]{:S(2)}, u32[]{:S(2)}) collective-permute-start(f32[152,128]{1,0:T(8,128)S(1)} %get-tuple-element.43), channel_id=1, source_target_pairs={{1,0},{2,1},{3,2},{4,3},{5,4},{6,5},{7,6},{9,8},{10,9},{11,10},{12... | collective-permute-start | bytes 233480 | tf_op jit(solution)/shard_map/ppermute | solution.py:726
  10.8 2.4 %collective-permute-start = (f32[152,128]{1,0:T(8,128)S(1)}, f32[152,128]{1,0:T(8,128)S(1)}, u32[]{:S(2)}, u32[]{:S(2)}) collective-permute-start(f32[152,128]{1,0:T(8,128)S(1)} %get-tuple-element.42.zown), channel_id=1, source_target_pairs={{0,1},{1,2},{2,3},{3,4},{4,5},{5,6},{6,7},{8,9},{9,10},{10,11},{11... | collective-permute-start | bytes 233480 | tf_op jit(solution)/shard_map/ppermute | solution.py:726
  13.2 7.6 %collective-permute-done.zlow = f32[152,128]{1,0:T(8,128)S(1)} collective-permute-done((f32[152,128]{1,0:T(8,128)S(1)}, f32[152,128]{1,0:T(8,128)S(1)}, u32[]{:S(2)}, u32[]{:S(2)}) %collective-permute-start) | collective-permute-done | bytes 77856 | tf_op jit(solution)/shard_map/ppermute | solution.py:726
  24.3 2.1 %collective-permute-done.2.low = f32[432,128]{1,0:T(8,128)S(1)} collective-permute-done((f32[432,128]{1,0:T(8,128)S(1)}, f32[432,128]{1,0:T(8,128)S(1)}, u32[]{:S(2)}, u32[]{:S(2)}) %collective-permute-start.2) | collective-permute-done | bytes 221216 | tf_op jit(solution)/shard_map/ppermute | solution.py:726
  26.4 4.4 %collective-permute-done.3.high = f32[432,128]{1,0:T(8,128)S(1)} collective-permute-done((f32[432,128]{1,0:T(8,128)S(1)}, f32[432,128]{1,0:T(8,128)S(1)}, u32[]{:S(2)}, u32[]{:S(2)}) %collective-permute-start.3) | collective-permute-done | bytes 221216 | tf_op jit(solution)/shard_map/ppermute | solution.py:726
  30.9 2.6 %collective-permute-start.4 = (f32[504,128]{1,0:T(8,128)S(1)}, f32[504,128]{1,0:T(8,128)S(1)}, u32[]{:S(2)}, u32[]{:S(2)}) collective-permute-start(f32[504,128]{1,0:T(8,128)S(1)} %get-tuple-element.49), channel_id=1, source_target_pairs={{0,8},{8,16},{16,24},{24,32},{32,40},{40,48},{48,56},{1,9},{9,17},... | collective-permute-start | bytes 774152 | tf_op jit(solution)/shard_map/ppermute | solution.py:726
  34.8 2.5 %collective-permute-done.4.below = f32[504,128]{1,0:T(8,128)S(1)} collective-permute-done((f32[504,128]{1,0:T(8,128)S(1)}, f32[504,128]{1,0:T(8,128)S(1)}, u32[]{:S(2)}, u32[]{:S(2)}) %collective-permute-start.4) | collective-permute-done | bytes 258080 | tf_op jit(solution)/shard_map/ppermute | solution.py:726
  37.3 4.9 %collective-permute-done.5.above = f32[504,128]{1,0:T(8,128)S(1)} collective-permute-done((f32[504,128]{1,0:T(8,128)S(1)}, f32[504,128]{1,0:T(8,128)S(1)}, u32[]{:S(2)}, u32[]{:S(2)}) %collective-permute-start.5) | collective-permute-done | bytes 258080 | tf_op jit(solution)/shard_map/ppermute | solution.py:726
  42.3 2.1 %fine_sweeps.1 = (f32[4032,128]{1,0:T(8,128)S(1)}, f32[224,128]{1,0:T(8,128)S(1)}, f32[192,128]{1,0:T(8,128)S(1)}, f32[384,128]{1,0:T(8,128)S(1)}, f32[192,128]{1,0:T(8,128)S(1)}, /*index=5*/f32[192,128]{1,0:T(8,128)S(1)}) custom-call(f32[1344,128]{1,0:T(8,128)S(1)} %get-tuple-element.44.stat.stat0, f32[192,128]{1,0:T(8,128)S(1)} %get-tuple-element.45.field.field0, ...), custom_call_target="tpu_custom_call" | custom-call | tf_op jit(solution)/shard_map/fine_sweeps/pallas_call | solution.py:43
  44.3 1.9 %collective-permute-start.6 = (f32[192,128]{1,0:T(8,128)S(1)}, f32[192,128]{1,0:T(8,128)S(1)}, u32[]{:S(2)}, u32[]{:S(2)}) collective-permute-start(f32[192,128]{1,0:T(8,128)S(1)} %get-tuple-element.57), channel_id=1, source_target_pairs={{0,1},{1,2},{2,3},{3,4},{4,5},{5,6},{6,7},{8,9},{9,10},{10,11},{11... | collective-permute-start | bytes 294920 | tf_op jit(solution)/shard_map/ppermute | solution.py:726
  46.2 3.6 %collective-permute-start.7 = (f32[192,128]{1,0:T(8,128)S(1)}, f32[192,128]{1,0:T(8,128)S(1)}, u32[]{:S(2)}, u32[]{:S(2)}) collective-permute-start(f32[192,128]{1,0:T(8,128)S(1)} %get-tuple-element.58), channel_id=1, source_target_pairs={{1,0},{2,1},{3,2},{4,3},{5,4},{6,5},{7,6},{9,8},{10,9},{11,10},{12... | collective-permute-start | bytes 294920 | tf_op jit(solution)/shard_map/ppermute | solution.py:726
  50.3 1.8 %collective-permute-done.7.zhigh = f32[192,128]{1,0:T(8,128)S(1)} collective-permute-done((f32[192,128]{1,0:T(8,128)S(1)}, f32[192,128]{1,0:T(8,128)S(1)}, u32[]{:S(2)}, u32[]{:S(2)}) %collective-permute-start.7) | collective-permute-done | bytes 98336 | tf_op jit(solution)/shard_map/ppermute | solution.py:726
  52.6 3.5 %collective-permute-start.8 = (f32[336,128]{1,0:T(8,128)S(1)}, f32[336,128]{1,0:T(8,128)S(1)}, u32[]{:S(2)}, u32[]{:S(2)}) collective-permute-start(f32[336,128]{1,0:T(8,128)S(1)} %get-tuple-element.64), channel_id=1, source_target_pairs={{0,64},{64,128},{128,192},{192,256},{256,320},{320,384},{384,448},... | collective-permute-start | bytes 516104 | tf_op jit(solution)/shard_map/ppermute | solution.py:726
  57.4 2.6 %collective-permute-done.8.low_packed = f32[336,128]{1,0:T(8,128)S(1)} collective-permute-done((f32[336,128]{1,0:T(8,128)S(1)}, f32[336,128]{1,0:T(8,128)S(1)}, u32[]{:S(2)}, u32[]{:S(2)}) %collective-permute-start.8) | collective-permute-done | bytes 172064 | tf_op jit(solution)/shard_map/ppermute | solution.py:726
  59.9 5.6 %collective-permute-done.9.high_packed = f32[336,128]{1,0:T(8,128)S(1)} collective-permute-done((f32[336,128]{1,0:T(8,128)S(1)}, f32[336,128]{1,0:T(8,128)S(1)}, u32[]{:S(2)}, u32[]{:S(2)}) %collective-permute-start.9) | collective-permute-done | bytes 172064 | tf_op jit(solution)/shard_map/ppermute | solution.py:726
  66.1 4.0 %collective-permute-start.10 = (f32[536,128]{1,0:T(8,128)S(1)}, f32[536,128]{1,0:T(8,128)S(1)}, u32[]{:S(2)}, u32[]{:S(2)}) collective-permute-start(f32[536,128]{1,0:T(8,128)S(1)} %get-tuple-element.68), channel_id=1, source_target_pairs={{0,8},{8,16},{16,24},{24,32},{32,40},{40,48},{48,56},{1,9},{9,17},... | collective-permute-start | bytes 823304 | tf_op jit(solution)/shard_map/ppermute | solution.py:726
  71.4 6.3 %collective-permute-done.10.below_packed = f32[536,128]{1,0:T(8,128)S(1)} collective-permute-done((f32[536,128]{1,0:T(8,128)S(1)}, f32[536,128]{1,0:T(8,128)S(1)}, u32[]{:S(2)}, u32[]{:S(2)}) %collective-permute-start.10) | collective-permute-done | bytes 274464 | tf_op jit(solution)/shard_map/ppermute | solution.py:726
  77.7 7.8 %collective-permute-done.11.above_packed = f32[536,128]{1,0:T(8,128)S(1)} collective-permute-done((f32[536,128]{1,0:T(8,128)S(1)}, f32[536,128]{1,0:T(8,128)S(1)}, u32[]{:S(2)}, u32[]{:S(2)}) %collective-permute-start.11) | collective-permute-done | bytes 274464 | tf_op jit(solution)/shard_map/ppermute | solution.py:726
  85.5 3.0 %middle_sweeps.1 = (f32[576,128]{1,0:T(8,128)S(1)}, f32[576,128]{1,0:T(8,128)S(1)}, f32[192,128]{1,0:T(8,128)S(1)}, f32[480,128]{1,0:T(8,128)S(1)}, f32[512,128]{1,0:T(8,128)}, /*index=5*/f32[49152,128]{1,0:T(8,128)}) custom-call(f32[288,128]{1,0:T(8,128)S(1)} %get-tuple-element.59.coef.coef0, f32[48,128]{1,0:T(8,128)S(1)} %get-tuple-element.60.right.right0, ...), custom_call_target="tpu_custom_call" | custom-call | tf_op jit(solution)/shard_map/middle_sweeps/pallas_call | solution.py:43
  88.4 13.2 %all-to-all-start = ((f32[64,8,128]{2,1,0:T(8,128)}), f32[64,8,128]{2,1,0:T(8,128)S(1)}, u32[]{:S(2)}, u32[]{:S(2)}) async-start(f32[64,8,128]{2,1,0:T(8,128)} %bitcast), calls=%async_computation | async-start | bytes 524288 | tf_op jit(solution)/shard_map/all_to_all | solution.py:731
  101.7 6.2 %all-gather.2.cloned.1.call-done.refs_0_ = f32[4096,128]{1,0:T(8,128)} async-done(((f32[64,128]{1,0:T(8,128)}), f32[4096,128]{1,0:T(8,128)}) %all-gather.2.cloned.1.call-update) | async-done | bytes 2097168 | tf_op jit(solution)/shard_map/all_gather | solution.py:744
  109.5 3.3 %coarse_coefs.1.refs_0_ = f32[49152,128]{1,0:T(8,128)} custom-call(f32[4096,128]{1,0:T(8,128)S(1)} %copy-done), custom_call_target="tpu_custom_call" | custom-call | tf_op jit(solution)/shard_map/coarse_coefs/pallas_call | solution.py:43
  112.8 4.0 %all-to-all-done = f32[64,8,128]{2,1,0:T(8,128)S(1)} async-done(((f32[64,8,128]{2,1,0:T(8,128)}), f32[64,8,128]{2,1,0:T(8,128)S(1)}, u32[]{:S(2)}, u32[]{:S(2)}) %all-to-all-start) | async-done | bytes 262176 | tf_op jit(solution)/shard_map/all_to_all | solution.py:731
  116.8 5.6 %finish.1 = f32[3,8,8,128]{3,2,1,0:T(8,128)} custom-call(f32[49152,128]{1,0:T(8,128)} %coarse_coefs.1.refs_0_, f32[49152,128]{1,0:T(8,128)} %get-tuple-element.71.refs_1_, f32[512,128]{1,0:T(8,128)S(1)} %bitcast.2, f32[480,128]{1,0:T(8,128)S(1)} %get-tuple-element.73.refs_3_, f32[576,128]{1,0:T(8,128)S(1)} %get-tuple-element.74.refs_4_, ...), custom_call_target="tpu_custom_call" | custom-call | tf_op jit(solution)/shard_map/finish/pallas_call | solution.py:782
  (18 shorter events, 12.8 us)
Async XLA Ops:
  6.5 101.4 %all-gather.2.cloned.1.call-start = ((), (), s32[]{:S(2)}) async-start(), calls=%async_computation.1 | async-start | bytes 2129920 | tf_op jit(solution)/shard_map/all_gather | solution.py:744
  8.9 4.3 %collective-permute-start.1 = (f32[152,128]{1,0:T(8,128)S(1)}, f32[152,128]{1,0:T(8,128)S(1)}, u32[]{:S(2)}, u32[]{:S(2)}) collective-permute-start(f32[152,128]{1,0:T(8,128)S(1)} %get-tuple-element.43), channel_id=1, source_target_pairs={{1,0},{2,1},{3,2},{4,3},{5,4},{6,5},{7,6},{9,8},{10,9},{11,10},{12... | collective-permute-start | bytes 233480 | tf_op jit(solution)/shard_map/ppermute | solution.py:726
  10.8 10.0 %collective-permute-start = (f32[152,128]{1,0:T(8,128)S(1)}, f32[152,128]{1,0:T(8,128)S(1)}, u32[]{:S(2)}, u32[]{:S(2)}) collective-permute-start(f32[152,128]{1,0:T(8,128)S(1)} %get-tuple-element.42.zown), channel_id=1, source_target_pairs={{0,1},{1,2},{2,3},{3,4},{4,5},{5,6},{6,7},{8,9},{9,10},{10,11},{11... | collective-permute-start | bytes 233480 | tf_op jit(solution)/shard_map/ppermute | solution.py:726
  21.7 4.7 %collective-permute-start.2 = (f32[432,128]{1,0:T(8,128)S(1)}, f32[432,128]{1,0:T(8,128)S(1)}, u32[]{:S(2)}, u32[]{:S(2)}) collective-permute-start(f32[432,128]{1,0:T(8,128)S(1)} %get-tuple-element.47), channel_id=1, source_target_pairs={{0,64},{64,128},{128,192},{192,256},{256,320},{320,384},{384,448},... | collective-permute-start | bytes 663560 | tf_op jit(solution)/shard_map/ppermute | solution.py:726
  23.0 7.8 %collective-permute-start.3 = (f32[432,128]{1,0:T(8,128)S(1)}, f32[432,128]{1,0:T(8,128)S(1)}, u32[]{:S(2)}, u32[]{:S(2)}) collective-permute-start(f32[432,128]{1,0:T(8,128)S(1)} %get-tuple-element.48), channel_id=1, source_target_pairs={{64,0},{128,64},{192,128},{256,192},{320,256},{384,320},{448,384},... | collective-permute-start | bytes 663560 | tf_op jit(solution)/shard_map/ppermute | solution.py:726
  30.9 6.4 %collective-permute-start.4 = (f32[504,128]{1,0:T(8,128)S(1)}, f32[504,128]{1,0:T(8,128)S(1)}, u32[]{:S(2)}, u32[]{:S(2)}) collective-permute-start(f32[504,128]{1,0:T(8,128)S(1)} %get-tuple-element.49), channel_id=1, source_target_pairs={{0,8},{8,16},{16,24},{24,32},{32,40},{40,48},{48,56},{1,9},{9,17},... | collective-permute-start | bytes 774152 | tf_op jit(solution)/shard_map/ppermute | solution.py:726
  33.5 8.7 %collective-permute-start.5 = (f32[504,128]{1,0:T(8,128)S(1)}, f32[504,128]{1,0:T(8,128)S(1)}, u32[]{:S(2)}, u32[]{:S(2)}) collective-permute-start(f32[504,128]{1,0:T(8,128)S(1)} %get-tuple-element.50), channel_id=1, source_target_pairs={{8,0},{16,8},{24,16},{32,24},{40,32},{48,40},{56,48},{9,1},{17,9},... | collective-permute-start | bytes 774152 | tf_op jit(solution)/shard_map/ppermute | solution.py:726
  44.3 5.9 %collective-permute-start.6 = (f32[192,128]{1,0:T(8,128)S(1)}, f32[192,128]{1,0:T(8,128)S(1)}, u32[]{:S(2)}, u32[]{:S(2)}) collective-permute-start(f32[192,128]{1,0:T(8,128)S(1)} %get-tuple-element.57), channel_id=1, source_target_pairs={{0,1},{1,2},{2,3},{3,4},{4,5},{5,6},{6,7},{8,9},{9,10},{10,11},{11... | collective-permute-start | bytes 294920 | tf_op jit(solution)/shard_map/ppermute | solution.py:726
  46.2 5.8 %collective-permute-start.7 = (f32[192,128]{1,0:T(8,128)S(1)}, f32[192,128]{1,0:T(8,128)S(1)}, u32[]{:S(2)}, u32[]{:S(2)}) collective-permute-start(f32[192,128]{1,0:T(8,128)S(1)} %get-tuple-element.58), channel_id=1, source_target_pairs={{1,0},{2,1},{3,2},{4,3},{5,4},{6,5},{7,6},{9,8},{10,9},{11,10},{12... | collective-permute-start | bytes 294920 | tf_op jit(solution)/shard_map/ppermute | solution.py:726
  52.6 7.4 %collective-permute-start.8 = (f32[336,128]{1,0:T(8,128)S(1)}, f32[336,128]{1,0:T(8,128)S(1)}, u32[]{:S(2)}, u32[]{:S(2)}) collective-permute-start(f32[336,128]{1,0:T(8,128)S(1)} %get-tuple-element.64), channel_id=1, source_target_pairs={{0,64},{64,128},{128,192},{192,256},{256,320},{320,384},{384,448},... | collective-permute-start | bytes 516104 | tf_op jit(solution)/shard_map/ppermute | solution.py:726
  56.1 9.4 %collective-permute-start.9 = (f32[336,128]{1,0:T(8,128)S(1)}, f32[336,128]{1,0:T(8,128)S(1)}, u32[]{:S(2)}, u32[]{:S(2)}) collective-permute-start(f32[336,128]{1,0:T(8,128)S(1)} %get-tuple-element.65), channel_id=1, source_target_pairs={{64,0},{128,64},{192,128},{256,192},{320,256},{384,320},{448,384},... | collective-permute-start | bytes 516104 | tf_op jit(solution)/shard_map/ppermute | solution.py:726
  66.1 11.6 %collective-permute-start.10 = (f32[536,128]{1,0:T(8,128)S(1)}, f32[536,128]{1,0:T(8,128)S(1)}, u32[]{:S(2)}, u32[]{:S(2)}) collective-permute-start(f32[536,128]{1,0:T(8,128)S(1)} %get-tuple-element.68), channel_id=1, source_target_pairs={{0,8},{8,16},{16,24},{24,32},{32,40},{40,48},{48,56},{1,9},{9,17},... | collective-permute-start | bytes 823304 | tf_op jit(solution)/shard_map/ppermute | solution.py:726
  70.1 15.4 %collective-permute-start.11 = (f32[536,128]{1,0:T(8,128)S(1)}, f32[536,128]{1,0:T(8,128)S(1)}, u32[]{:S(2)}, u32[]{:S(2)}) collective-permute-start(f32[536,128]{1,0:T(8,128)S(1)} %get-tuple-element.69), channel_id=1, source_target_pairs={{8,0},{16,8},{24,16},{32,24},{40,32},{48,40},{56,48},{9,1},{17,9},... | collective-permute-start | bytes 823304 | tf_op jit(solution)/shard_map/ppermute | solution.py:726
  88.4 28.3 %all-to-all-start = ((f32[64,8,128]{2,1,0:T(8,128)}), f32[64,8,128]{2,1,0:T(8,128)S(1)}, u32[]{:S(2)}, u32[]{:S(2)}) async-start(f32[64,8,128]{2,1,0:T(8,128)} %bitcast), calls=%async_computation | async-start | bytes 524288 | tf_op jit(solution)/shard_map/all_to_all | solution.py:731
  107.9 1.6 %copy-start = (f32[4096,128]{1,0:T(8,128)S(1)}, f32[4096,128]{1,0:T(8,128)}, u32[]{:S(2)}) copy-start(f32[4096,128]{1,0:T(8,128)} %all-gather.2.cloned.1.call-done.refs_0_) | copy-start | bytes 6291460
Sparse Core Ops, SparseCore 0:
  21.8 86.0 all-gather.1

commit v6 on v5

--- a/solution.py
+++ b/solution.py
@@ -502,30 +502,49 @@
 
 def coarse_parts(gx, gy):
     each = 4 * gx * gy
-    sizes = [3 * each, 3 * each, 6 * each, 6 * each, 6 * each, 21 * gx * gy]
+    sizes = [3 * each, 3 * each, 6 * each, 6 * each, 6 * each, 7 * gx * gy]
     return [(sum(sizes[:i]), size) for i, size in enumerate(sizes)]
 
 
 def coarse_coefs(gx, gy, shared, table_far, table, left):
-    (scale_at, _), (total_at, _), (coef_at, _), _, _, (coef3_at, size3) = coarse_parts(gx, gy)
+    parts = coarse_parts(gx, gy)
+    (scale_at, _), (total_at, _), (coef_at, _), _, _, (coef3_at, _) = parts
     lane = lanes_of(gy)
     used = lane < 72
+    keeps = [
+        pltpu.make_async_copy(table.at[pl.ds(first, size), :], table_far.at[pl.ds(first, size), :], left.at[i])
+        for i, (first, size) in enumerate(parts)
+    ]
+
+    def settle(w, d):
+        tot = d + (((w[0] + w[1]) + (w[2] + w[3])) + (w[4] + w[5]))
+        tot = jnp.where(tot > 0, tot, F32(1))
+        return tot, 0.8 / tot
+
+    def rows(g, r):
+        return shared[pl.ds(g * gy * SHARED + r, gy, SHARED), :]
+
     for g in range(gx):
-
-        def rows(r):
-            return shared[pl.ds(g * gy * SHARED + r, gy, SHARED), :]
-
-        tails = [rows(48 + r) for r in range(8)]
-        thirds = [rows(56 + r) for r in range(8)]
-
-        def settle(w, d):
-            tot = d + (((w[0] + w[1]) + (w[2] + w[3])) + (w[4] + w[5]))
-            tot = jnp.where(tot > 0, tot, F32(1))
-            return tot, 0.8 / tot
-
+        thirds = [rows(g, 56 + r) for r in range(8)]
+        mixed = [jnp.zeros((gy, LANES), F32)] * 7
         for e in range(3):
+
+            def mean3(a):
+                return rolled(thirds[a % 8], 36 * e - 36 * (a // 8), 1)
+
+            w = [mean3(6 * e + k) * 0.015625 for k in range(6)]
+            tot, inverse = settle(w, mean3(18 + e))
+            inside = (lane >= 36 * e) & (lane < 36 * e + 36)
+            found = [w[k] * inverse for k in range(6)] + [inverse]
+            mixed = [jnp.where(inside, new, old) for new, old in zip(found, mixed)]
+        for k in range(7):
+            table[pl.ds(coef3_at + (g * 7 + k) * gy, gy), :] = mixed[k]
+    keeps[5].start()
+    for e in range(3):
+        for g in range(gx):
+            tails = [rows(g, 48 + r) for r in range(8)]
             for j in range(2):
-                pairs = {a: rows(a * 2 + j) for a in [6 * e + k for k in range(6)] + [18 + e]}
+                pairs = {a: rows(g, a * 2 + j) for a in [6 * e + k for k in range(6)] + [18 + e]}
                 for i in range(2):
 
                     def mean(a):
@@ -541,18 +560,11 @@
                         table[pl.ds(coef_at + (base * 6 + k) * gy, gy), :] = w[k] * inverse
                     table[pl.ds(scale_at + base * gy, gy), :] = inverse
                     table[pl.ds(total_at + base * gy, gy), :] = tot * 1.25
-
-            def mean3(a):
-                return jnp.where(lane < 36, rolled(thirds[a % 8], -36 * (a // 8), 1), F32(0))
-
-            w = [mean3(6 * e + k) * 0.015625 for k in range(6)]
-            tot, inverse = settle(w, mean3(18 + e))
-            for k in range(6):
-                table[pl.ds(coef3_at + ((g * 3 + e) * 7 + k) * gy, gy), :] = w[k] * inverse
-            table[pl.ds(coef3_at + ((g * 3 + e) * 7 + 6) * gy, gy), :] = inverse
-    keep = pltpu.make_async_copy(table, table_far.at[pl.ds(0, coef3_at + size3), :], left.at[0])
-    keep.start()
-    keep.wait()
+        keeps[2 + e].start()
+    keeps[0].start()
+    keeps[1].start()
+    for keep in keeps:
+        keep.wait()
 
 
 def coarse_levels(gx, gy, me_x, me_y, packed, table, arrivals, right2, error2, rows6):
@@ -599,10 +611,10 @@
         return out
 
     cells = [(x, j) for x in range(planes) for j in range(2)]
-    halve = pair_matrix(0.125)
-    fine = lax.broadcasted_iota(jnp.int32, (LANES, LANES), 1)
-    coarse = lax.broadcasted_iota(jnp.int32, (LANES, LANES), 0)
-    double = jnp.where((fine >> 1) == coarse, F32(1), F32(0))
+    source = lax.broadcasted_iota(jnp.int32, (LANES, LANES), 0)
+    target = lax.broadcasted_iota(jnp.int32, (LANES, LANES), 1)
+    halves = [jnp.where((source < 72) & ((source >> 1) + 36 * e == target), F32(0.125), F32(0)) for e in range(3)]
+    doubles = [jnp.where((target < 72) & ((target >> 1) + 36 * e == source), F32(1), F32(0)) for e in range(3)]
     before, sums = [], []
     for e in range(3):
         if e == 0:
@@ -619,35 +631,33 @@
                 (resid[2 * g, 0] + resid[2 * g, 1]) + (resid[2 * g + 1, 0] + resid[2 * g + 1, 1])
             )
     arrivals[5].wait()
-    right3 = exact_dot(jnp.concatenate(sums, axis=0), halve)
-    found = []
-    for e in range(3):
-
-        def coef_of(g, k):
-            return table[pl.ds(coef3_at + ((g * 3 + e) * 7 + k) * gy, gy), :]
-
-        right = [right3[(e * gx + g) * gy : (e * gx + g + 1) * gy] * coef_of(g, 6) for g in range(gx)]
-        value = right
-        for step in range(7):
-            new = []
-            for g in range(gx):
-                v = value[g]
-                out = 0.2 * v + right[g]
-                if g + 1 < gx:
-                    out = out + coef_of(g, 0) * value[g + 1]
-                if g > 0:
-                    out = out + coef_of(g, 1) * value[g - 1]
-                out = out + coef_of(g, 2) * jnp.where(last_row, zero, rolled(v, -1, 0))
-                out = out + coef_of(g, 3) * jnp.where(first_row, zero, rolled(v, 1, 0))
-                out = out + coef_of(g, 4) * rolled(v, -1, 1)
-                out = out + coef_of(g, 5) * rolled(v, 1, 1)
-                new.append(out)
-            value = new
-        found.extend(value)
-    refined = exact_dot(jnp.concatenate(found, axis=0), double)
+    right3 = sum(exact_dot(jnp.concatenate(sums[e * gx : (e + 1) * gx], axis=0), halves[e]) for e in range(3))
+
+    def coef_of(g, k):
+        return table[pl.ds(coef3_at + (g * 7 + k) * gy, gy), :]
+
+    right = [right3[g * gy : (g + 1) * gy] * coef_of(g, 6) for g in range(gx)]
+    value = right
+    for step in range(7):
+        new = []
+        for g in range(gx):
+            v = value[g]
+            out = 0.2 * v + right[g]
+            if g + 1 < gx:
+                out = out + coef_of(g, 0) * value[g + 1]
+            if g > 0:
+                out = out + coef_of(g, 1) * value[g - 1]
+            out = out + coef_of(g, 2) * jnp.where(last_row, zero, rolled(v, -1, 0))
+            out = out + coef_of(g, 3) * jnp.where(first_row, zero, rolled(v, 1, 0))
+            out = out + coef_of(g, 4) * rolled(v, -1, 1)
+            out = out + coef_of(g, 5) * rolled(v, 1, 1)
+            new.append(out)
+        value = new
+    found = jnp.concatenate(value, axis=0)
+    refined = [exact_dot(found, doubles[e]) for e in range(3)]
     for e in range(3):
         value = {
-            (x, j): before[e][x, j] + refined[(e * gx + x // 2) * gy : (e * gx + x // 2 + 1) * gy] for x, j in cells
+            (x, j): before[e][x, j] + refined[e][(x // 2) * gy : (x // 2 + 1) * gy] for x, j in cells
         }
         for step in range(2):
             value = {(x, j): sweep2(value, x, e, j) for x, j in cells}
@@ -772,7 +782,7 @@
 
     rows = sum(coarse_parts(gx, gy)[-1])
     (table,) = call(
-        lambda *refs: coarse_coefs(gx, gy, *refs), "coarse_coefs", [], [shared], far_outs=[FAR], scratch=[rows], copies=1
+        lambda *refs: coarse_coefs(gx, gy, *refs), "coarse_coefs", [], [shared], far_outs=[FAR], scratch=[rows], copies=6
     )
 
     vmem = pl.BlockSpec(memory_space=pltpu.VMEM)

time: 130 us -> 130 us (level)
  no operation moved by 1% of the time
where the time goes in v6:
time: 130 us; the launch traced here: 129 us
  waiting for transfers between devices  56.5 us (43%)
  starting transfers between devices  39.6 us (30%)
  Pallas kernels  16.8 us (13%)
  between operations  13.6 us (10%)
  local copies, waits for them, and re-layouts  1.59 us (1%)
  other arithmetic  1.3 us (1%)
    ppermute x6, waiting for transfers between devices, both_ways(): lax.ppermute(down, axis, [(b, a) for a, b in pairs])  24.6 us
    ppermute x6, waiting for transfers between devices, both_ways(): lax.ppermute(up, axis, pairs)  21.4 us
    ppermute x6, starting transfers between devices, both_ways(): lax.ppermute(up, axis, pairs)  15.6 us
    all_to_all x1, starting transfers between devices, to_all(): return lax.all_to_all(blocks, ('gx', 'gy'), 0, 0).reshape(value.shape)  13.2 us
    pallas_call x9, Pallas kernels, call(): pl.pallas_call(body, name=name, out_shape=[jax.ShapeDtypeStruct((rows, LA...  11.1 us
    ppermute x6, starting transfers between devices, both_ways(): lax.ppermute(down, axis, [(b, a) for a, b in pairs])  10.7 us
    all_gather x1, waiting for transfers between devices, per_device(): shared = lax.all_gather(shared, ('gx', 'gy'), tiled=True)  6.24 us
    pallas_call x1, Pallas kernels, per_device(): pl.pallas_call(lambda *refs: finish(gx, gy, *refs), name='finish', out_sh...  5.67 us
  transfers between devices with their start and end apart: 14, of which 13 were waited for; matrix products, arithmetic and copies ran while one was open for 0% of the time, Pallas kernels for 7%

profile of v6, /device:TPU:2, one launch (start us, length us, event | category | flops | bytes accessed | tf_op | source)
XLA Modules:
  0.0 129.3 jit_solution(3355681032430823874)
XLA Ops:
  8.9 1.9 %collective-permute-start.1 = (f32[152,128]{1,0:T(8,128)S(1)}, f32[152,128]{1,0:T(8,128)S(1)}, u32[]{:S(2)}, u32[]{:S(2)}) collective-permute-start(f32[152,128]{1,0:T(8,128)S(1)} %get-tuple-element.43), channel_id=1, source_target_pairs={{1,0},{2,1},{3,2},{4,3},{5,4},{6,5},{7,6},{9,8},{10,9},{11,10},{12... | collective-permute-start | bytes 233480 | tf_op jit(solution)/shard_map/ppermute | solution.py:736
  10.8 2.4 %collective-permute-start = (f32[152,128]{1,0:T(8,128)S(1)}, f32[152,128]{1,0:T(8,128)S(1)}, u32[]{:S(2)}, u32[]{:S(2)}) collective-permute-start(f32[152,128]{1,0:T(8,128)S(1)} %get-tuple-element.42.zown), channel_id=1, source_target_pairs={{0,1},{1,2},{2,3},{3,4},{4,5},{5,6},{6,7},{8,9},{9,10},{10,11},{11... | collective-permute-start | bytes 233480 | tf_op jit(solution)/shard_map/ppermute | solution.py:736
  13.2 7.6 %collective-permute-done.zlow = f32[152,128]{1,0:T(8,128)S(1)} collective-permute-done((f32[152,128]{1,0:T(8,128)S(1)}, f32[152,128]{1,0:T(8,128)S(1)}, u32[]{:S(2)}, u32[]{:S(2)}) %collective-permute-start) | collective-permute-done | bytes 77856 | tf_op jit(solution)/shard_map/ppermute | solution.py:736
  24.3 2.1 %collective-permute-done.2.low = f32[432,128]{1,0:T(8,128)S(1)} collective-permute-done((f32[432,128]{1,0:T(8,128)S(1)}, f32[432,128]{1,0:T(8,128)S(1)}, u32[]{:S(2)}, u32[]{:S(2)}) %collective-permute-start.2) | collective-permute-done | bytes 221216 | tf_op jit(solution)/shard_map/ppermute | solution.py:736
  26.4 4.4 %collective-permute-done.3.high = f32[432,128]{1,0:T(8,128)S(1)} collective-permute-done((f32[432,128]{1,0:T(8,128)S(1)}, f32[432,128]{1,0:T(8,128)S(1)}, u32[]{:S(2)}, u32[]{:S(2)}) %collective-permute-start.3) | collective-permute-done | bytes 221216 | tf_op jit(solution)/shard_map/ppermute | solution.py:736
  30.9 2.6 %collective-permute-start.4 = (f32[504,128]{1,0:T(8,128)S(1)}, f32[504,128]{1,0:T(8,128)S(1)}, u32[]{:S(2)}, u32[]{:S(2)}) collective-permute-start(f32[504,128]{1,0:T(8,128)S(1)} %get-tuple-element.49), channel_id=1, source_target_pairs={{0,8},{8,16},{16,24},{24,32},{32,40},{40,48},{48,56},{1,9},{9,17},... | collective-permute-start | bytes 774152 | tf_op jit(solution)/shard_map/ppermute | solution.py:736
  34.8 2.5 %collective-permute-done.4.below = f32[504,128]{1,0:T(8,128)S(1)} collective-permute-done((f32[504,128]{1,0:T(8,128)S(1)}, f32[504,128]{1,0:T(8,128)S(1)}, u32[]{:S(2)}, u32[]{:S(2)}) %collective-permute-start.4) | collective-permute-done | bytes 258080 | tf_op jit(solution)/shard_map/ppermute | solution.py:736
  37.3 4.9 %collective-permute-done.5.above = f32[504,128]{1,0:T(8,128)S(1)} collective-permute-done((f32[504,128]{1,0:T(8,128)S(1)}, f32[504,128]{1,0:T(8,128)S(1)}, u32[]{:S(2)}, u32[]{:S(2)}) %collective-permute-start.5) | collective-permute-done | bytes 258080 | tf_op jit(solution)/shard_map/ppermute | solution.py:736
  42.3 2.1 %fine_sweeps.1 = (f32[4032,128]{1,0:T(8,128)S(1)}, f32[224,128]{1,0:T(8,128)S(1)}, f32[192,128]{1,0:T(8,128)S(1)}, f32[384,128]{1,0:T(8,128)S(1)}, f32[192,128]{1,0:T(8,128)S(1)}, /*index=5*/f32[192,128]{1,0:T(8,128)S(1)}) custom-call(f32[1344,128]{1,0:T(8,128)S(1)} %get-tuple-element.44.stat.stat0, f32[192,128]{1,0:T(8,128)S(1)} %get-tuple-element.45.field.field0, ...), custom_call_target="tpu_custom_call" | custom-call | tf_op jit(solution)/shard_map/fine_sweeps/pallas_call | solution.py:43
  44.3 1.9 %collective-permute-start.6 = (f32[192,128]{1,0:T(8,128)S(1)}, f32[192,128]{1,0:T(8,128)S(1)}, u32[]{:S(2)}, u32[]{:S(2)}) collective-permute-start(f32[192,128]{1,0:T(8,128)S(1)} %get-tuple-element.57), channel_id=1, source_target_pairs={{0,1},{1,2},{2,3},{3,4},{4,5},{5,6},{6,7},{8,9},{9,10},{10,11},{11... | collective-permute-start | bytes 294920 | tf_op jit(solution)/shard_map/ppermute | solution.py:736
  46.2 3.6 %collective-permute-start.7 = (f32[192,128]{1,0:T(8,128)S(1)}, f32[192,128]{1,0:T(8,128)S(1)}, u32[]{:S(2)}, u32[]{:S(2)}) collective-permute-start(f32[192,128]{1,0:T(8,128)S(1)} %get-tuple-element.58), channel_id=1, source_target_pairs={{1,0},{2,1},{3,2},{4,3},{5,4},{6,5},{7,6},{9,8},{10,9},{11,10},{12... | collective-permute-start | bytes 294920 | tf_op jit(solution)/shard_map/ppermute | solution.py:736
  50.3 1.8 %collective-permute-done.7.zhigh = f32[192,128]{1,0:T(8,128)S(1)} collective-permute-done((f32[192,128]{1,0:T(8,128)S(1)}, f32[192,128]{1,0:T(8,128)S(1)}, u32[]{:S(2)}, u32[]{:S(2)}) %collective-permute-start.7) | collective-permute-done | bytes 98336 | tf_op jit(solution)/shard_map/ppermute | solution.py:736
  52.6 3.5 %collective-permute-start.8 = (f32[336,128]{1,0:T(8,128)S(1)}, f32[336,128]{1,0:T(8,128)S(1)}, u32[]{:S(2)}, u32[]{:S(2)}) collective-permute-start(f32[336,128]{1,0:T(8,128)S(1)} %get-tuple-element.64), channel_id=1, source_target_pairs={{0,64},{64,128},{128,192},{192,256},{256,320},{320,384},{384,448},... | collective-permute-start | bytes 516104 | tf_op jit(solution)/shard_map/ppermute | solution.py:736
  57.4 2.6 %collective-permute-done.8.low_packed = f32[336,128]{1,0:T(8,128)S(1)} collective-permute-done((f32[336,128]{1,0:T(8,128)S(1)}, f32[336,128]{1,0:T(8,128)S(1)}, u32[]{:S(2)}, u32[]{:S(2)}) %collective-permute-start.8) | collective-permute-done | bytes 172064 | tf_op jit(solution)/shard_map/ppermute | solution.py:736
  59.9 5.6 %collective-permute-done.9.high_packed = f32[336,128]{1,0:T(8,128)S(1)} collective-permute-done((f32[336,128]{1,0:T(8,128)S(1)}, f32[336,128]{1,0:T(8,128)S(1)}, u32[]{:S(2)}, u32[]{:S(2)}) %collective-permute-start.9) | collective-permute-done | bytes 172064 | tf_op jit(solution)/shard_map/ppermute | solution.py:736
  66.1 4.0 %collective-permute-start.10 = (f32[536,128]{1,0:T(8,128)S(1)}, f32[536,128]{1,0:T(8,128)S(1)}, u32[]{:S(2)}, u32[]{:S(2)}) collective-permute-start(f32[536,128]{1,0:T(8,128)S(1)} %get-tuple-element.68), channel_id=1, source_target_pairs={{0,8},{8,16},{16,24},{24,32},{32,40},{40,48},{48,56},{1,9},{9,17},... | collective-permute-start | bytes 823304 | tf_op jit(solution)/shard_map/ppermute | solution.py:736
  71.4 6.3 %collective-permute-done.10.below_packed = f32[536,128]{1,0:T(8,128)S(1)} collective-permute-done((f32[536,128]{1,0:T(8,128)S(1)}, f32[536,128]{1,0:T(8,128)S(1)}, u32[]{:S(2)}, u32[]{:S(2)}) %collective-permute-start.10) | collective-permute-done | bytes 274464 | tf_op jit(solution)/shard_map/ppermute | solution.py:736
  77.7 7.8 %collective-permute-done.11.above_packed = f32[536,128]{1,0:T(8,128)S(1)} collective-permute-done((f32[536,128]{1,0:T(8,128)S(1)}, f32[536,128]{1,0:T(8,128)S(1)}, u32[]{:S(2)}, u32[]{:S(2)}) %collective-permute-start.11) | collective-permute-done | bytes 274464 | tf_op jit(solution)/shard_map/ppermute | solution.py:736
  85.5 3.0 %middle_sweeps.1 = (f32[576,128]{1,0:T(8,128)S(1)}, f32[576,128]{1,0:T(8,128)S(1)}, f32[192,128]{1,0:T(8,128)S(1)}, f32[480,128]{1,0:T(8,128)S(1)}, f32[512,128]{1,0:T(8,128)}, /*index=5*/f32[49152,128]{1,0:T(8,128)}) custom-call(f32[288,128]{1,0:T(8,128)S(1)} %get-tuple-element.59.coef.coef0, f32[48,128]{1,0:T(8,128)S(1)} %get-tuple-element.60.right.right0, ...), custom_call_target="tpu_custom_call" | custom-call | tf_op jit(solution)/shard_map/middle_sweeps/pallas_call | solution.py:43
  88.4 13.2 %all-to-all-start = ((f32[64,8,128]{2,1,0:T(8,128)}), f32[64,8,128]{2,1,0:T(8,128)S(1)}, u32[]{:S(2)}, u32[]{:S(2)}) async-start(f32[64,8,128]{2,1,0:T(8,128)} %bitcast), calls=%async_computation | async-start | bytes 524288 | tf_op jit(solution)/shard_map/all_to_all | solution.py:741
  101.7 6.2 %all-gather.2.cloned.1.call-done.refs_0_ = f32[4096,128]{1,0:T(8,128)} async-done(((f32[64,128]{1,0:T(8,128)}), f32[4096,128]{1,0:T(8,128)}) %all-gather.2.cloned.1.call-update) | async-done | bytes 2097168 | tf_op jit(solution)/shard_map/all_gather | solution.py:754
  109.5 3.0 %coarse_coefs.1.refs_0_ = f32[49152,128]{1,0:T(8,128)} custom-call(f32[4096,128]{1,0:T(8,128)S(1)} %copy-done), custom_call_target="tpu_custom_call" | custom-call | tf_op jit(solution)/shard_map/coarse_coefs/pallas_call | solution.py:43
  112.5 4.3 %all-to-all-done = f32[64,8,128]{2,1,0:T(8,128)S(1)} async-done(((f32[64,8,128]{2,1,0:T(8,128)}), f32[64,8,128]{2,1,0:T(8,128)S(1)}, u32[]{:S(2)}, u32[]{:S(2)}) %all-to-all-start) | async-done | bytes 262176 | tf_op jit(solution)/shard_map/all_to_all | solution.py:741
  116.8 5.7 %finish.1 = f32[3,8,8,128]{3,2,1,0:T(8,128)} custom-call(f32[49152,128]{1,0:T(8,128)} %coarse_coefs.1.refs_0_, f32[49152,128]{1,0:T(8,128)} %get-tuple-element.71.refs_1_, f32[512,128]{1,0:T(8,128)S(1)} %bitcast.2, f32[480,128]{1,0:T(8,128)S(1)} %get-tuple-element.73.refs_3_, f32[576,128]{1,0:T(8,128)S(1)} %get-tuple-element.74.refs_4_, ...), custom_call_target="tpu_custom_call" | custom-call | tf_op jit(solution)/shard_map/finish/pallas_call | solution.py:792
  (18 shorter events, 12.8 us)
Async XLA Ops:
  6.5 101.4 %all-gather.2.cloned.1.call-start = ((), (), s32[]{:S(2)}) async-start(), calls=%async_computation.1 | async-start | bytes 2129920 | tf_op jit(solution)/shard_map/all_gather | solution.py:754
  8.9 4.3 %collective-permute-start.1 = (f32[152,128]{1,0:T(8,128)S(1)}, f32[152,128]{1,0:T(8,128)S(1)}, u32[]{:S(2)}, u32[]{:S(2)}) collective-permute-start(f32[152,128]{1,0:T(8,128)S(1)} %get-tuple-element.43), channel_id=1, source_target_pairs={{1,0},{2,1},{3,2},{4,3},{5,4},{6,5},{7,6},{9,8},{10,9},{11,10},{12... | collective-permute-start | bytes 233480 | tf_op jit(solution)/shard_map/ppermute | solution.py:736
  10.8 10.0 %collective-permute-start = (f32[152,128]{1,0:T(8,128)S(1)}, f32[152,128]{1,0:T(8,128)S(1)}, u32[]{:S(2)}, u32[]{:S(2)}) collective-permute-start(f32[152,128]{1,0:T(8,128)S(1)} %get-tuple-element.42.zown), channel_id=1, source_target_pairs={{0,1},{1,2},{2,3},{3,4},{4,5},{5,6},{6,7},{8,9},{9,10},{10,11},{11... | collective-permute-start | bytes 233480 | tf_op jit(solution)/shard_map/ppermute | solution.py:736
  21.7 4.7 %collective-permute-start.2 = (f32[432,128]{1,0:T(8,128)S(1)}, f32[432,128]{1,0:T(8,128)S(1)}, u32[]{:S(2)}, u32[]{:S(2)}) collective-permute-start(f32[432,128]{1,0:T(8,128)S(1)} %get-tuple-element.47), channel_id=1, source_target_pairs={{0,64},{64,128},{128,192},{192,256},{256,320},{320,384},{384,448},... | collective-permute-start | bytes 663560 | tf_op jit(solution)/shard_map/ppermute | solution.py:736
  23.0 7.8 %collective-permute-start.3 = (f32[432,128]{1,0:T(8,128)S(1)}, f32[432,128]{1,0:T(8,128)S(1)}, u32[]{:S(2)}, u32[]{:S(2)}) collective-permute-start(f32[432,128]{1,0:T(8,128)S(1)} %get-tuple-element.48), channel_id=1, source_target_pairs={{64,0},{128,64},{192,128},{256,192},{320,256},{384,320},{448,384},... | collective-permute-start | bytes 663560 | tf_op jit(solution)/shard_map/ppermute | solution.py:736
  30.9 6.4 %collective-permute-start.4 = (f32[504,128]{1,0:T(8,128)S(1)}, f32[504,128]{1,0:T(8,128)S(1)}, u32[]{:S(2)}, u32[]{:S(2)}) collective-permute-start(f32[504,128]{1,0:T(8,128)S(1)} %get-tuple-element.49), channel_id=1, source_target_pairs={{0,8},{8,16},{16,24},{24,32},{32,40},{40,48},{48,56},{1,9},{9,17},... | collective-permute-start | bytes 774152 | tf_op jit(solution)/shard_map/ppermute | solution.py:736
  33.5 8.7 %collective-permute-start.5 = (f32[504,128]{1,0:T(8,128)S(1)}, f32[504,128]{1,0:T(8,128)S(1)}, u32[]{:S(2)}, u32[]{:S(2)}) collective-permute-start(f32[504,128]{1,0:T(8,128)S(1)} %get-tuple-element.50), channel_id=1, source_target_pairs={{8,0},{16,8},{24,16},{32,24},{40,32},{48,40},{56,48},{9,1},{17,9},... | collective-permute-start | bytes 774152 | tf_op jit(solution)/shard_map/ppermute | solution.py:736
  44.3 5.9 %collective-permute-start.6 = (f32[192,128]{1,0:T(8,128)S(1)}, f32[192,128]{1,0:T(8,128)S(1)}, u32[]{:S(2)}, u32[]{:S(2)}) collective-permute-start(f32[192,128]{1,0:T(8,128)S(1)} %get-tuple-element.57), channel_id=1, source_target_pairs={{0,1},{1,2},{2,3},{3,4},{4,5},{5,6},{6,7},{8,9},{9,10},{10,11},{11... | collective-permute-start | bytes 294920 | tf_op jit(solution)/shard_map/ppermute | solution.py:736
  46.2 5.8 %collective-permute-start.7 = (f32[192,128]{1,0:T(8,128)S(1)}, f32[192,128]{1,0:T(8,128)S(1)}, u32[]{:S(2)}, u32[]{:S(2)}) collective-permute-start(f32[192,128]{1,0:T(8,128)S(1)} %get-tuple-element.58), channel_id=1, source_target_pairs={{1,0},{2,1},{3,2},{4,3},{5,4},{6,5},{7,6},{9,8},{10,9},{11,10},{12... | collective-permute-start | bytes 294920 | tf_op jit(solution)/shard_map/ppermute | solution.py:736
  52.6 7.4 %collective-permute-start.8 = (f32[336,128]{1,0:T(8,128)S(1)}, f32[336,128]{1,0:T(8,128)S(1)}, u32[]{:S(2)}, u32[]{:S(2)}) collective-permute-start(f32[336,128]{1,0:T(8,128)S(1)} %get-tuple-element.64), channel_id=1, source_target_pairs={{0,64},{64,128},{128,192},{192,256},{256,320},{320,384},{384,448},... | collective-permute-start | bytes 516104 | tf_op jit(solution)/shard_map/ppermute | solution.py:736
  56.1 9.4 %collective-permute-start.9 = (f32[336,128]{1,0:T(8,128)S(1)}, f32[336,128]{1,0:T(8,128)S(1)}, u32[]{:S(2)}, u32[]{:S(2)}) collective-permute-start(f32[336,128]{1,0:T(8,128)S(1)} %get-tuple-element.65), channel_id=1, source_target_pairs={{64,0},{128,64},{192,128},{256,192},{320,256},{384,320},{448,384},... | collective-permute-start | bytes 516104 | tf_op jit(solution)/shard_map/ppermute | solution.py:736
  66.1 11.6 %collective-permute-start.10 = (f32[536,128]{1,0:T(8,128)S(1)}, f32[536,128]{1,0:T(8,128)S(1)}, u32[]{:S(2)}, u32[]{:S(2)}) collective-permute-start(f32[536,128]{1,0:T(8,128)S(1)} %get-tuple-element.68), channel_id=1, source_target_pairs={{0,8},{8,16},{16,24},{24,32},{32,40},{40,48},{48,56},{1,9},{9,17},... | collective-permute-start | bytes 823304 | tf_op jit(solution)/shard_map/ppermute | solution.py:736
  70.1 15.4 %collective-permute-start.11 = (f32[536,128]{1,0:T(8,128)S(1)}, f32[536,128]{1,0:T(8,128)S(1)}, u32[]{:S(2)}, u32[]{:S(2)}) collective-permute-start(f32[536,128]{1,0:T(8,128)S(1)} %get-tuple-element.69), channel_id=1, source_target_pairs={{8,0},{16,8},{24,16},{32,24},{40,32},{48,40},{56,48},{9,1},{17,9},... | collective-permute-start | bytes 823304 | tf_op jit(solution)/shard_map/ppermute | solution.py:736
  88.4 28.3 %all-to-all-start = ((f32[64,8,128]{2,1,0:T(8,128)}), f32[64,8,128]{2,1,0:T(8,128)S(1)}, u32[]{:S(2)}, u32[]{:S(2)}) async-start(f32[64,8,128]{2,1,0:T(8,128)} %bitcast), calls=%async_computation | async-start | bytes 524288 | tf_op jit(solution)/shard_map/all_to_all | solution.py:741
  107.9 1.6 %copy-start = (f32[4096,128]{1,0:T(8,128)S(1)}, f32[4096,128]{1,0:T(8,128)}, u32[]{:S(2)}) copy-start(f32[4096,128]{1,0:T(8,128)} %all-gather.2.cloned.1.call-done.refs_0_) | copy-start | bytes 6291460
Sparse Core Ops, SparseCore 0:
  21.8 86.0 all-gather.1
